TPU v7x, 128 devices: a whole 4x4x4 slice. The times are simulated.
128 devices in a mesh: slab: 8 (over z, core), pencil: 16 (over y, x).
Axes of the slice: x: 4, y: 4, z: 4, core: 2. Of those that a mesh axis runs over, the one named last changes fastest.
Arguments:
- charges: float32 [32768, 128], P(('slab', 'pencil')), may hold values from -6 to 6
- projection: float32 [32768, 64, 128], P(('slab', 'pencil')), may hold values from -0.5 to 0.5
- anchors: int32 [32768, 3], P(('slab', 'pencil')), may hold values from 0 to 511, as said below
- block_count: int32 [128], P(('slab', 'pencil')), may hold values from 64 to 256, as said below
- near_pairs: int32 [32768, 2], P(('slab', 'pencil')), may hold values from 0 to 255, as said below
- near_matrices: bfloat16 [32768, 128, 128], P(('slab', 'pencil')), may hold values from -0.5 to 0.5
- kernel_hat: float32 [512, 512, 256], P(None, ('slab', 'pencil')), may hold values from 0.2 to 2, as said below
Outputs:
- panel_potential: float32 [32768, 128], P(('slab', 'pencil'))
Inputs may be any that keep to these rules, and one draw needn't show every extreme that they name: Device d = slab index * pencil size + pencil index holds slots d * 256 to (d + 1) * 256 - 1; its first block_count[d] slots are in use, and some device uses all 256. `anchors`: column 0 is x, 1 is y, 2 is z. A block of the device with slab index s and pencil index p has x in [p * 32, (p + 1) * 32) and z in [s * 32, (s + 1) * 32). `near_pairs`: both slots of each pair of a device are in use on that device; target and source may coincide. The Green's function is real and even in space: kernel_hat[kx, ky, kz] equals kernel_hat[(-kx) mod 512, (-ky) mod 512, (-kz) mod 256].
All inputs are finite; a program needn't handle non-finite values.
Results may differ from a plain program's by a relative error of at most 0.0025.
Values sent between devices are 32-bit elements; how exact they have to be, the bound alone decides.
A program may use at most 192 MiB of HBM per device.

v0:
```python
import jax
import jax.numpy as jnp
from jax import lax
from jax.sharding import PartitionSpec as P

NX = 512
NY = 512
NZ = 256
BOX = 64


precise = lax.Precision.HIGHEST


def extended_2(cells, sides, width):
    for axis, dim in sides:
        count = lax.axis_size(axis)
        head = lax.slice_in_dim(cells, 0, width, axis=dim)
        tail = lax.slice_in_dim(cells, cells.shape[dim] - width, cells.shape[dim], axis=dim)
        cells = jnp.concatenate(
            [
                lax.ppermute(tail, axis, [(i, (i + 1) % count) for i in range(count)]),
                cells,
                lax.ppermute(head, axis, [((i + 1) % count, i) for i in range(count)]),
            ],
            axis=dim,
        )
    return cells


def box_index(anchors, x_start, z_start, z_dev, length_y):
    point_id = jnp.arange(BOX, dtype=jnp.int32)
    off_x = point_id // 16 - 2
    off_y = point_id // 4 % 4 - 2
    off_z = point_id % 4 - 2
    local_x = anchors[:, 0:1] - x_start + off_x[None, :] + 2
    local_z = anchors[:, 2:3] - z_start + off_z[None, :] + 2
    local_y = (anchors[:, 1:2] + off_y[None, :]) % length_y
    return (local_x * (z_dev + 4) + local_z) * length_y + local_y


def tables(length):
    position = jnp.arange(length, dtype=jnp.int32)
    phase_angle = (position[:, None] * position[None, :] % length).astype(jnp.float32) * (
        2.0 * jnp.pi / length
    )
    return (jnp.cos(phase_angle), jnp.sin(phase_angle))


def forward_x(table, field):
    return jnp.einsum("kx,wxz->kwz", table, field, precision=precise)


def inverse_x(table, field):
    return jnp.einsum("xk,kwz->xwz", table, field, precision=precise)


def last_dim(field, table):
    return jnp.dot(field, table, precision=precise)


def frequency_of(owner, within, y_dev):
    return owner * y_dev + within


def shards(charges, projection, anchors, block_count, near_pairs, near_matrices, kernel_hat):
    slot_count, panels = charges.shape
    n_slab = lax.axis_size("slab")
    n_pencil = lax.axis_size("pencil")
    n_dev = n_slab * n_pencil
    x_dev = NX // n_pencil
    z_dev = NZ // n_slab
    y_dev = NY // n_dev
    x_start = lax.axis_index("pencil") * x_dev
    z_start = lax.axis_index("slab") * z_dev
    in_use = jnp.arange(slot_count, dtype=jnp.int32) < block_count[0]
    masked = jnp.where(in_use[:, None], charges, 0.0)
    box_charge = jnp.einsum("bnp,bp->bn", projection, masked, precision=precise)
    flat_index = box_index(anchors, x_start, z_start, z_dev, NY).reshape(-1)
    extended = (
        jnp.zeros(((x_dev + 4) * (z_dev + 4) * NY,), jnp.float32)
        .at[flat_index]
        .add(box_charge.reshape(-1))
    )
    extended = extended.reshape(x_dev + 4, z_dev + 4, NY)
    plane_rims = jnp.concatenate([extended[:, :2], extended[:, z_dev + 2 :]], axis=1)
    plane_rims = extended_2(plane_rims, (("slab", 1),), 2)
    planes = extended[:, 2 : z_dev + 2]
    planes = planes.at[:, :2].add(plane_rims[:, :2])
    planes = planes.at[:, z_dev - 2 :].add(plane_rims[:, 6:])
    row_rims = jnp.concatenate([planes[:2], planes[x_dev + 2 :]], axis=0)
    row_rims = extended_2(row_rims, (("pencil", 0),), 2)
    grid_charge = planes[2 : x_dev + 2]
    grid_charge = grid_charge.at[:2].add(row_rims[:2])
    grid_charge = grid_charge.at[x_dev - 2 :].add(row_rims[6:])
    position = jnp.arange(NY, dtype=jnp.int32)
    columns = jnp.arange(n_dev * y_dev, dtype=jnp.int32)
    forward_freq = frequency_of(columns // y_dev, columns % y_dev, y_dev)
    forward_angle = (position[:, None] * forward_freq[None, :] % NY).astype(jnp.float32) * (
        2.0 * jnp.pi / NY
    )
    forward_cos = jnp.cos(forward_angle)
    forward_sin = jnp.sin(forward_angle)
    flat_charge = grid_charge.reshape(x_dev * z_dev, NY)
    real_cols = jnp.einsum("yc,ay->ca", forward_cos, flat_charge, precision=precise)
    imag_cols = -jnp.einsum("yc,ay->ca", forward_sin, flat_charge, precision=precise)
    stacked = jnp.stack([real_cols, imag_cols]).reshape(2, n_dev * y_dev, x_dev, z_dev)
    cos_x, sin_x = tables(NX)
    cos_z, sin_z = tables(NZ)
    spectrum = lax.all_to_all(
        lax.all_to_all(stacked, "slab", split_axis=1, concat_axis=3, tiled=True),
        "pencil",
        split_axis=1,
        concat_axis=2,
        tiled=True,
    )
    real_part, imag_part = (spectrum[0], spectrum[1])
    real_z = last_dim(real_part, cos_z) + last_dim(imag_part, sin_z)
    imag_z = last_dim(imag_part, cos_z) - last_dim(real_part, sin_z)
    real_x = forward_x(cos_x, real_z) + forward_x(sin_x, imag_z)
    imag_x = forward_x(cos_x, imag_z) - forward_x(sin_x, real_z)
    real_kernel = real_x * kernel_hat
    imag_kernel = imag_x * kernel_hat
    real_back = inverse_x(cos_x, real_kernel) - inverse_x(sin_x, imag_kernel)
    imag_back = inverse_x(cos_x, imag_kernel) + inverse_x(sin_x, real_kernel)
    real_space = last_dim(real_back, cos_z) - last_dim(imag_back, sin_z)
    imag_space = last_dim(imag_back, cos_z) + last_dim(real_back, sin_z)
    outgoing = jnp.stack([real_space, imag_space])
    returned = lax.all_to_all(
        lax.all_to_all(outgoing, "slab", split_axis=3, concat_axis=2, tiled=True),
        "pencil",
        split_axis=1,
        concat_axis=2,
        tiled=True,
    )
    from_pencil = columns // (n_slab * y_dev)
    from_slab = columns // y_dev % n_slab
    back_owner = from_slab * n_pencil + from_pencil
    back_within = columns % y_dev
    back_freq = frequency_of(back_owner, back_within, y_dev)
    back_angle = (back_freq[:, None] * position[None, :] % NY).astype(jnp.float32) * (
        2.0 * jnp.pi / NY
    )
    back_cos = jnp.cos(back_angle)
    back_sin = jnp.sin(back_angle)
    scale = 1.0 / (NX * NY * NZ)
    potential = (
        jnp.einsum("xcz,cy->xzy", returned[0], back_cos, precision=precise)
        - jnp.einsum("xcz,cy->xzy", returned[1], back_sin, precision=precise)
    ) * scale
    rimmed = extended_2(potential, (("slab", 1), ("pencil", 0)), 2)
    box_potential = rimmed.reshape(-1)[flat_index].reshape(slot_count, BOX)
    far_term = jnp.einsum("bnp,bn->bp", projection, box_potential, precision=precise)
    coarse = masked.astype(jnp.bfloat16)
    sources = coarse[near_pairs[:, 1]]
    pair_terms = jnp.einsum(
        "ntp,np->nt", near_matrices, sources, preferred_element_type=jnp.float32
    )
    near_term = jnp.zeros((slot_count, panels), jnp.float32).at[near_pairs[:, 0]].add(pair_terms)
    return jnp.where(in_use[:, None], far_term + near_term, 0.0)


def solution(mesh):
    return jax.shard_map(
        shards,
        mesh=mesh,
        in_specs=(
            P(("slab", "pencil"), None),
            P(("slab", "pencil"), None, None),
            P(("slab", "pencil"), None),
            P(("slab", "pencil")),
            P(("slab", "pencil"), None),
            P(("slab", "pencil"), None, None),
            P(None, ("slab", "pencil"), None),
        ),
        out_specs=P(("slab", "pencil"), None),
        check_vma=False,
    )
```

profile of v0, /device:TPU:1, one launch (start us, length us, event | category | flops | bytes accessed | tf_op | source)
XLA Modules:
  0.0 822.1 jit_solution(15802664847117583267)
XLA Ops:
  3.1 15.4 %fusion.197 = f32[256,1,64]{2,1,0:T(1,128)S(1)} fusion(f32[256,128,1]{1,2,0:T(1,128)S(1)} %bitcast.142, f32[256,64,128]{2,1,0:T(8,128)} %param.16), kind=kOutput, calls=%fused_computation.249 | convolution fusion | flops 25165824 | bytes 8585216 | tf_op jit(solution)/shard_map/bnp,bp->bn/dot_general | solution.py:78
  19.5 87.4 %scatter_custom_fusion = f32[663552]{0:T(1024)} fusion(s32[16384]{0:T(1024)S(1)} %bitcast.145, f32[16384]{0:T(1024)S(1)} %reshape.422, f32[]{:T(128)} %constant.271.clone.1), kind=kCustom, calls=%fused_computation.27 | custom fusion | flops 16384 | bytes 2654212 | tf_op jit(solution)/shard_map/scatter-add | solution.py:83
  109.6 3.0 collective-permute-start
  119.0 3.8 collective-permute-start.3
  122.8 3.0 collective-permute-done.2
  125.9 8.8 %convolution_bitcast_fusion = f32[1,512,32,32]{1,3,2,0:T(8,128)} fusion(f32[32,32,512]{2,1,0:T(8,128)S(1)} %fusion.74, s32[512]{0:T(512)S(1)} %fusion.102), kind=kOutput, calls=%fused_computation.13 | convolution fusion | flops 3224895488 | bytes 4196352 | tf_op jit(solution)/shard_map/yc,ay->ca/dot_general | solution.py:105
  134.7 11.7 %convolution_negate_fusion = f32[512,1024]{1,0:T(8,128)} fusion(f32[1024,512]{1,0:T(8,128)S(1)} %bitcast.139, s32[512]{0:T(512)S(1)} %fusion.102), kind=kOutput, calls=%fused_computation.12 | convolution fusion | flops 3225419776 | bytes 4196352 | tf_op jit(solution)/shard_map/yc,ay->ca/dot_general | solution.py:106
  148.3 4.2 pad_maximum_fusion
  152.5 14.4 %copy.40 = f32[2,512,32,32]{3,2,0,1:T(8,128)} copy(f32[2,512,32,32]{1,3,2,0:T(8,128)} %pad_maximum_fusion) | data formatting | bytes 8388608 | tf_op jit(solution)/shard_map/stack | solution.py:107
  166.9 12.8 %reshape.450 = f32[8,1,131072]{2,1,0:T(1,128)} reshape(f32[512,2,32,32]{3,2,1,0:T(8,128)} %bitcast.124) | data formatting | bytes 8388608
  179.7 55.0 %all_to_all.66 = f32[8,1,131072]{2,1,0:T(1,128)} all-to-all(f32[8,1,131072]{2,1,0:T(1,128)} %reshape.450), channel_id=1, replica_groups=mesh['slab'=8,'pencil'=16] {'slab'}, dimensions={0} | all-to-all | bytes 8388608 | tf_op jit(solution)/shard_map/all_to_all | solution.py:111
  235.2 13.6 %reduce.8 = f32[8,131072]{1,0:T(8,128)} reduce(f32[8,1,131072]{2,1,0:T(1,128)} %all_to_all.66, f32[]{:T(128)} %broadcast.631), dimensions={1}, to_apply=%all_to_all.48.reduce_sub_computation | reduce | bytes 8388612 | tf_op jit(solution)/shard_map/all_to_all | solution.py:111
  248.8 13.4 %reshape.451 = f32[512,2,32,32]{3,2,1,0:T(8,128)} reshape(f32[8,131072]{1,0:T(8,128)} %reduce.8) | data formatting | bytes 8388608
  262.1 12.8 %copy.41 = f32[2,8,64,32,32]{2,4,1,3,0:T(8,128)} copy(f32[2,8,64,32,32]{4,3,0,2,1:T(8,128)} %bitcast.125) | data formatting | bytes 8388608 | tf_op jit(solution)/shard_map/all_to_all | solution.py:111
  275.0 7.3 copy.42
  282.3 56.1 %all_to_all.67 = f32[2,64,32,256]{3,2,0,1:T(8,128)S(1)} all-to-all(f32[2,64,32,256]{3,2,0,1:T(8,128)} %copy.42), channel_id=1, replica_groups=mesh['slab'=8,'pencil'=16] {'pencil'}, dimensions={1} | all-to-all | bytes 8388608 | tf_op jit(solution)/shard_map/all_to_all | solution.py:110
  345.5 2.9 convolution_add_fusion
  348.4 7.7 fusion.25
  356.2 2.9 convolution_subtract_fusion
  359.1 7.5 fusion.21
  366.6 7.9 add_multiply_fusion
  374.5 7.5 fusion.23
  382.0 8.3 %subtract_multiply_fusion.1 = f32[512,4,256]{2,0,1:T(8,128)S(1)} fusion(f32[512,4,256]{2,0,1:T(8,128)S(1)} %fusion.21, f32[512,4,256]{2,1,0:T(4,128)S(1)} %copy-done, f32[4,512,256]{2,1,0:T(8,128)S(1)} %convolution_add_fusion), kind=kOutput, calls=%fused_computation.10 | convolution fusion | flops 3225944064 | bytes 8388608 | tf_op jit(solution)/shard_map/kx,wxz->kwz/dot_general | solution.py:51
  390.3 7.3 fusion.19
  397.7 7.6 convolution_subtract_fusion.1
  408.1 7.8 convolution_add_fusion.1
  418.7 2.9 subtract_bitcast_fusion
  421.6 2.9 add_bitcast_fusion
  426.7 5.5 copy.48
  432.3 55.3 %all_to_all.68 = f32[2,512,4,256]{1,2,0,3:T(4,128)S(1)} all-to-all(f32[2,512,4,256]{1,2,0,3:T(4,128)} %copy.48), channel_id=1, replica_groups=mesh['slab'=8,'pencil'=16] {'slab'}, dimensions={3} | all-to-all | bytes 8388608 | tf_op jit(solution)/shard_map/all_to_all | solution.py:130
  492.4 14.4 %copy.51 = f32[2,512,32,32]{3,2,0,1:T(8,128)} copy(f32[2,512,32,32]{1,3,2,0:T(8,128)} %bitcast.134) | data formatting | bytes 8388608 | tf_op jit(solution)/shard_map/all_to_all | solution.py:130
  506.8 16.0 %reshape.452 = f32[16,1,65536]{2,1,0:T(1,128)} reshape(f32[512,2,32,32]{3,2,1,0:T(8,128)} %bitcast.126) | data formatting | bytes 8388608
  522.7 4.7 all-to-all-start.3
  528.3 61.1 %all-to-all-done.3 = f32[16,1,65536]{2,1,0:T(1,128)} async-done(((f32[16,1,65536]{2,1,0:T(1,128)}), f32[16,1,65536]{2,1,0:T(1,128)}, u32[]{:S(2)}, u32[]{:S(2)}) %all-to-all-start.3) | async-done | bytes 4194336 | tf_op jit(solution)/shard_map/all_to_all | solution.py:129
  589.4 13.6 %reduce.9 = f32[16,65536]{1,0:T(8,128)} reduce(f32[16,1,65536]{2,1,0:T(1,128)} %all-to-all-done.3, f32[]{:T(128)} %broadcast.631), dimensions={1}, to_apply=%all_to_all.59.reduce_sub_computation | reduce | bytes 8388612 | tf_op jit(solution)/shard_map/all_to_all | solution.py:129
  603.1 15.1 %reshape.453 = f32[512,2,32,32]{3,2,1,0:T(8,128)} reshape(f32[16,65536]{1,0:T(8,128)} %reduce.9) | data formatting | bytes 8388608
  618.2 19.6 %copy.61 = f32[2,16,32,32,32]{2,1,4,3,0:T(8,128)} copy(f32[2,16,32,32,32]{4,3,0,2,1:T(8,128)} %bitcast.127) | data formatting | bytes 8388608 | tf_op jit(solution)/shard_map/all_to_all | solution.py:129
  637.7 11.1 %fusion.191 = (f32[1,32,16,32,32]{1,2,4,3,0:T(8,128)}, f32[1,32,16,32,32]{1,2,4,3,0:T(8,128)}) fusion(f32[2,32,16,32,32]{1,2,4,3,0:T(8,128)} %bitcast.128), kind=kLoop, calls=%fused_computation.243 | loop fusion | bytes 8388608 | tf_op jit(solution)/shard_map/slice | solution.py:149
  648.9 9.4 %copy.53 = f32[1,32,16,32,32]{3,2,4,1,0:T(8,128)} copy(f32[1,32,16,32,32]{1,2,4,3,0:T(8,128)} %get-tuple-element.56) | data formatting | bytes 4194304 | tf_op jit(solution)/shard_map/slice | solution.py:148
  658.3 6.2 squeeze.20
  664.5 9.4 %copy.54 = f32[1,32,16,32,32]{3,2,4,1,0:T(8,128)} copy(f32[1,32,16,32,32]{1,2,4,3,0:T(8,128)} %get-tuple-element.55) | data formatting | bytes 4194304 | tf_op jit(solution)/shard_map/slice | solution.py:149
  674.0 7.7 squeeze.21
  681.7 7.3 fusion.12
  689.1 7.7 subtract_multiply_fusion
  699.0 7.8 fusion.76
  707.0 4.8 collective-permute-start.7
  719.0 90.5 %gather_fusion = f32[16384]{0:T(1024)S(1)} fusion(f32[663552]{0:T(1024)S(1)} %reshape.398, s32[16384]{0:T(1024)S(1)} %broadcast_clamp_fusion), kind=kCustom, calls=%fused_computation | custom fusion | bytes 196608 | tf_op jit(solution)/shard_map/gather | solution.py:152
  809.7 9.5 %fusion.198 = f32[256,1,128]{2,1,0:T(1,128)S(1)} fusion(f32[256,64,1]{1,2,0:T(1,128)S(1)} %bitcast.144, f32[256,64,128]{2,1,0:T(8,128)} %param.16), kind=kOutput, calls=%fused_computation.250 | convolution fusion | flops 25165824 | bytes 8585216 | tf_op jit(solution)/shard_map/bnp,bn->bp/dot_general | solution.py:153
  (73 shorter events, 48.0 us)
Async XLA Ops:
  2.0 16.4 %copy-start.4 = (pred[256]{0:T(512)(128)(4,1)}, pred[256]{0:T(512)(128)(4,1)S(1)}, u32[]{:S(2)}) copy-start(pred[256]{0:T(512)(128)(4,1)S(1)} %iota_compare_fusion) | copy-start | bytes 772
  18.8 0.6 copy-start.2
  109.6 5.1 collective-permute-start
  112.7 4.6 collective-permute-start.1
  117.4 8.4 %collective-permute-start.2 = (f32[2,32,512]{2,1,0:T(8,128)S(1)}, f32[2,32,512]{2,1,0:T(8,128)S(1)}, u32[]{:S(2)}, u32[]{:S(2)}) collective-permute-start(f32[2,32,512]{2,1,0:T(8,128)S(1)} %get-tuple-element.64), channel_id=1, source_target_pairs={{0,1},{1,2},{2,3},{3,4},{4,5},{5,6},{6,7},{7,8},{8,9},{9,10},{10,1... | collective-permute-start | bytes 393224 | tf_op jit(solution)/shard_map/ppermute | solution.py:22
  119.0 6.9 collective-permute-start.3
  359.1 7.5 copy-start
  522.7 4.7 copy-start.6
  522.7 66.7 %all-to-all-start.3 = ((f32[16,1,65536]{2,1,0:T(1,128)}), f32[16,1,65536]{2,1,0:T(1,128)}, u32[]{:S(2)}, u32[]{:S(2)}) async-start(f32[16,1,65536]{2,1,0:T(1,128)} %reshape.452), calls=%async_computation.3 | async-start | bytes 8388608 | tf_op jit(solution)/shard_map/all_to_all | solution.py:129
  681.7 7.4 copy-start.1
  696.9 9.9 %collective-permute-start.4 = (f32[32,2,512]{2,1,0:T(2,128)S(1)}, f32[32,2,512]{2,1,0:T(2,128)S(1)}, u32[]{:S(2)}, u32[]{:S(2)}) collective-permute-start(f32[32,2,512]{2,1,0:T(2,128)S(1)} %get-tuple-element.65), channel_id=1, source_target_pairs={{0,16},{16,32},{32,48},{48,64},{64,80},{80,96},{96,112},{112,0},{1... | collective-permute-start | bytes 393224 | tf_op jit(solution)/shard_map/ppermute | solution.py:22
  699.0 7.8 collective-permute-start.5
  706.8 5.0 copy-start.3
  706.9 7.6 collective-permute-start.6
  707.0 7.5 collective-permute-start.7
  819.1 2.0 copy-start.5
where the time goes:
time: 834 us; the launch traced here: 822 us
  local copies, waits for them, and re-layouts  283 us (34%)
  blocking collectives  166 us (20%)
  matrix products  153 us (18%)
  other arithmetic  129 us (15%)
  waiting for transfers between devices  70.9 us (9%)
  starting transfers between devices  19.8 us (2%)
    gather x1, local copies, waits for them, and re-layouts, shards(): box_potential = rimmed.reshape(-1)[flat_index].reshape(slot_count, BOX)  90.5 us
    scatter-add x1, other arithmetic, shards(): extended = jnp.zeros(((x_dev + 4) * (z_dev + 4) * NY,), jnp.float32).at[f...  87.4 us
    all_to_all x1, waiting for transfers between devices, shards(): lax.all_to_all(lax.all_to_all(outgoing, 'slab', split_axis=3, concat_axis...  61.1 us
    unnamed x18, local copies, waits for them, and re-layouts  57.9 us
    all_to_all x1, blocking collectives, shards(): lax.all_to_all(lax.all_to_all(stacked, 'slab', split_axis=1, concat_axis=...  56.1 us
    all_to_all x1, blocking collectives, shards(): lax.all_to_all(outgoing, 'slab', split_axis=3, concat_axis=2, tiled=True)  55.3 us
    all_to_all x1, blocking collectives, shards(): lax.all_to_all(stacked, 'slab', split_axis=1, concat_axis=3, tiled=True)  55 us
    dot_general x4, matrix products, forward_x(): return jnp.einsum('kx,wxz->kwz', table, field, precision=precise)  31.4 us
  transfers between devices with their start and end apart: 9, of which 5 were waited for; matrix products, arithmetic and copies ran while one was open for 1% of the time, Pallas kernels for 0%

commit v1 on v0

--- a/solution.py
+++ b/solution.py
@@ -1,12 +1,148 @@
 import jax
 import jax.numpy as jnp
 from jax import lax
+from jax.experimental import pallas as pl
+from jax.experimental.pallas import tpu as pltpu
 from jax.sharding import PartitionSpec as P
 
-NX = 512
-NY = 512
-NZ = 256
-BOX = 64
+NX, NY, NZ, BOX = 512, 512, 256, 64
+GROUP = 16
+F32, BF16 = jnp.float32, jnp.bfloat16
+
+
+def halves(value):
+    high = value.astype(BF16)
+    return high, (value - high.astype(F32)).astype(BF16)
+
+
+def lane_sums(value):
+    ones = jnp.ones((128, 128), BF16)
+    high, low = halves(value)
+    return jnp.dot(high, ones, preferred_element_type=F32) + jnp.dot(low, ones, preferred_element_type=F32)
+
+
+def window(code):
+    x_at = code % 32
+    z_at = code // 32 % 32
+    y_at = code // 1024
+    tile_0 = y_at // 128
+    return x_at, z_at + 6, tile_0, (tile_0 + 1) % 4, y_at % 128
+
+
+def window_masks(lane_0):
+    row = lax.broadcasted_iota(jnp.int32, (8, 128), 0)
+    lane = lax.broadcasted_iota(jnp.int32, (8, 128), 1)
+    shifted = lane - row // 4 - lane_0
+    return (shifted == 0, shifted == 2), (shifted == -128, shifted == -126)
+
+
+def scatter_kernel(codes, count, projection, charges, grid, values):
+    step = pl.program_id(0)
+
+    @pl.when(step == 0)
+    def _():
+        def clear(x, carry):
+            grid[x] = jnp.zeros(grid.shape[1:], F32)
+            return carry
+
+        lax.fori_loop(0, grid.shape[0], clear, 0)
+
+    slot = step * GROUP + lax.broadcasted_iota(jnp.int32, (GROUP, 128), 0)
+    masked = jnp.where(slot < count[0], charges[...], 0.0)
+    products = projection[...] * masked[:, None, :]
+    values[...] = lane_sums(products.reshape(GROUP * BOX, 128)).reshape(GROUP, BOX, 128)
+    top = lax.broadcasted_iota(jnp.int32, (8, 128), 0) < 4
+
+    def place(b, carry):
+        x_at, z_row, tile_0, tile_1, lane_0 = window(codes[step * GROUP + b])
+        for tile, masks in zip((tile_0, tile_1), window_masks(lane_0)):
+            for i in range(4):
+                patch = jnp.where(masks[0], values[b, 16 * i : 16 * i + 8], 0.0)
+                patch = jnp.where(masks[1], values[b, 16 * i + 8 : 16 * i + 16], patch)
+                patch = jnp.where(top, patch + pltpu.roll(patch, 4, 0), 0.0)
+                grid[x_at + i, tile, pl.ds(z_row, 8), :] += patch
+        return carry
+
+    lax.fori_loop(0, GROUP, place, 0)
+
+
+def scatter(codes, count, projection, charges):
+    slots = charges.shape[0]
+    return pl.pallas_call(
+        scatter_kernel,
+        grid_spec=pltpu.PrefetchScalarGridSpec(
+            num_scalar_prefetch=2,
+            grid=(slots // GROUP,),
+            in_specs=[
+                pl.BlockSpec((GROUP, BOX, 128), lambda i, *_: (i, 0, 0)),
+                pl.BlockSpec((GROUP, 128), lambda i, *_: (i, 0)),
+            ],
+            out_specs=pl.BlockSpec((36, 4, 48, 128), lambda i, *_: (0, 0, 0, 0)),
+            scratch_shapes=[pltpu.VMEM((GROUP, BOX, 128), F32)],
+        ),
+        out_shape=jax.ShapeDtypeStruct((36, 4, 48, 128), F32),
+        compiler_params=pltpu.CompilerParams(vmem_limit_bytes=32 << 20),
+    )(codes, count, projection, charges)
+
+
+def gather_kernel(codes, count, targets, projection, grid, pair_terms, out, near, picked):
+    step = pl.program_id(0)
+
+    @pl.when(step == 0)
+    def _():
+        slots, pairs = near.shape[0], pair_terms.shape[0]
+        slot = lax.broadcasted_iota(jnp.int32, (slots, pairs), 0)
+        chosen = jnp.where(slot == targets[...], 1.0, 0.0).astype(BF16)
+        rest = pair_terms[...]
+        total = jnp.zeros(near.shape, F32)
+        for _ in range(3):
+            part = rest.astype(BF16)
+            rest = rest - part.astype(F32)
+            total = total + jnp.dot(chosen, part, preferred_element_type=F32)
+        near[...] = total
+
+    top = lax.broadcasted_iota(jnp.int32, (8, 128), 0) < 4
+
+    def pick(b, carry):
+        x_at, z_row, tile_0, tile_1, lane_0 = window(codes[step * GROUP + b])
+        masks_0, masks_1 = window_masks(lane_0)
+        for i in range(4):
+            both = []
+            for tile in (tile_0, tile_1):
+                rows = grid[x_at + i, tile, pl.ds(z_row, 8), :]
+                both.append(jnp.where(top, rows, pltpu.roll(rows, 4, 0)))
+            for j in range(2):
+                value = jnp.where(masks_0[j], both[0], jnp.where(masks_1[j], both[1], 0.0))
+                picked[b, 16 * i + 8 * j : 16 * i + 8 * j + 8] = value
+        return carry
+
+    lax.fori_loop(0, GROUP, pick, 0)
+    box = lane_sums(picked[...].reshape(GROUP * BOX, 128)).reshape(GROUP, BOX, 128)
+    far = jnp.sum(projection[...] * box, axis=1)
+    slot = step * GROUP + lax.broadcasted_iota(jnp.int32, (GROUP, 128), 0)
+    total = far + near[pl.ds(pl.multiple_of(step * GROUP, GROUP), GROUP), :]
+    out[...] = jnp.where(slot < count[0], total, 0.0)
+
+
+def gather(codes, count, targets, projection, grid, pair_terms):
+    slots, pairs = projection.shape[0], pair_terms.shape[0]
+    return pl.pallas_call(
+        gather_kernel,
+        grid_spec=pltpu.PrefetchScalarGridSpec(
+            num_scalar_prefetch=2,
+            grid=(slots // GROUP,),
+            in_specs=[
+                pl.BlockSpec((1, pairs), lambda i, *_: (0, 0)),
+                pl.BlockSpec((GROUP, BOX, 128), lambda i, *_: (i, 0, 0)),
+                pl.BlockSpec((36, 4, 48, 128), lambda i, *_: (0, 0, 0, 0)),
+                pl.BlockSpec((pairs, 128), lambda i, *_: (0, 0)),
+            ],
+            out_specs=pl.BlockSpec((GROUP, 128), lambda i, *_: (i, 0)),
+            scratch_shapes=[pltpu.VMEM((slots, 128), F32), pltpu.VMEM((GROUP, BOX, 128), F32)],
+        ),
+        out_shape=jax.ShapeDtypeStruct((slots, 128), F32),
+        compiler_params=pltpu.CompilerParams(vmem_limit_bytes=32 << 20),
+    )(codes, count, targets, projection, grid, pair_terms)
 
 
 precise = lax.Precision.HIGHEST
@@ -28,17 +164,6 @@
     return cells
 
 
-def box_index(anchors, x_start, z_start, z_dev, length_y):
-    point_id = jnp.arange(BOX, dtype=jnp.int32)
-    off_x = point_id // 16 - 2
-    off_y = point_id // 4 % 4 - 2
-    off_z = point_id % 4 - 2
-    local_x = anchors[:, 0:1] - x_start + off_x[None, :] + 2
-    local_z = anchors[:, 2:3] - z_start + off_z[None, :] + 2
-    local_y = (anchors[:, 1:2] + off_y[None, :]) % length_y
-    return (local_x * (z_dev + 4) + local_z) * length_y + local_y
-
-
 def tables(length):
     position = jnp.arange(length, dtype=jnp.int32)
     phase_angle = (position[:, None] * position[None, :] % length).astype(jnp.float32) * (
@@ -75,14 +200,10 @@
     z_start = lax.axis_index("slab") * z_dev
     in_use = jnp.arange(slot_count, dtype=jnp.int32) < block_count[0]
     masked = jnp.where(in_use[:, None], charges, 0.0)
-    box_charge = jnp.einsum("bnp,bp->bn", projection, masked, precision=precise)
-    flat_index = box_index(anchors, x_start, z_start, z_dev, NY).reshape(-1)
-    extended = (
-        jnp.zeros(((x_dev + 4) * (z_dev + 4) * NY,), jnp.float32)
-        .at[flat_index]
-        .add(box_charge.reshape(-1))
-    )
-    extended = extended.reshape(x_dev + 4, z_dev + 4, NY)
+    local = anchors - jnp.stack([x_start, 2, z_start])[None, :]
+    codes = local[:, 0] + 32 * local[:, 2] + 1024 * (local[:, 1] % NY)
+    extended = scatter(codes, block_count, projection, charges)
+    extended = jnp.transpose(extended[:, :, 6:42, :], (0, 2, 1, 3)).reshape(x_dev + 4, z_dev + 4, NY)
     plane_rims = jnp.concatenate([extended[:, :2], extended[:, z_dev + 2 :]], axis=1)
     plane_rims = extended_2(plane_rims, (("slab", 1),), 2)
     planes = extended[:, 2 : z_dev + 2]
@@ -149,15 +270,14 @@
         - jnp.einsum("xcz,cy->xzy", returned[1], back_sin, precision=precise)
     ) * scale
     rimmed = extended_2(potential, (("slab", 1), ("pencil", 0)), 2)
-    box_potential = rimmed.reshape(-1)[flat_index].reshape(slot_count, BOX)
-    far_term = jnp.einsum("bnp,bn->bp", projection, box_potential, precision=precise)
     coarse = masked.astype(jnp.bfloat16)
     sources = coarse[near_pairs[:, 1]]
     pair_terms = jnp.einsum(
         "ntp,np->nt", near_matrices, sources, preferred_element_type=jnp.float32
     )
-    near_term = jnp.zeros((slot_count, panels), jnp.float32).at[near_pairs[:, 0]].add(pair_terms)
-    return jnp.where(in_use[:, None], far_term + near_term, 0.0)
+    rimmed = jnp.transpose(rimmed.reshape(x_dev + 4, z_dev + 4, 4, 128), (0, 2, 1, 3))
+    rimmed = jnp.pad(rimmed, ((0, 0), (0, 0), (6, 6), (0, 0)))
+    return gather(codes, block_count, near_pairs[:, 0][None, :], projection, rimmed, pair_terms)
 
 
 def solution(mesh):

time: 834 us -> 662 us (0.79)
  other arithmetic: 129 us -> 35.5 us
  local copies, waits for them, and re-layouts: 283 us -> 203 us
  Pallas kernels: 0 us -> 28.5 us
  matrix products: 153 us -> 128 us
    gather x1 -> x0, local copies, waits for them, and re-layouts: 90.5 us -> none  [shards(): box_potential = rimmed.reshape(-1)[flat_index].reshape(slot_count, BOX)]
    scatter-add x2 -> x0, other arithmetic: 89.4 us -> none  [the longest x1 87.4 us: shards(): extended = jnp.zeros(((x_dev + 4) * (z_dev + 4) * NY,), jnp.float32).at[f...]
    pallas_call x0 -> x2, Pallas kernels: none -> 28.5 us  [the longest x1 14.7 us: gather(): pl.pallas_call(gather_kernel, grid_spec=pltpu.PrefetchScalarGridSpec(num_...]
    dot_general x2 -> x0, matrix products: 24.9 us -> none  [the longest x1 15.4 us: shards(): box_charge = jnp.einsum('bnp,bp->bn', projection, masked, precision=precise)]
    unnamed x18 -> x26, local copies, waits for them, and re-layouts: 57.9 us -> 65.2 us
  transfers between devices with their start and end apart: 9 -> 9, of which waited for: 5 -> 6; matrix products, arithmetic and copies ran while one was open for 1% -> 1% of each run, Pallas kernels for 0% -> 0%
where the time goes in v1:
time: 662 us; the launch traced here: 656 us
  local copies, waits for them, and re-layouts  203 us (31%)
  blocking collectives  166 us (25%)
  matrix products  128 us (19%)
  waiting for transfers between devices  72.8 us (11%)
  other arithmetic  35.5 us (5%)
  Pallas kernels  28.5 us (4%)
  starting transfers between devices  19.8 us (3%)
    unnamed x26, local copies, waits for them, and re-layouts  65.2 us
    all_to_all x1, waiting for transfers between devices, shards(): lax.all_to_all(lax.all_to_all(outgoing, 'slab', split_axis=3, concat_axis...  61.9 us
    all_to_all x1, blocking collectives, shards(): lax.all_to_all(lax.all_to_all(stacked, 'slab', split_axis=1, concat_axis=...  56.1 us
    all_to_all x1, blocking collectives, shards(): lax.all_to_all(outgoing, 'slab', split_axis=3, concat_axis=2, tiled=True)  55.3 us
    all_to_all x1, blocking collectives, shards(): lax.all_to_all(stacked, 'slab', split_axis=1, concat_axis=3, tiled=True)  55 us
    dot_general x4, matrix products, forward_x(): return jnp.einsum('kx,wxz->kwz', table, field, precision=precise)  31.4 us
    dot_general x4, matrix products, inverse_x(): return jnp.einsum('xk,kwz->xwz', table, field, precision=precise)  30.2 us
    dot_general x8, matrix products, last_dim(): return jnp.dot(field, table, precision=precise)  22.9 us
  transfers between devices with their start and end apart: 9, of which 6 were waited for; matrix products, arithmetic and copies ran while one was open for 1% of the time, Pallas kernels for 0%

profile of v1, /device:TPU:1, one launch (start us, length us, event | category | flops | bytes accessed | tf_op | source)
XLA Modules:
  0.0 655.9 jit_solution(3986173771606675922)
XLA Ops:
  1.5 3.4 copy-done
  5.8 13.8 %shard_map.73 = f32[36,4,48,128]{3,2,1,0:T(8,128)S(1)} custom-call(s32[256]{0:T(256)S(1)} %fusion.103.codes, s32[1]{0:T(128)} %copy.55.count, f32[256,64,128]{2,1,0:T(8,128)S(1)} %copy-done, f32[256,128]{1,0:T(8,128)S(1)} %copy-done.2), custom_call_target="tpu_custom_call" | custom-call | tf_op jit(solution)/shard_map/pallas_call | solution.py:71
  22.2 3.0 reshape.218
  25.4 3.0 collective-permute-start
  34.7 3.8 collective-permute-start.3
  38.5 3.0 collective-permute-done.2
  41.6 8.8 %convolution_bitcast_fusion = f32[1,512,32,32]{1,3,2,0:T(8,128)} fusion(f32[32,32,512]{2,1,0:T(8,128)S(1)} %fusion.72, s32[512]{0:T(512)S(1)} %fusion.98), kind=kOutput, calls=%fused_computation.12 | convolution fusion | flops 3224895488 | bytes 4196352 | tf_op jit(solution)/shard_map/yc,ay->ca/dot_general | solution.py:226
  50.5 11.7 %convolution_negate_fusion = f32[512,1024]{1,0:T(8,128)} fusion(f32[1024,512]{1,0:T(8,128)S(1)} %bitcast.134, s32[512]{0:T(512)S(1)} %fusion.98), kind=kOutput, calls=%fused_computation.11 | convolution fusion | flops 3225419776 | bytes 4196352 | tf_op jit(solution)/shard_map/yc,ay->ca/dot_general | solution.py:227
  64.1 4.2 pad_maximum_fusion
  68.2 14.4 %copy.26 = f32[2,512,32,32]{3,2,0,1:T(8,128)} copy(f32[2,512,32,32]{1,3,2,0:T(8,128)} %pad_maximum_fusion) | data formatting | bytes 8388608 | tf_op jit(solution)/shard_map/stack | solution.py:228
  82.6 12.8 %reshape.238 = f32[8,1,131072]{2,1,0:T(1,128)} reshape(f32[512,2,32,32]{3,2,1,0:T(8,128)} %bitcast.119) | data formatting | bytes 8388608
  95.4 55.0 %all_to_all.66 = f32[8,1,131072]{2,1,0:T(1,128)} all-to-all(f32[8,1,131072]{2,1,0:T(1,128)} %reshape.238), channel_id=1, replica_groups=mesh['slab'=8,'pencil'=16] {'slab'}, dimensions={0} | all-to-all | bytes 8388608 | tf_op jit(solution)/shard_map/all_to_all | solution.py:232
  150.9 13.6 %reduce.8 = f32[8,131072]{1,0:T(8,128)} reduce(f32[8,1,131072]{2,1,0:T(1,128)} %all_to_all.66, f32[]{:T(128)} %broadcast.387), dimensions={1}, to_apply=%all_to_all.48.reduce_sub_computation | reduce | bytes 8388612 | tf_op jit(solution)/shard_map/all_to_all | solution.py:232
  164.5 13.3 %reshape.239 = f32[512,2,32,32]{3,2,1,0:T(8,128)} reshape(f32[8,131072]{1,0:T(8,128)} %reduce.8) | data formatting | bytes 8388608
  177.8 12.8 %copy.27 = f32[2,8,64,32,32]{2,4,1,3,0:T(8,128)} copy(f32[2,8,64,32,32]{4,3,0,2,1:T(8,128)} %bitcast.120) | data formatting | bytes 8388608 | tf_op jit(solution)/shard_map/all_to_all | solution.py:232
  190.7 7.3 %copy.28 = f32[2,64,32,256]{3,2,0,1:T(8,128)} copy(f32[2,64,32,256]{1,3,2,0:T(8,128)} %bitcast.124) | data formatting | bytes 8388608 | tf_op jit(solution)/shard_map/all_to_all | solution.py:232
  198.0 56.1 %all_to_all.67 = f32[2,64,32,256]{3,2,0,1:T(8,128)S(1)} all-to-all(f32[2,64,32,256]{3,2,0,1:T(8,128)} %copy.28), channel_id=1, replica_groups=mesh['slab'=8,'pencil'=16] {'pencil'}, dimensions={1} | all-to-all | bytes 8388608 | tf_op jit(solution)/shard_map/all_to_all | solution.py:231
  261.2 2.9 convolution_add_fusion
  264.1 7.7 %fusion.23 = f32[512,4,256]{2,0,1:T(8,128)S(1)} fusion(f32[4,512,256]{2,1,0:T(8,128)S(1)} %convolution_add_fusion), kind=kOutput, calls=%fused_computation.49 | convolution fusion | flops 3224895488 | bytes 4194304 | tf_op jit(solution)/shard_map/kx,wxz->kwz/dot_general | solution.py:176
  271.9 2.9 convolution_subtract_fusion
  274.8 7.5 %fusion.19 = f32[512,4,256]{2,0,1:T(8,128)S(1)} fusion(f32[4,512,256]{2,1,0:T(8,128)S(1)} %convolution_subtract_fusion), kind=kOutput, calls=%fused_computation.45 | convolution fusion | flops 3224895488 | bytes 4194304 | tf_op jit(solution)/shard_map/kx,wxz->kwz/dot_general | solution.py:176
  282.3 7.9 %add_multiply_fusion = f32[512,4,256]{2,0,1:T(8,128)S(1)} fusion(f32[512,4,256]{2,0,1:T(8,128)S(1)} %fusion.23, f32[512,4,256]{2,1,0:T(4,128)S(1)} %copy-done.8, f32[4,512,256]{2,1,0:T(8,128)S(1)} %convolution_subtract_fusion), kind=kOutput, calls=%fused_computation.10 | convolution fusion | flops 3225944064 | bytes 8388608 | tf_op jit(solution)/shard_map/kx,wxz->kwz/dot_general | solution.py:176
  290.2 7.5 %fusion.21 = f32[512,4,256]{2,0,1:T(8,128)S(1)} fusion(f32[512,4,256]{2,0,1:T(8,128)S(1)} %add_multiply_fusion), kind=kOutput, calls=%fused_computation.47 | convolution fusion | flops 3224895488 | bytes 4194304 | tf_op jit(solution)/shard_map/xk,kwz->xwz/dot_general | solution.py:180
  297.7 8.3 %subtract_multiply_fusion.1 = f32[512,4,256]{2,0,1:T(8,128)S(1)} fusion(f32[512,4,256]{2,0,1:T(8,128)S(1)} %fusion.19, f32[512,4,256]{2,1,0:T(4,128)S(1)} %copy-done.8, f32[4,512,256]{2,1,0:T(8,128)S(1)} %convolution_add_fusion), kind=kOutput, calls=%fused_computation.9 | convolution fusion | flops 3225944064 | bytes 8388608 | tf_op jit(solution)/shard_map/kx,wxz->kwz/dot_general | solution.py:176
  306.0 7.3 %fusion.17 = f32[512,4,256]{2,0,1:T(8,128)S(1)} fusion(f32[512,4,256]{2,0,1:T(8,128)S(1)} %subtract_multiply_fusion.1), kind=kOutput, calls=%fused_computation.43 | convolution fusion | flops 3224895488 | bytes 4194304 | tf_op jit(solution)/shard_map/xk,kwz->xwz/dot_general | solution.py:180
  313.4 7.6 %convolution_subtract_fusion.1 = f32[512,4,256]{2,0,1:T(8,128)S(1)} fusion(f32[512,4,256]{2,0,1:T(8,128)S(1)} %fusion.21, f32[512,4,256]{2,0,1:T(8,128)S(1)} %subtract_multiply_fusion.1), kind=kOutput, calls=%fused_computation.16 | convolution fusion | flops 3225419776 | bytes 6291456 | tf_op jit(solution)/shard_map/xk,kwz->xwz/dot_general | solution.py:180
  323.8 7.8 %convolution_add_fusion.1 = f32[512,4,256]{2,0,1:T(8,128)S(1)} fusion(f32[512,4,256]{2,0,1:T(8,128)S(1)} %fusion.17, f32[512,4,256]{2,0,1:T(8,128)S(1)} %add_multiply_fusion), kind=kOutput, calls=%fused_computation.15 | convolution fusion | flops 3225419776 | bytes 6291456 | tf_op jit(solution)/shard_map/xk,kwz->xwz/dot_general | solution.py:180
  334.4 2.9 subtract_bitcast_fusion
  342.4 5.5 copy.34
  348.0 55.3 %all_to_all.68 = f32[2,512,4,256]{1,2,0,3:T(4,128)S(1)} all-to-all(f32[2,512,4,256]{1,2,0,3:T(4,128)} %copy.34), channel_id=1, replica_groups=mesh['slab'=8,'pencil'=16] {'slab'}, dimensions={3} | all-to-all | bytes 8388608 | tf_op jit(solution)/shard_map/all_to_all | solution.py:251
  408.1 14.4 %copy.37 = f32[2,512,32,32]{3,2,0,1:T(8,128)} copy(f32[2,512,32,32]{1,3,2,0:T(8,128)} %bitcast.129) | data formatting | bytes 8388608 | tf_op jit(solution)/shard_map/all_to_all | solution.py:251
  422.4 16.0 %reshape.240 = f32[16,1,65536]{2,1,0:T(1,128)} reshape(f32[512,2,32,32]{3,2,1,0:T(8,128)} %bitcast.121) | data formatting | bytes 8388608
  438.4 4.7 all-to-all-start.3
  443.2 61.9 %all-to-all-done.3 = f32[16,1,65536]{2,1,0:T(1,128)} async-done(((f32[16,1,65536]{2,1,0:T(1,128)}), f32[16,1,65536]{2,1,0:T(1,128)}, u32[]{:S(2)}, u32[]{:S(2)}) %all-to-all-start.3) | async-done | bytes 4194336 | tf_op jit(solution)/shard_map/all_to_all | solution.py:250
  505.1 13.7 %reduce.9 = f32[16,65536]{1,0:T(8,128)} reduce(f32[16,1,65536]{2,1,0:T(1,128)} %all-to-all-done.3, f32[]{:T(128)} %broadcast.387), dimensions={1}, to_apply=%all_to_all.59.reduce_sub_computation | reduce | bytes 8388612 | tf_op jit(solution)/shard_map/all_to_all | solution.py:250
  518.8 15.1 %reshape.241 = f32[512,2,32,32]{3,2,1,0:T(8,128)} reshape(f32[16,65536]{1,0:T(8,128)} %reduce.9) | data formatting | bytes 8388608
  533.9 19.6 %copy.44 = f32[2,16,32,32,32]{2,1,4,3,0:T(8,128)} copy(f32[2,16,32,32,32]{4,3,0,2,1:T(8,128)} %bitcast.122) | data formatting | bytes 8388608 | tf_op jit(solution)/shard_map/all_to_all | solution.py:250
  553.5 11.2 %fusion.186 = (f32[1,32,16,32,32]{1,2,4,3,0:T(8,128)}, f32[1,32,16,32,32]{1,2,4,3,0:T(8,128)}) fusion(f32[2,32,16,32,32]{1,2,4,3,0:T(8,128)} %bitcast.123), kind=kLoop, calls=%fused_computation.223 | loop fusion | bytes 8388608 | tf_op jit(solution)/shard_map/slice | solution.py:270
  564.6 9.4 %copy.39 = f32[1,32,16,32,32]{3,2,4,1,0:T(8,128)} copy(f32[1,32,16,32,32]{1,2,4,3,0:T(8,128)} %get-tuple-element.54) | data formatting | bytes 4194304 | tf_op jit(solution)/shard_map/slice | solution.py:269
  574.0 6.2 squeeze.24
  580.3 9.4 %copy.40 = f32[1,32,16,32,32]{3,2,4,1,0:T(8,128)} copy(f32[1,32,16,32,32]{1,2,4,3,0:T(8,128)} %get-tuple-element.53) | data formatting | bytes 4194304 | tf_op jit(solution)/shard_map/slice | solution.py:270
  589.7 7.5 %squeeze.25 = f32[32,512,32]{1,2,0:T(8,128)} reshape(f32[1,32,16,32,32]{3,2,4,1,0:T(8,128)} %copy.40) | data formatting | bytes 4194304 | tf_op jit(solution)/shard_map/squeeze | solution.py:270
  597.2 7.3 %fusion.10 = f32[32,32,512]{2,1,0:T(8,128)S(1)} fusion(f32[32,512,32]{1,2,0:T(8,128)S(1)} %squeeze.24, s32[512]{0:T(512)S(1)} %fusion.94), kind=kOutput, calls=%fused_computation.36 | convolution fusion | flops 3224895488 | bytes 4196352 | tf_op jit(solution)/shard_map/xcz,cy->xzy/dot_general | solution.py:269
  604.6 7.8 %subtract_multiply_fusion = f32[32,32,512]{2,1,0:T(8,128)S(1)} fusion(f32[32,32,512]{2,1,0:T(8,128)S(1)} %fusion.10, f32[32,512,32]{1,2,0:T(8,128)S(1)} %copy-done.9, s32[512]{0:T(512)S(1)} %fusion.94), kind=kOutput, calls=%fused_computation.6 | convolution fusion | flops 3225944064 | bytes 6293504 | tf_op jit(solution)/shard_map/xcz,cy->xzy/dot_general | solution.py:270
  619.4 4.8 collective-permute-start.7
  624.2 7.9 %fusion.74 = f32[256,1,128]{2,1,0:T(1,128)S(1)} fusion(bf16[256,128,128]{2,1,0:T(8,128)(2,1)} %param.20, bf16[256,128,1]{1,0,2:T(8,128)(2,1)S(1)} %bitcast.135), kind=kOutput, calls=%fused_computation.98 | convolution fusion | flops 8388608 | bytes 8585216 | tf_op jit(solution)/shard_map/ntp,np->nt/dot_general | solution.py:275
  637.4 3.4 copy-done.1
  640.8 14.7 %shard_map.74 = f32[256,128]{1,0:T(8,128)} custom-call(s32[256]{0:T(256)S(1)} %copy-done.5, s32[1]{0:T(128)} %copy.55.count, s32[1,256]{1,0:T(1,128)S(1)} %get-tuple-element.68.targets, f32[256,64,128]{2,1,0:T(8,128)S(1)} %copy-done.1, f32[36,4,48,128]{3,2,1,0:T(8,128)S(1)} %pad.12.grid, f32[256,128]{1,0:T(8,128)S(1)} %bitcast.118), custom_call_target="tpu_custom_call" | custom-call | tf_op jit(solution)/shard_map/pallas_call | solution.py:129
  (73 shorter events, 48.3 us)
Async XLA Ops:
  1.5 3.4 copy-start
  4.9 0.9 copy-start.2
  5.8 13.8 %copy-start.4 = (s32[256]{0:T(256)}, s32[256]{0:T(256)S(1)}, u32[]{:S(2)}) copy-start(s32[256]{0:T(256)S(1)} %fusion.103.codes) | copy-start | bytes 3076
  25.4 5.1 collective-permute-start
  28.4 4.6 collective-permute-start.1
  33.1 8.4 %collective-permute-start.2 = (f32[2,32,512]{2,1,0:T(8,128)S(1)}, f32[2,32,512]{2,1,0:T(8,128)S(1)}, u32[]{:S(2)}, u32[]{:S(2)}) collective-permute-start(f32[2,32,512]{2,1,0:T(8,128)S(1)} %get-tuple-element.62), channel_id=1, source_target_pairs={{0,1},{1,2},{2,3},{3,4},{4,5},{5,6},{6,7},{7,8},{8,9},{9,10},{10,1... | collective-permute-start | bytes 393224 | tf_op jit(solution)/shard_map/ppermute | solution.py:158
  34.7 6.9 %collective-permute-start.3 = (f32[2,32,512]{2,1,0:T(8,128)S(1)}, f32[2,32,512]{2,1,0:T(8,128)S(1)}, u32[]{:S(2)}, u32[]{:S(2)}) collective-permute-start(f32[2,32,512]{2,1,0:T(8,128)S(1)} %get-tuple-element.61), channel_id=1, source_target_pairs={{1,0},{2,1},{3,2},{4,3},{5,4},{6,5},{7,6},{8,7},{9,8},{10,9},{11,1... | collective-permute-start | bytes 393224 | tf_op jit(solution)/shard_map/ppermute | solution.py:160
  274.8 7.5 %copy-start.8 = (f32[512,4,256]{2,1,0:T(4,128)S(1)}, f32[512,4,256]{2,1,0:T(4,128)}, u32[]{:S(2)}) copy-start(f32[512,4,256]{2,1,0:T(4,128)} %param.21) | copy-start | bytes 6291460
  438.4 4.7 copy-start.3
  438.4 66.7 %all-to-all-start.3 = ((f32[16,1,65536]{2,1,0:T(1,128)}), f32[16,1,65536]{2,1,0:T(1,128)}, u32[]{:S(2)}, u32[]{:S(2)}) async-start(f32[16,1,65536]{2,1,0:T(1,128)} %reshape.240), calls=%async_computation.3 | async-start | bytes 8388608 | tf_op jit(solution)/shard_map/all_to_all | solution.py:250
  597.2 7.4 %copy-start.9 = (f32[32,512,32]{1,2,0:T(8,128)S(1)}, f32[32,512,32]{1,2,0:T(8,128)}, u32[]{:S(2)}) copy-start(f32[32,512,32]{1,2,0:T(8,128)} %squeeze.25) | copy-start | bytes 6291460
  604.6 10.0 %copy-start.10 = (s32[256,2]{0,1:T(2,128)S(1)}, s32[256,2]{0,1:T(2,128)}, u32[]{:S(2)}) copy-start(s32[256,2]{0,1:T(2,128)} %param.19) | copy-start | bytes 6148
  612.4 11.8 %copy-start.6 = (f32[32,32,512]{2,1,0:T(8,128)}, f32[32,32,512]{2,1,0:T(8,128)S(1)}, u32[]{:S(2)}) copy-start(f32[32,32,512]{2,1,0:T(8,128)S(1)} %subtract_multiply_fusion) | copy-start | bytes 6291460
  612.5 4.1 collective-permute-start.4
  614.6 4.7 collective-permute-start.5
  619.3 12.8 %collective-permute-start.6 = (f32[2,36,512]{2,1,0:T(8,128)S(1)}, f32[2,36,512]{2,1,0:T(8,128)S(1)}, u32[]{:S(2)}, u32[]{:S(2)}) collective-permute-start(f32[2,36,512]{2,1,0:T(8,128)S(1)} %get-tuple-element.59), channel_id=1, source_target_pairs={{0,1},{1,2},{2,3},{3,4},{4,5},{5,6},{6,7},{7,8},{8,9},{9,10},{10,1... | collective-permute-start | bytes 442376 | tf_op jit(solution)/shard_map/ppermute | solution.py:158
  619.4 12.7 %collective-permute-start.7 = (f32[2,36,512]{2,1,0:T(8,128)S(1)}, f32[2,36,512]{2,1,0:T(8,128)S(1)}, u32[]{:S(2)}, u32[]{:S(2)}) collective-permute-start(f32[2,36,512]{2,1,0:T(8,128)S(1)} %get-tuple-element.60), channel_id=1, source_target_pairs={{1,0},{2,1},{3,2},{4,3},{5,4},{6,5},{7,6},{8,7},{9,8},{10,9},{11,1... | collective-permute-start | bytes 442376 | tf_op jit(solution)/shard_map/ppermute | solution.py:160
  624.2 8.0 %copy-start.7 = (f32[32,32,512]{2,1,0:T(8,128)S(1)}, f32[32,32,512]{2,1,0:T(8,128)}, u32[]{:S(2)}) copy-start(f32[32,32,512]{2,1,0:T(8,128)} %copy-done.6) | copy-start | bytes 6291460
  636.7 0.7 copy-start.5
  637.4 3.4 copy-start.1

commit v2 on v1

v2 whole, which is shorter than its diff:
```python
import jax
import jax.numpy as jnp
import ml_dtypes
import numpy as np
from jax import lax
from jax.experimental import pallas as pl
from jax.experimental.pallas import tpu as pltpu
from jax.sharding import PartitionSpec as P

NX, NY, NZ, BOX = 512, 512, 256, 64
GROUP = 16
F32, BF16 = jnp.float32, jnp.bfloat16


def halves(value):
    high = value.astype(BF16)
    return high, (value - high.astype(F32)).astype(BF16)


def lane_sums(value):
    ones = jnp.ones((128, 128), BF16)
    high, low = halves(value)
    return jnp.dot(high, ones, preferred_element_type=F32) + jnp.dot(low, ones, preferred_element_type=F32)


def window(code):
    x_at = code % 32
    z_at = code // 32 % 32
    y_at = code // 1024
    tile_0 = y_at // 128
    return x_at, z_at + 6, tile_0, (tile_0 + 1) % 4, y_at % 128


def window_masks(lane_0):
    row = lax.broadcasted_iota(jnp.int32, (8, 128), 0)
    lane = lax.broadcasted_iota(jnp.int32, (8, 128), 1)
    shifted = lane - row // 4 - lane_0
    return (shifted == 0, shifted == 2), (shifted == -128, shifted == -126)


def scatter_kernel(codes, count, projection, charges, grid, values):
    step = pl.program_id(0)

    @pl.when(step == 0)
    def _():
        def clear(x, carry):
            grid[x] = jnp.zeros(grid.shape[1:], F32)
            return carry

        lax.fori_loop(0, grid.shape[0], clear, 0)

    slot = step * GROUP + lax.broadcasted_iota(jnp.int32, (GROUP, 128), 0)
    masked = jnp.where(slot < count[0], charges[...], 0.0)
    products = projection[...] * masked[:, None, :]
    values[...] = lane_sums(products.reshape(GROUP * BOX, 128)).reshape(GROUP, BOX, 128)
    top = lax.broadcasted_iota(jnp.int32, (8, 128), 0) < 4

    def place(b, carry):
        x_at, z_row, tile_0, tile_1, lane_0 = window(codes[step * GROUP + b])
        for tile, masks in zip((tile_0, tile_1), window_masks(lane_0)):
            for i in range(4):
                patch = jnp.where(masks[0], values[b, 16 * i : 16 * i + 8], 0.0)
                patch = jnp.where(masks[1], values[b, 16 * i + 8 : 16 * i + 16], patch)
                patch = jnp.where(top, patch + pltpu.roll(patch, 4, 0), 0.0)
                grid[x_at + i, tile, pl.ds(z_row, 8), :] += patch
        return carry

    lax.fori_loop(0, GROUP, place, 0)


def scatter(codes, count, projection, charges):
    slots = charges.shape[0]
    return pl.pallas_call(
        scatter_kernel,
        grid_spec=pltpu.PrefetchScalarGridSpec(
            num_scalar_prefetch=2,
            grid=(slots // GROUP,),
            in_specs=[
                pl.BlockSpec((GROUP, BOX, 128), lambda i, *_: (i, 0, 0)),
                pl.BlockSpec((GROUP, 128), lambda i, *_: (i, 0)),
            ],
            out_specs=pl.BlockSpec((36, 4, 48, 128), lambda i, *_: (0, 0, 0, 0)),
            scratch_shapes=[pltpu.VMEM((GROUP, BOX, 128), F32)],
        ),
        out_shape=jax.ShapeDtypeStruct((36, 4, 48, 128), F32),
        compiler_params=pltpu.CompilerParams(vmem_limit_bytes=32 << 20),
    )(codes, count, projection, charges)


def gather_kernel(codes, count, targets, projection, grid, pair_terms, out, near, picked):
    step = pl.program_id(0)

    @pl.when(step == 0)
    def _():
        slots, pairs = near.shape[0], pair_terms.shape[0]
        slot = lax.broadcasted_iota(jnp.int32, (slots, pairs), 0)
        chosen = jnp.where(slot == targets[...], 1.0, 0.0).astype(BF16)
        rest = pair_terms[...]
        total = jnp.zeros(near.shape, F32)
        for _ in range(3):
            part = rest.astype(BF16)
            rest = rest - part.astype(F32)
            total = total + jnp.dot(chosen, part, preferred_element_type=F32)
        near[...] = total

    top = lax.broadcasted_iota(jnp.int32, (8, 128), 0) < 4

    def pick(b, carry):
        x_at, z_row, tile_0, tile_1, lane_0 = window(codes[step * GROUP + b])
        masks_0, masks_1 = window_masks(lane_0)
        for i in range(4):
            both = []
            for tile in (tile_0, tile_1):
                rows = grid[x_at + i, tile, pl.ds(z_row, 8), :]
                both.append(jnp.where(top, rows, pltpu.roll(rows, 4, 0)))
            for j in range(2):
                value = jnp.where(masks_0[j], both[0], jnp.where(masks_1[j], both[1], 0.0))
                picked[b, 16 * i + 8 * j : 16 * i + 8 * j + 8] = value
        return carry

    lax.fori_loop(0, GROUP, pick, 0)
    box = lane_sums(picked[...].reshape(GROUP * BOX, 128)).reshape(GROUP, BOX, 128)
    far = jnp.sum(projection[...] * box, axis=1)
    slot = step * GROUP + lax.broadcasted_iota(jnp.int32, (GROUP, 128), 0)
    total = far + near[pl.ds(pl.multiple_of(step * GROUP, GROUP), GROUP), :]
    out[...] = jnp.where(slot < count[0], total, 0.0)


def gather(codes, count, targets, projection, grid, pair_terms):
    slots, pairs = projection.shape[0], pair_terms.shape[0]
    return pl.pallas_call(
        gather_kernel,
        grid_spec=pltpu.PrefetchScalarGridSpec(
            num_scalar_prefetch=2,
            grid=(slots // GROUP,),
            in_specs=[
                pl.BlockSpec((1, pairs), lambda i, *_: (0, 0)),
                pl.BlockSpec((GROUP, BOX, 128), lambda i, *_: (i, 0, 0)),
                pl.BlockSpec((36, 4, 48, 128), lambda i, *_: (0, 0, 0, 0)),
                pl.BlockSpec((pairs, 128), lambda i, *_: (0, 0)),
            ],
            out_specs=pl.BlockSpec((GROUP, 128), lambda i, *_: (i, 0)),
            scratch_shapes=[pltpu.VMEM((slots, 128), F32), pltpu.VMEM((GROUP, BOX, 128), F32)],
        ),
        out_shape=jax.ShapeDtypeStruct((slots, 128), F32),
        compiler_params=pltpu.CompilerParams(vmem_limit_bytes=32 << 20),
    )(codes, count, targets, projection, grid, pair_terms)


CHUNKS = 4
MESH = pl.DeviceIdType.MESH


def phases(product, length):
    angle = 2.0 * np.pi * (product % length) / length
    return np.cos(angle), np.sin(angle)


def split_table(table):
    table = table.astype(np.float32)
    high = table.astype(ml_dtypes.bfloat16)
    return high, (table - high.astype(np.float32)).astype(ml_dtypes.bfloat16)


def y_tables():
    slab, part, pencil = np.meshgrid(np.arange(8), np.arange(2), np.arange(16), indexing="ij")
    device = (slab * 16 + pencil).reshape(-1, 1)
    part = part.reshape(-1, 1)
    even = np.where(device < 64, 4 * device, 4 * device + 2)
    odd = 4 * device + 1
    position = np.arange(256)[None, :]
    result = []
    for freq in (even, odd):
        cos, sin = phases(freq * position, NY)
        table = np.where(part == 0, cos, -sin)
        if freq is even:
            table[(device[:, 0] == 0) & (part[:, 0] == 1)] = 1.0 - 2.0 * (position[0] % 2)
        result.append(table)
    return np.stack(result)


def z_table():
    position = np.arange(NZ)
    cos, sin = phases(position[:, None] * position[None, :], NZ)
    return np.block([[cos, -sin], [sin, cos]])


def x_tables():
    position = np.arange(256)
    result = []
    for parity in range(2):
        cos, sin = phases((2 * position[:, None] + parity) * position[None, :], NX)
        result.append(np.concatenate([cos, sin], axis=1))
        if parity:
            result.append(np.concatenate([cos.T, sin.T], axis=1))
    return np.stack(result)


def dot_3(left, right, dims=((1,), (0,))):
    def one(a, b):
        return lax.dot_general(a, b, (dims, ((), ())), preferred_element_type=F32)

    return one(left[0], right[0]) + (one(left[0], right[1]) + one(left[1], right[0]))


def swap_groups(tiles):
    lane = lax.broadcasted_iota(jnp.int32, tiles[0].shape, 1)
    low, even = lane < 64, lane % 64 < 32
    firsts, lasts = [], []
    for a, b in ((tiles[0], tiles[2]), (tiles[1], tiles[3])):
        firsts.append(jnp.where(low, a, pltpu.roll(b, 64, 1)))
        lasts.append(jnp.where(low, pltpu.roll(a, 64, 1), b))
    result = []
    for a, b in (firsts, lasts):
        result.append(jnp.where(even, a, pltpu.roll(b, 32, 1)))
        result.append(jnp.where(even, pltpu.roll(a, 96, 1), b))
    return result


def field_kernel(
    grid, kernel, nyquist, ty_high, ty_low, tz_high, tz_low, tx_high, tx_low,
    out,
    charge, z_out, z_in, x_in, sent_1, got_1, sent_2, got_2, spectra, back_2, took_2, back_1, took_1, lines,
    last_z_out, last_z_in, last_x_out, last_x_in,
    rim_send, rim_recv, send_1, recv_1, send_2, recv_2, send_3, recv_3, send_4, recv_4,
):
    slab, pencil = lax.axis_index("slab"), lax.axis_index("pencil")
    n_slab, n_pencil = 8, 16

    def on_slab(step):
        return (lax.rem(slab + step, n_slab), pencil)

    def on_pencil(step):
        return (slab, lax.rem(pencil + step, n_pencil))

    def remote(source, target, send_sem, recv_sem, device):
        return pltpu.make_async_remote_copy(
            src_ref=source, dst_ref=target, send_sem=send_sem, recv_sem=recv_sem, device_id=device, device_id_type=MESH
        )

    def wait_recv(ref, sem):
        remote(ref, ref, sem, sem, on_slab(1)).wait_recv()

    def wait_send(ref, sem):
        remote(ref, ref, sem, sem, on_slab(1)).wait_send()

    barrier = pltpu.get_barrier_semaphore()

    def greet_slab(step, carry):
        pl.semaphore_signal(barrier, inc=1, device_id=on_slab(step), device_id_type=MESH)
        return carry

    def greet_pencil(step, carry):
        pl.semaphore_signal(barrier, inc=1, device_id=on_pencil(step), device_id_type=MESH)
        return carry

    lax.fori_loop(1, n_slab, greet_slab, 0)
    lax.fori_loop(1, n_pencil, greet_pencil, 0)

    def pack_rims(x, carry):
        for tile in range(4):
            z_out[0, x, 2 * tile : 2 * tile + 2, :] = grid[x, tile, 6:8, :]
            z_out[1, x, 2 * tile : 2 * tile + 2, :] = grid[x, tile, 40:42, :]
        return carry

    lax.fori_loop(0, 36, pack_rims, 0)
    pl.semaphore_wait(barrier, n_slab + n_pencil - 2)
    remote(z_out.at[0], z_in.at[1], rim_send.at[0], rim_recv.at[0], on_slab(n_slab - 1)).start()
    remote(z_out.at[1], z_in.at[0], rim_send.at[1], rim_recv.at[1], on_slab(1)).start()
    def clear(x, carry):
        out[x] = jnp.zeros(out.shape[1:], F32)
        return carry

    lax.fori_loop(0, 36, clear, 0)
    wait_recv(z_in.at[1], rim_recv.at[0])
    wait_recv(z_in.at[0], rim_recv.at[1])

    def add_rims(step, carry):
        x = lax.rem(step + 34, 36)
        for tile in range(4):
            charge[x, tile] = grid[x, tile, 8:40, :]
            charge[x, tile, 0:2, :] += z_in[0, x, 2 * tile : 2 * tile + 2, :]
            charge[x, tile, 30:32, :] += z_in[1, x, 2 * tile : 2 * tile + 2, :]
        return carry

    lax.fori_loop(0, 4, add_rims, 0)
    remote(charge.at[0:2], x_in.at[1], rim_send.at[2], rim_recv.at[2], on_pencil(n_pencil - 1)).start()
    remote(charge.at[34:36], x_in.at[0], rim_send.at[3], rim_recv.at[3], on_pencil(1)).start()
    lax.fori_loop(4, 36, add_rims, 0)

    def forward_y(step, carry):
        chunk = lax.rem(step + 1, CHUNKS)

        @pl.when(step == 2)
        def _():
            wait_recv(x_in.at[1], rim_recv.at[2])
            wait_recv(x_in.at[0], rim_recv.at[3])
            charge[2:4] += x_in[0]
            charge[32:34] += x_in[1]

        tiles = [charge[pl.ds(2 + 8 * chunk, 8), tile].reshape(256, 128) for tile in range(4)]
        for parity in range(2):
            if parity:
                halved = [tiles[0] - tiles[2], tiles[1] - tiles[3]]
            else:
                halved = [tiles[0] + tiles[2], tiles[1] + tiles[3]]
            columns = halves(jnp.concatenate(halved, axis=1))
            freqs = dot_3((ty_high[parity], ty_low[parity]), columns, ((1,), (1,)))
            sent_1[chunk, :, 32 * parity : 32 * parity + 32, :] = freqs.reshape(n_slab, 32, 256)
        got_1[chunk, slab] = sent_1[chunk, slab]

        def send(k, carry):
            device = on_slab(k)
            remote(sent_1.at[chunk, device[0]], got_1.at[chunk, slab], send_1, recv_1.at[chunk], device).start()
            return carry

        return lax.fori_loop(1, n_slab, send, carry)

    lax.fori_loop(0, CHUNKS, forward_y, 0)

    def forward_z(step, carry):
        chunk = lax.rem(step + 1, CHUNKS)
        wait_recv(got_1.at[chunk, 0 : n_slab - 1], recv_1.at[chunk])
        for h in range(2):
            for q in range(2):
                tiles = swap_groups([got_1[chunk, 4 * q + s, :, 128 * h : 128 * h + 128] for s in range(4)])
                for a in range(4):
                    for parity in range(2):
                        for part in range(2):
                            row = 32 * parity + 16 * part
                            lines[2 * part + q, pl.ds(128 * parity + 4 * h + a, 16, stride=8), :] = tiles[a][row : row + 16]
        rows = halves(jnp.concatenate([lines[i] for i in range(4)], axis=1))
        freqs = dot_3(rows, (tz_high[...], tz_low[...]))
        for parity in range(2):
            for part in range(2):
                block = freqs[128 * parity : 128 * parity + 128, 256 * part : 256 * part + 256]
                sent_2[chunk, :, parity, part] = block.reshape(n_pencil, 8, 256)
        mine = pl.ds(pl.multiple_of(pencil * 32 + chunk * 8, 8), 8)
        got_2[:, :, mine, :] = sent_2[chunk, pencil]

        def send(k, carry):
            device = on_pencil(k)
            remote(sent_2.at[chunk, device[1]], got_2.at[:, :, mine, :], send_2, recv_2, device).start()
            return carry

        return lax.fori_loop(1, n_pencil, send, carry)

    lax.fori_loop(0, CHUNKS, forward_z, 0)
    wait_recv(got_2.at[:, :, 0 : 32 * (n_pencil - 1), :], recv_2)

    first = jnp.logical_and(slab == 0, pencil == 0)
    unit = 1.0 / (NX * NY * NZ)

    def level(ref, start, stride):
        return jnp.concatenate([ref[pl.ds(start + i, 256, stride=stride), :] for i in range(2)], axis=1)

    def stacked(real, imag):
        real, imag = halves(real), halves(imag)
        return tuple(
            jnp.concatenate([jnp.concatenate([r, i], axis=1), jnp.concatenate([i, -r], axis=1)], axis=0)
            for r, i in zip(real, imag)
        )

    for parity in range(2):
        for kx in range(2):
            parts = []
            for part in range(2):
                low, high = got_2[parity, part, 0:256, :], got_2[parity, part, 256:512, :]
                parts.append(low - high if kx else low + high)
            table = (tx_high[kx], tx_low[kx])
            found = dot_3(table, stacked(*parts))
            if parity:
                green = jnp.concatenate(
                    [kernel[pl.ds(8 * kx + 4 * i + 1, 256, stride=16), :] for i in range(2)], axis=1
                ) * (2.0 * unit)
            else:
                own = jnp.where(slab < 4, 0, 2)
                green = jnp.concatenate(
                    [kernel[pl.ds(own + 8 * kx + 4 * i, 256, stride=16), :] for i in range(2)], axis=1
                ) * jnp.where(first, unit, 2.0 * unit)
            spectra[kx, 0] = found[:, 0:256] * green
            spectra[kx, 1] = found[:, 256:512] * green
            if not parity:

                @pl.when(first)
                def _():
                    other = level(nyquist, 2 * kx, 4) * unit
                    row = lax.broadcasted_iota(jnp.int32, (256, 256), 0)
                    lane = lax.broadcasted_iota(jnp.int32, (256, 256), 1)
                    mirror = jnp.where((row + lane) % 256 == 0, 1.0, 0.0).astype(BF16)
                    flipped = [
                        sum(jnp.dot(piece, mirror, preferred_element_type=F32) for piece in halves(value)) for value in parts
                    ]
                    twin = dot_3(table, stacked(flipped[0], -flipped[1]))
                    mean, rest = 0.5 * (green + other), 0.5 * (green - other)
                    for part in range(2):
                        lanes = slice(256 * part, 256 * part + 256)
                        spectra[kx, part] = mean * found[:, lanes] + rest * twin[:, lanes]

        ends = []
        for kx in range(2):
            table = (tx_high[2 * kx], tx_low[2 * kx])
            real, imag = halves(spectra[kx, 0]), halves(spectra[kx, 1])
            right = tuple(
                jnp.concatenate([jnp.concatenate([r, i], axis=1), jnp.concatenate([-i, r], axis=1)], axis=0)
                for r, i in zip(real, imag)
            )
            ends.append(dot_3(table, right))
        for part in range(2):
            lanes = slice(256 * part, 256 * part + 256)
            back_2[parity, part, 0:256, :] = ends[0][:, lanes] + ends[1][:, lanes]
            back_2[parity, part, 256:512, :] = ends[0][:, lanes] - ends[1][:, lanes]

    def return_x(chunk, carry):
        own = pl.ds(pl.multiple_of(pencil * 32 + chunk * 8, 8), 8)
        took_2[chunk, pencil] = back_2[:, :, own, :]

        def send(k, carry):
            device = on_pencil(k)
            rows = pl.ds(pl.multiple_of(device[1] * 32 + chunk * 8, 8), 8)
            remote(back_2.at[:, :, rows, :], took_2.at[chunk, pencil], send_3, recv_3.at[chunk], device).start()
            return carry

        return lax.fori_loop(1, n_pencil, send, carry)

    lax.fori_loop(0, CHUNKS, return_x, 0)

    def inverse_z(chunk, carry):
        wait_recv(took_2.at[chunk, 0 : n_pencil - 1], recv_3.at[chunk])
        blocks = []
        for parity in range(2):
            blocks.append(jnp.concatenate([took_2[chunk, :, parity, part].reshape(128, 256) for part in range(2)], axis=1))
        rows = halves(jnp.concatenate(blocks, axis=0))
        space = dot_3(rows, (tz_high[...], tz_low[...]), ((1,), (1,)))
        for i in range(4):
            lines[i] = space[:, 128 * i : 128 * i + 128]
        for h in range(2):
            for q in range(2):
                tiles = []
                for a in range(4):
                    tiles.append(
                        jnp.concatenate(
                            [
                                lines[2 * part + q, pl.ds(128 * parity + 4 * h + a, 16, stride=8), :]
                                for parity in range(2)
                                for part in range(2)
                            ],
                            axis=0,
                        )
                    )
                for s, tile in enumerate(swap_groups(tiles)):
                    back_1[chunk, 4 * q + s, :, 128 * h : 128 * h + 128] = tile
        took_1[chunk, slab] = back_1[chunk, slab]

        def send(k, carry):
            device = on_slab(k)
            remote(back_1.at[chunk, device[0]], took_1.at[chunk, slab], send_4, recv_4.at[chunk], device).start()
            return carry

        return lax.fori_loop(1, n_slab, send, carry)

    lax.fori_loop(0, CHUNKS, inverse_z, 0)

    def inverse_y(chunk, carry):
        wait_recv(took_1.at[chunk, 0 : n_slab - 1], recv_4.at[chunk])
        ends = []
        for parity in range(2):
            columns = took_1[chunk, :, 32 * parity : 32 * parity + 32, :].reshape(256, 256).T
            ends.append(dot_3(halves(columns), (ty_high[parity], ty_low[parity])))
        space = (ends[0] + ends[1], ends[0] - ends[1])
        for tile in range(4):
            lanes = slice(128 * (tile % 2), 128 * (tile % 2) + 128)
            cells = space[tile // 2][:, lanes].reshape(8, 32, 128)
            out[pl.ds(2 + 8 * chunk, 8), tile, 8:40, :] = cells
            last_z_out[chunk, 0, :, 2 * tile : 2 * tile + 2, :] = cells[:, 0:2, :]
            last_z_out[chunk, 1, :, 2 * tile : 2 * tile + 2, :] = cells[:, 30:32, :]
        remote(
            last_z_out.at[chunk, 0], last_z_in.at[chunk, 1], rim_send.at[4], rim_recv.at[4], on_slab(n_slab - 1)
        ).start()
        remote(last_z_out.at[chunk, 1], last_z_in.at[chunk, 0], rim_send.at[5], rim_recv.at[5], on_slab(1)).start()
        return carry

    lax.fori_loop(0, CHUNKS, inverse_y, 0)
    wait_recv(last_z_in.at[:, 1], rim_recv.at[4])
    wait_recv(last_z_in.at[:, 0], rim_recv.at[5])

    def spread(step, carry):
        for tile in range(4):
            out[2 + step, tile, 6:8, :] = last_z_in[step // 8, 0, step % 8, 2 * tile : 2 * tile + 2, :]
            out[2 + step, tile, 40:42, :] = last_z_in[step // 8, 1, step % 8, 2 * tile : 2 * tile + 2, :]
        return carry

    lax.fori_loop(0, 32, spread, 0)
    last_x_out[0] = out[2:4]
    last_x_out[1] = out[32:34]
    remote(last_x_out.at[0], last_x_in.at[1], rim_send.at[6], rim_recv.at[6], on_pencil(n_pencil - 1)).start()
    remote(last_x_out.at[1], last_x_in.at[0], rim_send.at[7], rim_recv.at[7], on_pencil(1)).start()
    wait_send(z_out.at[0], rim_send.at[0])
    wait_send(z_out.at[1], rim_send.at[1])
    wait_send(charge.at[0:2], rim_send.at[2])
    wait_send(charge.at[34:36], rim_send.at[3])
    wait_send(sent_1.at[:, 0 : n_slab - 1], send_1)
    wait_send(got_2.at[:, :, 0 : 32 * (n_pencil - 1), :], send_2)
    wait_send(got_2.at[:, :, 0 : 32 * (n_pencil - 1), :], send_3)
    wait_send(back_1.at[:, 0 : n_slab - 1], send_4)
    wait_send(last_z_out.at[:, 0], rim_send.at[4])
    wait_send(last_z_out.at[:, 1], rim_send.at[5])
    wait_recv(last_x_in.at[1], rim_recv.at[6])
    wait_recv(last_x_in.at[0], rim_recv.at[7])
    out[0:2] = last_x_in[0]
    out[34:36] = last_x_in[1]
    wait_send(last_x_out.at[0], rim_send.at[6])
    wait_send(last_x_out.at[1], rim_send.at[7])


def field(grid, kernel, nyquist):
    ty, tz, tx = (split_table(table) for table in (y_tables(), z_table(), x_tables()))
    dma = pltpu.SemaphoreType.DMA
    vmem = pltpu.VMEM
    operands = (grid, kernel, nyquist, *map(jnp.asarray, (*ty, *tz, *tx)))
    return pl.pallas_call(
        field_kernel,
        in_specs=[pl.BlockSpec(memory_space=vmem)] * len(operands),
        out_specs=pl.BlockSpec(memory_space=vmem),
        out_shape=jax.ShapeDtypeStruct((36, 4, 48, 128), F32),
        scratch_shapes=[
            vmem((36, 4, 32, 128), F32),
            vmem((2, 36, 8, 128), F32),
            vmem((2, 36, 8, 128), F32),
            vmem((2, 2, 4, 32, 128), F32),
            vmem((CHUNKS, 8, 64, 256), F32),
            vmem((CHUNKS, 8, 64, 256), F32),
            vmem((CHUNKS, 16, 2, 2, 8, 256), F32),
            vmem((2, 2, 512, 256), F32),
            vmem((2, 2, 256, 256), F32),
            vmem((2, 2, 512, 256), F32),
            vmem((CHUNKS, 16, 2, 2, 8, 256), F32),
            vmem((CHUNKS, 8, 64, 256), F32),
            vmem((CHUNKS, 8, 64, 256), F32),
            vmem((4, 256, 128), F32),
            vmem((CHUNKS, 2, 8, 8, 128), F32),
            vmem((CHUNKS, 2, 8, 8, 128), F32),
            vmem((2, 2, 4, 48, 128), F32),
            vmem((2, 2, 4, 48, 128), F32),
            dma((8,)),
            dma((8,)),
            dma,
            dma((CHUNKS,)),
            dma,
            dma,
            dma,
            dma((CHUNKS,)),
            dma,
            dma((CHUNKS,)),
        ],
        compiler_params=pltpu.CompilerParams(
            collective_id=0, has_side_effects=True, vmem_limit_bytes=56 << 20
        ),
        cost_estimate=pl.CostEstimate(flops=10**10, bytes_accessed=10**7, transcendentals=0),
    )(*operands)


def shards(charges, projection, anchors, block_count, near_pairs, near_matrices, kernel_hat):
    slot_count, panels = charges.shape
    x_start = lax.axis_index("pencil") * 32
    z_start = lax.axis_index("slab") * 32
    nyquist = lax.ppermute(kernel_hat[:, 0, :], ("slab", "pencil"), [(64, 0)])
    local = anchors - jnp.stack([x_start, 2, z_start])[None, :]
    codes = local[:, 0] + 32 * local[:, 2] + 1024 * (local[:, 1] % NY)
    grid = scatter(codes, block_count, projection, charges)
    levels = jnp.transpose(kernel_hat.reshape(NX, 4, 2, 128), (0, 2, 1, 3)).reshape(NX * 8, 128)
    potential = field(grid, levels, nyquist.reshape(NX * 2, 128))
    in_use = jnp.arange(slot_count, dtype=jnp.int32) < block_count[0]
    coarse = jnp.where(in_use[:, None], charges, 0.0).astype(BF16)
    sources = coarse[near_pairs[:, 1]]
    pair_terms = jnp.einsum("ntp,np->nt", near_matrices, sources, preferred_element_type=F32)
    return gather(codes, block_count, near_pairs[:, 0][None, :], projection, potential, pair_terms)


def solution(mesh):
    return jax.shard_map(
        shards,
        mesh=mesh,
        in_specs=(
            P(("slab", "pencil"), None),
            P(("slab", "pencil"), None, None),
            P(("slab", "pencil"), None),
            P(("slab", "pencil")),
            P(("slab", "pencil"), None),
            P(("slab", "pencil"), None, None),
            P(None, ("slab", "pencil"), None),
        ),
        out_specs=P(("slab", "pencil"), None),
        check_vma=False,
    )
```

time: 662 us -> 159 us (0.24)
  local copies, waits for them, and re-layouts: 203 us -> 15.1 us
  blocking collectives: 166 us -> 0 us
  matrix products: 128 us -> 7.78 us
  Pallas kernels: 28.5 us -> 131 us
  waiting for transfers between devices: 72.8 us -> 0.01 us
  other arithmetic: 35.5 us -> 2.64 us
  starting transfers between devices: 19.8 us -> 0.69 us
    all_to_all x3 -> x0, blocking collectives: 166 us -> none  [the longest x1 56.1 us: shards(): lax.all_to_all(lax.all_to_all(stacked, 'slab', split_axis=1, concat_axis=...]
    dot_general x21 -> x1, matrix products: 128 us -> 7.78 us  [shards(): jnp.einsum('ntp,np->nt', near_matrices, sources, preferred_element_type=F32)]
    pallas_call x0 -> x1, Pallas kernels: none -> 103 us  [field(): pl.pallas_call(field_kernel, in_specs=[pl.BlockSpec(memory_space=vmem)] *...]
    all_to_all x1 -> x0, waiting for transfers between devices: 61.9 us -> none  [shards(): lax.all_to_all(lax.all_to_all(outgoing, 'slab', split_axis=3, concat_axis...]
    all_to_all x8 -> x0, local copies, waits for them, and re-layouts: 60 us -> none  [the longest x3 20.7 us: shards(): lax.all_to_all(stacked, 'slab', split_axis=1, concat_axis=3, tiled=True)]
    unnamed x26 -> x11, local copies, waits for them, and re-layouts: 65.2 us -> 11.4 us
    slice x11 -> x1, local copies, waits for them, and re-layouts: 31.7 us -> 1.95 us  [shards(): nyquist = lax.ppermute(kernel_hat[:, 0, :], ('slab', 'pencil'), [(64, 0)])]
    all_to_all x2 -> x0, other arithmetic: 27.2 us -> none  [the longest x1 13.7 us: shards(): lax.all_to_all(lax.all_to_all(outgoing, 'slab', split_axis=3, concat_axis...]
  transfers between devices with their start and end apart: 9 -> 1, of which waited for: 6 -> 0; matrix products, arithmetic and copies ran while one was open for 1% -> 7% of each run, Pallas kernels for 0% -> 9%
where the time goes in v2:
time: 159 us; the launch traced here: 158 us
  Pallas kernels  131 us (82%)
  local copies, waits for them, and re-layouts  15.1 us (9%)
  matrix products  7.78 us (5%)
  other arithmetic  2.64 us (2%)
    pallas_call x1, Pallas kernels, field(): pl.pallas_call(field_kernel, in_specs=[pl.BlockSpec(memory_space=vmem)] *...  103 us
    pallas_call x1, Pallas kernels, gather(): pl.pallas_call(gather_kernel, grid_spec=pltpu.PrefetchScalarGridSpec(num_...  14.7 us
    pallas_call x1, Pallas kernels, scatter(): pl.pallas_call(scatter_kernel, grid_spec=pltpu.PrefetchScalarGridSpec(num...  13.8 us
    unnamed x11, local copies, waits for them, and re-layouts  11.4 us
    dot_general x1, matrix products, shards(): jnp.einsum('ntp,np->nt', near_matrices, sources, preferred_element_type=F32)  7.78 us
  transfers between devices with their start and end apart: 1, of which 0 were waited for; matrix products, arithmetic and copies ran while one was open for 7% of the time, Pallas kernels for 9%

profile of v2, /device:TPU:1, one launch (start us, length us, event | category | flops | bytes accessed | tf_op | source)
XLA Modules:
  0.0 158.1 jit_solution(1446640459047074607)
XLA Ops:
  0.0 2.0 %slice.22 = f32[512,1,256]{2,1,0:T(1,128)S(1)} slice(f32[512,4,256]{2,1,0:T(4,128)} %param.19), slice={[0:512], [0:1], [0:256]} | slice | bytes 1048576 | tf_op jit(solution)/shard_map/slice | solution.py:567
  2.0 0.7 collective-permute-start
  2.7 0.1 pad_add_fusion
  2.8 0.8 broadcast_subtract_fusion
  4.2 0.8 compare_select_fusion
  5.0 1.0 select_convert_fusion
  6.0 0.0 copy-start
  6.0 3.4 %copy-done = f32[256,64,128]{2,1,0:T(8,128)S(1)} copy-done((f32[256,64,128]{2,1,0:T(8,128)S(1)}, f32[256,64,128]{2,1,0:T(8,128)}, u32[]{:S(2)}) %copy-start) | copy-done | bytes 8388632
  9.4 0.0 copy-start.4
  9.4 0.9 copy-done.4
  10.3 13.8 %shard_map.127.grid = f32[36,4,48,128]{3,2,1,0:T(8,128)S(1)} custom-call(s32[256]{0:T(256)S(1)} %fusion.3.codes, s32[1]{0:T(128)} %copy.24.count, f32[256,64,128]{2,1,0:T(8,128)S(1)} %copy-done, f32[256,128]{1,0:T(8,128)S(1)} %copy-done.4), custom_call_target="tpu_custom_call" | custom-call | tf_op jit(solution)/shard_map/pallas_call | solution.py:73
  24.1 0.0 copy-start.2
  24.1 1.7 %copy-done.2 = f32[36,4,48,128]{3,2,1,0:T(8,128)} copy-done((f32[36,4,48,128]{3,2,1,0:T(8,128)}, f32[36,4,48,128]{3,2,1,0:T(8,128)S(1)}, u32[]{:S(2)}) %copy-start.2) | copy-done | bytes 3538968
  25.9 0.9 gather_fusion
  26.7 7.8 %fusion = f32[256,1,128]{2,1,0:T(1,128)S(1)} fusion(bf16[256,128,128]{2,1,0:T(8,128)(2,1)} %param.18, bf16[256,128,1]{1,0,2:T(8,128)(2,1)S(1)} %bitcast.22), kind=kOutput, calls=%fused_computation.2 | convolution fusion | flops 8388608 | bytes 8585216 | tf_op jit(solution)/shard_map/ntp,np->nt/dot_general | solution.py:576
  34.5 0.0 collective-permute-done
  34.5 0.9 reshape.19.nyquist
  35.4 102.7 %shard_map.128.grid = f32[36,4,48,128]{3,2,1,0:T(8,128)} custom-call(f32[36,4,48,128]{3,2,1,0:T(8,128)} %copy-done.2, f32[4096,128]{1,0:T(8,128)} %bitcast.24, f32[1024,128]{1,0:T(8,128)} %reshape.19.nyquist, bf16[2,256,256]{2,1,0:T(8,128)(2,1)} %constant.48.clone.ty_high, bf16[2,256,256]{2,1,0:T(8,128)(2,1)} %constant.49.clone.ty_low, ...), custom_call_target="tpu_custom_call" | custom-call | flops 10000000000 | bytes 10000000 | tf_op jit(solution)/shard_map/pallas_call | solution.py:521
  138.0 0.0 copy-start.1
  138.0 3.4 %copy-done.1 = f32[256,64,128]{2,1,0:T(8,128)S(1)} copy-done((f32[256,64,128]{2,1,0:T(8,128)S(1)}, f32[256,64,128]{2,1,0:T(8,128)}, u32[]{:S(2)}) %copy-start.1) | copy-done | bytes 8388632
  141.4 0.0 copy-start.3
  141.4 2.0 %copy-done.3 = f32[36,4,48,128]{3,2,1,0:T(8,128)S(1)} copy-done((f32[36,4,48,128]{3,2,1,0:T(8,128)S(1)}, f32[36,4,48,128]{3,2,1,0:T(8,128)}, u32[]{:S(2)}) %copy-start.3) | copy-done | bytes 3538968
  143.4 14.7 %shard_map.129 = f32[256,128]{1,0:T(8,128)} custom-call(s32[256]{0:T(256)S(1)} %fusion.3.codes, s32[1]{0:T(128)} %copy.24.count, s32[1,256]{1,0:T(1,128)S(1)} %get-tuple-element.8.targets, f32[256,64,128]{2,1,0:T(8,128)S(1)} %copy-done.1, f32[36,4,48,128]{3,2,1,0:T(8,128)S(1)} %copy-done.3, f32[256,128]{1,0:T(8,128)S(1)} %bitcast.21), custom_call_target="tpu_custom_call" | custom-call | tf_op jit(solution)/shard_map/pallas_call | solution.py:131
  (5 shorter events, 0.1 us)
Async XLA Ops:
  2.0 32.5 %collective-permute-start = (f32[512,256]{1,0:T(8,128)S(1)}, f32[512,256]{1,0:T(8,128)S(1)}, u32[]{:S(2)}, u32[]{:S(2)}) collective-permute-start(f32[512,256]{1,0:T(8,128)S(1)} %bitcast.23), channel_id=1, source_target_pairs={{64,0}} | collective-permute-start | bytes 1572872 | tf_op jit(solution)/shard_map/ppermute | solution.py:567
  6.0 3.4 %copy-start = (f32[256,64,128]{2,1,0:T(8,128)S(1)}, f32[256,64,128]{2,1,0:T(8,128)}, u32[]{:S(2)}) copy-start(f32[256,64,128]{2,1,0:T(8,128)} %projection.3) | copy-start | bytes 25165828
  9.4 0.9 copy-start.4
  24.1 1.8 %copy-start.2 = (f32[36,4,48,128]{3,2,1,0:T(8,128)}, f32[36,4,48,128]{3,2,1,0:T(8,128)S(1)}, u32[]{:S(2)}) copy-start(f32[36,4,48,128]{3,2,1,0:T(8,128)S(1)} %shard_map.127.grid) | copy-start | bytes 10616836
  138.0 3.4 %copy-start.1 = (f32[256,64,128]{2,1,0:T(8,128)S(1)}, f32[256,64,128]{2,1,0:T(8,128)}, u32[]{:S(2)}) copy-start(f32[256,64,128]{2,1,0:T(8,128)} %projection.3) | copy-start | bytes 25165828
  141.4 2.0 %copy-start.3 = (f32[36,4,48,128]{3,2,1,0:T(8,128)S(1)}, f32[36,4,48,128]{3,2,1,0:T(8,128)}, u32[]{:S(2)}) copy-start(f32[36,4,48,128]{3,2,1,0:T(8,128)} %shard_map.128.grid) | copy-start | bytes 10616836

commit v3 on v2

v3 whole, which is shorter than its diff:
```python
import jax
import jax.numpy as jnp
import ml_dtypes
import numpy as np
from jax import lax
from jax.experimental import pallas as pl
from jax.experimental.pallas import tpu as pltpu
from jax.sharding import PartitionSpec as P

NX, NY, NZ, BOX = 512, 512, 256, 64
GROUP = 32
UNROLL = 4
F32, BF16 = jnp.float32, jnp.bfloat16


def halves(value):
    high = value.astype(BF16)
    return high, (value - high.astype(F32)).astype(BF16)


def lane_sums(value):
    both = jnp.concatenate(halves(value), axis=1)
    return jnp.dot(both, jnp.ones((256, 128), BF16), preferred_element_type=F32)


def window(anchors, slot):
    x_at = anchors[0, slot] - lax.axis_index("pencil") * 32
    z_at = anchors[2, slot] - lax.axis_index("slab") * 32
    y_at = lax.rem(anchors[1, slot] + (NY - 2), NY)
    tile_0 = y_at // 128
    return x_at, z_at + 6, tile_0, lax.rem(tile_0 + 1, 4), lax.rem(y_at, 128)


def window_masks(lane_0):
    row = lax.broadcasted_iota(jnp.int32, (8, 128), 0)
    lane = lax.broadcasted_iota(jnp.int32, (8, 128), 1)
    shifted = lane - row // 4 - lane_0
    return (shifted == 0, shifted == 2), (shifted == -128, shifted == -126)


def scatter_kernel(anchors, count, projection, charges, grid, values):
    step = pl.program_id(0)

    @pl.when(step == 0)
    def _():
        def clear(x, carry):
            grid[x] = jnp.zeros(grid.shape[1:], F32)
            return carry

        lax.fori_loop(0, grid.shape[0], clear, 0)

    slot = step * GROUP + lax.broadcasted_iota(jnp.int32, (GROUP, 128), 0)
    masked = jnp.where(slot < count[0], charges[...], 0.0)
    products = projection[...] * masked[:, None, :]
    values[...] = lane_sums(products.reshape(GROUP * BOX, 128)).reshape(GROUP, BOX, 128)
    top = lax.broadcasted_iota(jnp.int32, (8, 128), 0) < 4

    def place(turn, carry):
        patches = []
        for u in range(UNROLL):
            b = turn * UNROLL + u
            x_at, z_row, tile_0, tile_1, lane_0 = window(anchors, step * GROUP + b)
            for tile, masks in zip((tile_0, tile_1), window_masks(lane_0)):
                for i in range(4):
                    patch = jnp.where(masks[0], values[b, 16 * i : 16 * i + 8], 0.0)
                    patch = jnp.where(masks[1], values[b, 16 * i + 8 : 16 * i + 16], patch)
                    patch = jnp.where(top, patch + pltpu.roll(patch, 4, 0), 0.0)
                    patches.append((x_at + i, tile, pl.ds(z_row, 8), patch))
        for x_at, tile, rows, patch in patches:
            grid[x_at, tile, rows, :] += patch
        return carry

    lax.fori_loop(0, GROUP // UNROLL, place, 0)


def scatter(anchors, count, projection, charges):
    slots = charges.shape[0]
    return pl.pallas_call(
        scatter_kernel,
        grid_spec=pltpu.PrefetchScalarGridSpec(
            num_scalar_prefetch=2,
            grid=(slots // GROUP,),
            in_specs=[
                pl.BlockSpec((GROUP, BOX, 128), lambda i, *_: (i, 0, 0)),
                pl.BlockSpec((GROUP, 128), lambda i, *_: (i, 0)),
            ],
            out_specs=pl.BlockSpec((36, 4, 48, 128), lambda i, *_: (0, 0, 0, 0)),
            scratch_shapes=[pltpu.VMEM((GROUP, BOX, 128), F32)],
        ),
        out_shape=jax.ShapeDtypeStruct((36, 4, 48, 128), F32),
        compiler_params=pltpu.CompilerParams(vmem_limit_bytes=60 << 20),
    )(anchors, count, projection, charges)


def gather_kernel(anchors, count, projection, grid, near, out, picked):
    step = pl.program_id(0)
    top = lax.broadcasted_iota(jnp.int32, (8, 128), 0) < 4

    def pick(turn, carry):
        for u in range(UNROLL):
            b = turn * UNROLL + u
            x_at, z_row, tile_0, tile_1, lane_0 = window(anchors, step * GROUP + b)
            masks_0, masks_1 = window_masks(lane_0)
            for i in range(4):
                both = []
                for tile in (tile_0, tile_1):
                    rows = grid[x_at + i, tile, pl.ds(z_row, 8), :]
                    both.append(jnp.where(top, rows, pltpu.roll(rows, 4, 0)))
                for j in range(2):
                    value = jnp.where(masks_0[j], both[0], jnp.where(masks_1[j], both[1], 0.0))
                    picked[b, 16 * i + 8 * j : 16 * i + 8 * j + 8] = value
        return carry

    lax.fori_loop(0, GROUP // UNROLL, pick, 0)
    box = lane_sums(picked[...].reshape(GROUP * BOX, 128)).reshape(GROUP, BOX, 128)
    far = jnp.sum(projection[...] * box, axis=1)
    slot = step * GROUP + lax.broadcasted_iota(jnp.int32, (GROUP, 128), 0)
    out[...] = jnp.where(slot < count[0], far + near[...], 0.0)


def gather(anchors, count, projection, grid, near):
    slots = projection.shape[0]
    return pl.pallas_call(
        gather_kernel,
        grid_spec=pltpu.PrefetchScalarGridSpec(
            num_scalar_prefetch=2,
            grid=(slots // GROUP,),
            in_specs=[
                pl.BlockSpec((GROUP, BOX, 128), lambda i, *_: (i, 0, 0)),
                pl.BlockSpec((36, 4, 48, 128), lambda i, *_: (0, 0, 0, 0)),
                pl.BlockSpec((GROUP, 128), lambda i, *_: (i, 0)),
            ],
            out_specs=pl.BlockSpec((GROUP, 128), lambda i, *_: (i, 0)),
            scratch_shapes=[pltpu.VMEM((GROUP, BOX, 128), F32)],
        ),
        out_shape=jax.ShapeDtypeStruct((slots, 128), F32),
        compiler_params=pltpu.CompilerParams(vmem_limit_bytes=60 << 20),
    )(anchors, count, projection, grid, near)


CHUNKS = 4
MESH = pl.DeviceIdType.MESH


def phases(product, length):
    angle = 2.0 * np.pi * (product % length) / length
    return np.cos(angle), np.sin(angle)


def split_table(table):
    table = table.astype(np.float32)
    high = table.astype(ml_dtypes.bfloat16)
    return high, (table - high.astype(np.float32)).astype(ml_dtypes.bfloat16)


def y_tables():
    slab, part, pencil = np.meshgrid(np.arange(8), np.arange(2), np.arange(16), indexing="ij")
    device = (slab * 16 + pencil).reshape(-1, 1)
    part = part.reshape(-1, 1)
    even = np.where(device < 64, 4 * device, 4 * device + 2)
    odd = 4 * device + 1
    position = np.arange(256)[None, :]
    result = []
    for freq in (even, odd):
        cos, sin = phases(freq * position, NY)
        table = np.where(part == 0, cos, -sin)
        if freq is even:
            table[(device[:, 0] == 0) & (part[:, 0] == 1)] = 1.0 - 2.0 * (position[0] % 2)
        result.append(table)
    return np.stack(result)


def z_table():
    position = np.arange(NZ)
    cos, sin = phases(position[:, None] * position[None, :], NZ)
    return np.block([[cos, -sin], [sin, cos]])


def x_tables():
    position = np.arange(256)
    result = []
    for parity in range(2):
        cos, sin = phases((2 * position[:, None] + parity) * position[None, :], NX)
        result.append(np.concatenate([cos, sin], axis=1))
        if parity:
            result.append(np.concatenate([cos.T, sin.T], axis=1))
    return np.stack(result)


def dot_3(left, right, dims=((1,), (0,))):
    def one(a, b):
        return lax.dot_general(a, b, (dims, ((), ())), preferred_element_type=F32)

    return one(left[0], right[0]) + (one(left[0], right[1]) + one(left[1], right[0]))


def swap_groups(tiles):
    lane = lax.broadcasted_iota(jnp.int32, tiles[0].shape, 1)
    low, even = lane < 64, lane % 64 < 32
    firsts, lasts = [], []
    for a, b in ((tiles[0], tiles[2]), (tiles[1], tiles[3])):
        firsts.append(jnp.where(low, a, pltpu.roll(b, 64, 1)))
        lasts.append(jnp.where(low, pltpu.roll(a, 64, 1), b))
    result = []
    for a, b in (firsts, lasts):
        result.append(jnp.where(even, a, pltpu.roll(b, 32, 1)))
        result.append(jnp.where(even, pltpu.roll(a, 96, 1), b))
    return result


def field_kernel(
    grid, count, pairs, charges, matrices_at, kernel_at, ty_at, tz_at, tx_at,
    out, near,
    matrices, kernel, ty, tz, tx, sources, terms,
    charge, z_out, z_in, x_in, corner_in, sent_1, got_1, sent_2, got_2, level_out, level_in, spectra, back_2, took_2,
    back_1, took_1, lines, last_z_out, last_z_in, last_x_in, last_corner_in,
    load, level_send, level_recv, rim_send, rim_recv, last_send, last_recv, corner_recv,
    send_1, recv_1, send_2, recv_2, send_3, recv_3, send_4, recv_4,
):
    slab, pencil = lax.axis_index("slab"), lax.axis_index("pencil")
    n_slab, n_pencil = 8, 16

    def at(slab_step, pencil_step):
        return (lax.rem(slab + n_slab + slab_step, n_slab), lax.rem(pencil + n_pencil + pencil_step, n_pencil))

    def on_slab(step):
        return at(step, 0)

    def on_pencil(step):
        return at(0, step)

    def remote(source, target, send_sem, recv_sem, device):
        return pltpu.make_async_remote_copy(
            src_ref=source, dst_ref=target, send_sem=send_sem, recv_sem=recv_sem, device_id=device, device_id_type=MESH
        )

    def wait_recv(ref, sem):
        remote(ref, ref, sem, sem, on_slab(1)).wait_recv()

    def wait_send(ref, sem):
        remote(ref, ref, sem, sem, on_slab(1)).wait_send()

    barrier = pltpu.get_barrier_semaphore()

    def greet(device):
        pl.semaphore_signal(barrier, inc=1, device_id=device, device_id_type=MESH)

    def greet_slab(step, carry):
        greet(on_slab(step))
        return carry

    def greet_pencil(step, carry):
        greet(on_pencil(step))
        return carry

    sides = ((0, -1), (1, 1))
    lax.fori_loop(1, n_slab, greet_slab, 0)
    lax.fori_loop(1, n_pencil, greet_pencil, 0)
    for _, dz in sides:
        for _, dx in sides:
            greet(at(dz, dx))

    loads = [
        pltpu.make_async_copy(source, target, load.at[i])
        for i, (source, target) in enumerate(
            ((ty_at, ty), (tz_at, tz), (kernel_at, kernel), (tx_at, tx), (matrices_at, matrices))
        )
    ]
    for copy in loads:
        copy.start()

    def pack_rims(x, carry):
        for tile in range(4):
            z_out[0, x, 2 * tile : 2 * tile + 2, :] = grid[x, tile, 6:8, :]
            z_out[1, x, 2 * tile : 2 * tile + 2, :] = grid[x, tile, 40:42, :]
        return carry

    lax.fori_loop(0, 36, pack_rims, 0, unroll=4)
    pl.semaphore_wait(barrier, n_slab + n_pencil + 2)
    ends = ((0, 2), (34, 36))
    rims = []
    for a, dz in sides:
        rims.append((z_out.at[a, 2:34], z_in.at[1 - a], on_slab(dz)))
    for b, dx in sides:
        rims.append((grid.at[ends[b][0] : ends[b][1], :, 8:40, :], x_in.at[1 - b], on_pencil(dx)))
    for a, dz in sides:
        for b, dx in sides:
            rims.append((z_out.at[a, ends[b][0] : ends[b][1]], corner_in.at[1 - a, 1 - b], at(dz, dx)))
    for i, (source, target, device) in enumerate(rims):
        remote(source, target, rim_send.at[i], rim_recv.at[i], device).start()

    def bring(x, carry):
        charge[x] = grid[2 + x, :, 8:40, :]
        return carry

    lax.fori_loop(0, 32, bring, 0, unroll=2)
    wait_recv(z_in.at[1], rim_recv.at[0])
    wait_recv(z_in.at[0], rim_recv.at[1])

    def add_rims(x, carry):
        for tile in range(4):
            charge[x, tile, 0:2, :] += z_in[0, x, 2 * tile : 2 * tile + 2, :]
            charge[x, tile, 30:32, :] += z_in[1, x, 2 * tile : 2 * tile + 2, :]
        return carry

    lax.fori_loop(0, 32, add_rims, 0, unroll=4)
    loads[0].wait()

    def forward_y(step, carry):
        chunk = lax.rem(step + 1, CHUNKS)

        @pl.when(step == 2)
        def _():
            for i in range(2, 8):
                wait_recv(rims[i][1], rim_recv.at[i])
            for b, start in ((0, 0), (1, 30)):
                charge[start : start + 2] += x_in[b]
                for a, row in ((0, 0), (1, 30)):
                    for x in range(2):
                        for tile in range(4):
                            charge[start + x, tile, row : row + 2, :] += corner_in[a, b, x, 2 * tile : 2 * tile + 2, :]

        tiles = [charge[pl.ds(8 * chunk, 8), tile].reshape(256, 128) for tile in range(4)]
        for parity in range(2):
            if parity:
                halved = [tiles[0] - tiles[2], tiles[1] - tiles[3]]
            else:
                halved = [tiles[0] + tiles[2], tiles[1] + tiles[3]]
            columns = halves(jnp.concatenate(halved, axis=1))
            freqs = dot_3((ty[0, parity], ty[1, parity]), columns, ((1,), (1,)))
            sent_1[chunk, :, 32 * parity : 32 * parity + 32, :] = freqs.reshape(n_slab, 32, 256)
        got_1[chunk, slab] = sent_1[chunk, slab]

        def send(k, carry):
            device = on_slab(k)
            remote(sent_1.at[chunk, device[0]], got_1.at[chunk, slab], send_1, recv_1.at[chunk], device).start()
            return carry

        return lax.fori_loop(1, n_slab, send, carry)

    lax.fori_loop(0, CHUNKS, forward_y, 0)

    slots, panels = charges.shape
    loads[2].wait()
    first = jnp.logical_and(slab == 0, pencil == 0)
    middle = jnp.logical_and(slab == 4, pencil == 0)

    @pl.when(middle)
    def _():
        for kx in range(2):
            for i in range(2):
                level_out[kx, :, 128 * i : 128 * i + 128] = kernel[pl.ds(8 * kx + 4 * i, 256, stride=16), :]
        remote(level_out, level_in, level_send, level_recv, (0, pencil)).start()

    slot = lax.broadcasted_iota(jnp.int32, (slots, panels), 0)
    coarse = jnp.where(slot < count[...], charges[...], 0.0).astype(BF16)
    slot = lax.broadcasted_iota(jnp.int32, (slots, slots), 0)
    chosen = jnp.where(slot == pairs[1:2, :], 1.0, 0.0)
    sources[...] = jnp.dot(chosen.T.astype(BF16), coarse, preferred_element_type=F32)
    loads[1].wait()
    loads[4].wait()

    def near_group(group, carry):
        rows = pl.ds(pl.multiple_of(8 * group, 8), 8)
        taken = sources[rows, :].astype(BF16)
        row = lax.broadcasted_iota(jnp.int32, (8, panels), 0)
        total = jnp.zeros((8, panels), F32)
        for i in range(8):
            found = lax.dot_general(
                taken, matrices[8 * group + i], (((1,), (1,)), ((), ())), preferred_element_type=F32
            )
            total = jnp.where(row == i, found, total)
        terms[rows, :] = total
        return carry

    near_groups = slots // 8 // (2 * CHUNKS)

    def near_share(turn):
        lax.fori_loop(turn * near_groups, (turn + 1) * near_groups, near_group, 0)

    def forward_z(step, carry):
        chunk = lax.rem(step + 1, CHUNKS)
        near_share(step)
        wait_recv(got_1.at[chunk, 0 : n_slab - 1], recv_1.at[chunk])
        for h in range(2):
            for q in range(2):
                tiles = swap_groups([got_1[chunk, 4 * q + s, :, 128 * h : 128 * h + 128] for s in range(4)])
                for a in range(4):
                    for parity in range(2):
                        for part in range(2):
                            row = 32 * parity + 16 * part
                            lines[2 * part + q, pl.ds(128 * parity + 4 * h + a, 16, stride=8), :] = tiles[a][row : row + 16]
        rows = halves(jnp.concatenate([lines[i] for i in range(4)], axis=1))
        freqs = dot_3(rows, (tz[0], tz[1]))
        for parity in range(2):
            for part in range(2):
                block = freqs[128 * parity : 128 * parity + 128, 256 * part : 256 * part + 256]
                sent_2[chunk, :, parity, part] = block.reshape(n_pencil, 8, 256)
        mine = pl.ds(pl.multiple_of(pencil * 32 + chunk * 8, 8), 8)
        got_2[:, :, mine, :] = sent_2[chunk, pencil]

        def send(k, carry):
            device = on_pencil(k)
            remote(sent_2.at[chunk, device[1]], got_2.at[:, :, mine, :], send_2, recv_2, device).start()
            return carry

        return lax.fori_loop(1, n_pencil, send, carry)

    lax.fori_loop(0, CHUNKS, forward_z, 0)
    wait_recv(got_2.at[:, :, 0 : 32 * (n_pencil - 1), :], recv_2)

    loads[3].wait()
    unit = 1.0 / (NX * NY * NZ)

    def stacked(real, imag):
        real, imag = halves(real), halves(imag)
        return tuple(
            jnp.concatenate([jnp.concatenate([r, i], axis=1), jnp.concatenate([i, -r], axis=1)], axis=0)
            for r, i in zip(real, imag)
        )

    for parity in range(2):
        for kx in range(2):
            parts = []
            for part in range(2):
                low, high = got_2[parity, part, 0:256, :], got_2[parity, part, 256:512, :]
                parts.append(low - high if kx else low + high)
            table = (tx[0, kx], tx[1, kx])
            found = dot_3(table, stacked(*parts))
            if parity:
                green = jnp.concatenate(
                    [kernel[pl.ds(8 * kx + 4 * i + 1, 256, stride=16), :] for i in range(2)], axis=1
                ) * (2.0 * unit)
            else:
                own = jnp.where(slab < 4, 0, 2)
                green = jnp.concatenate(
                    [kernel[pl.ds(own + 8 * kx + 4 * i, 256, stride=16), :] for i in range(2)], axis=1
                ) * jnp.where(first, unit, 2.0 * unit)
            spectra[kx, 0] = found[:, 0:256] * green
            spectra[kx, 1] = found[:, 256:512] * green
            if not parity:

                @pl.when(first)
                def _():
                    if not kx:
                        wait_recv(level_in, level_recv)
                    other = level_in[kx] * unit
                    row = lax.broadcasted_iota(jnp.int32, (256, 256), 0)
                    lane = lax.broadcasted_iota(jnp.int32, (256, 256), 1)
                    mirror = jnp.where((row + lane) % 256 == 0, 1.0, 0.0).astype(BF16)
                    flipped = [
                        sum(jnp.dot(piece, mirror, preferred_element_type=F32) for piece in halves(value)) for value in parts
                    ]
                    twin = dot_3(table, stacked(flipped[0], -flipped[1]))
                    mean, rest = 0.5 * (green + other), 0.5 * (green - other)
                    for part in range(2):
                        lanes = slice(256 * part, 256 * part + 256)
                        spectra[kx, part] = mean * found[:, lanes] + rest * twin[:, lanes]

        ends = []
        for kx in range(2):
            table = (tx[0, 2 * kx], tx[1, 2 * kx])
            real, imag = halves(spectra[kx, 0]), halves(spectra[kx, 1])
            right = tuple(
                jnp.concatenate([jnp.concatenate([r, i], axis=1), jnp.concatenate([-i, r], axis=1)], axis=0)
                for r, i in zip(real, imag)
            )
            ends.append(dot_3(table, right))
        for part in range(2):
            lanes = slice(256 * part, 256 * part + 256)
            back_2[parity, part, 0:256, :] = ends[0][:, lanes] + ends[1][:, lanes]
            back_2[parity, part, 256:512, :] = ends[0][:, lanes] - ends[1][:, lanes]

    def turns(step):
        return jnp.where(step < 2, 3 * step, step - 1)

    def return_x(step, carry):
        chunk = turns(step)
        own = pl.ds(pl.multiple_of(pencil * 32 + chunk * 8, 8), 8)
        took_2[chunk, pencil] = back_2[:, :, own, :]

        def send(k, carry):
            device = on_pencil(k)
            rows = pl.ds(pl.multiple_of(device[1] * 32 + chunk * 8, 8), 8)
            remote(back_2.at[:, :, rows, :], took_2.at[chunk, pencil], send_3, recv_3.at[chunk], device).start()
            return carry

        return lax.fori_loop(1, n_pencil, send, carry)

    lax.fori_loop(0, CHUNKS, return_x, 0)

    def inverse_z(step, carry):
        chunk = turns(step)
        near_share(CHUNKS + step)
        wait_recv(took_2.at[chunk, 0 : n_pencil - 1], recv_3.at[chunk])
        blocks = []
        for parity in range(2):
            blocks.append(jnp.concatenate([took_2[chunk, :, parity, part].reshape(128, 256) for part in range(2)], axis=1))
        rows = halves(jnp.concatenate(blocks, axis=0))
        space = dot_3(rows, (tz[0], tz[1]), ((1,), (1,)))
        for i in range(4):
            lines[i] = space[:, 128 * i : 128 * i + 128]
        for h in range(2):
            for q in range(2):
                tiles = []
                for a in range(4):
                    tiles.append(
                        jnp.concatenate(
                            [
                                lines[2 * part + q, pl.ds(128 * parity + 4 * h + a, 16, stride=8), :]
                                for parity in range(2)
                                for part in range(2)
                            ],
                            axis=0,
                        )
                    )
                for s, tile in enumerate(swap_groups(tiles)):
                    back_1[chunk, 4 * q + s, :, 128 * h : 128 * h + 128] = tile
        took_1[chunk, slab] = back_1[chunk, slab]

        def send(k, carry):
            device = on_slab(k)
            remote(back_1.at[chunk, device[0]], took_1.at[chunk, slab], send_4, recv_4.at[chunk], device).start()
            return carry

        return lax.fori_loop(1, n_slab, send, carry)

    lax.fori_loop(0, CHUNKS, inverse_z, 0)

    slot = lax.broadcasted_iota(jnp.int32, (slots, slots), 0)
    chosen = jnp.where(slot == pairs[0:1, :], 1.0, 0.0).astype(BF16)
    rest = terms[...]
    total = jnp.zeros(near.shape, F32)
    for _ in range(3):
        part = rest.astype(BF16)
        rest = rest - part.astype(F32)
        total = total + jnp.dot(chosen, part, preferred_element_type=F32)
    near[...] = total

    row_ends = ((2, 4), (32, 34))
    last = []
    for b, dx in sides:
        last.append((out.at[row_ends[b][0] : row_ends[b][1], :, 8:40, :], last_x_in.at[1 - b], on_pencil(dx)))
        for a, dz in sides:
            rows = (0, 2) if b == 0 else (6, 8)
            last.append(
                (last_z_out.at[3 * b, a, rows[0] : rows[1]], last_corner_in.at[1 - b, 1 - a], at(dz, dx))
            )

    def planes(chunk, a):
        return (last_z_out.at[chunk, a], last_z_in.at[chunk, 1 - a], last_send.at[6 + a], last_recv.at[chunk, 1 - a])

    def take_planes(step, carry):
        chunk = turns(step)
        for a, row in ((0, 6), (1, 40)):
            wait_recv(last_z_in.at[chunk, a], last_recv.at[chunk, a])
            for x in range(8):
                for tile in range(4):
                    out[2 + 8 * chunk + x, tile, row : row + 2, :] = last_z_in[chunk, a, x, 2 * tile : 2 * tile + 2, :]
        return carry

    def inverse_y(step, carry):
        chunk = turns(step)
        wait_recv(took_1.at[chunk, 0 : n_slab - 1], recv_4.at[chunk])
        ends = []
        for parity in range(2):
            columns = took_1[chunk, :, 32 * parity : 32 * parity + 32, :].reshape(256, 256).T
            ends.append(dot_3(halves(columns), (ty[0, parity], ty[1, parity])))
        space = (ends[0] + ends[1], ends[0] - ends[1])
        for tile in range(4):
            lanes = slice(128 * (tile % 2), 128 * (tile % 2) + 128)
            cells = space[tile // 2][:, lanes].reshape(8, 32, 128)
            out[pl.ds(2 + 8 * chunk, 8), tile, 8:40, :] = cells
            last_z_out[chunk, 0, :, 2 * tile : 2 * tile + 2, :] = cells[:, 0:2, :]
            last_z_out[chunk, 1, :, 2 * tile : 2 * tile + 2, :] = cells[:, 30:32, :]
        for a, dz in sides:
            remote(*planes(chunk, a), on_slab(dz)).start()
        for b in range(2):

            @pl.when(chunk == 3 * b)
            def _():
                for i in range(3 * b, 3 * b + 3):
                    source, target, device = last[i]
                    remote(source, target, last_send.at[i], corner_recv.at[i], device).start()

        return carry

    lax.fori_loop(0, CHUNKS, inverse_y, 0)
    lax.fori_loop(0, CHUNKS - 1, take_planes, 0)
    for i, (source, target, device) in enumerate(last):
        wait_recv(target, corner_recv.at[i])
        wait_send(source, last_send.at[i])
    for b, start in ((0, 0), (1, 34)):
        out[start : start + 2, :, 8:40, :] = last_x_in[b]
        for a, row in ((0, 6), (1, 40)):
            for x in range(2):
                for tile in range(4):
                    out[start + x, tile, row : row + 2, :] = last_corner_in[b, a, x, 2 * tile : 2 * tile + 2, :]
    for i, (source, target, device) in enumerate(rims):
        wait_send(source, rim_send.at[i])
    wait_send(sent_1.at[:, 0 : n_slab - 1], send_1)
    wait_send(got_2.at[:, :, 0 : 32 * (n_pencil - 1), :], send_2)
    wait_send(got_2.at[:, :, 0 : 32 * (n_pencil - 1), :], send_3)
    wait_send(back_1.at[:, 0 : n_slab - 1], send_4)

    @pl.when(middle)
    def _():
        wait_send(level_out, level_send)

    take_planes(CHUNKS - 1, 0)
    for a in range(2):
        wait_send(last_z_out.at[:, a], last_send.at[6 + a])


def field(grid, count, pairs, charges, matrices, kernel):
    tables = [jnp.asarray(np.stack(split_table(table))) for table in (y_tables(), z_table(), x_tables())]
    slots, panels = charges.shape
    dma = pltpu.SemaphoreType.DMA
    vmem = pltpu.VMEM
    return pl.pallas_call(
        field_kernel,
        in_specs=[pl.BlockSpec(memory_space=vmem)] * 4 + [pl.BlockSpec(memory_space=pl.ANY)] * 5,
        out_specs=[pl.BlockSpec(memory_space=vmem)] * 2,
        out_shape=[
            jax.ShapeDtypeStruct((36, 4, 48, 128), F32),
            jax.ShapeDtypeStruct((slots, panels), F32),
        ],
        scratch_shapes=[
            vmem(matrices.shape, BF16),
            vmem(kernel.shape, F32),
            *(vmem(table.shape, BF16) for table in tables),
            vmem((slots, panels), F32),
            vmem((slots, panels), F32),
            vmem((32, 4, 32, 128), F32),
            vmem((2, 36, 8, 128), F32),
            vmem((2, 32, 8, 128), F32),
            vmem((2, 2, 4, 32, 128), F32),
            vmem((2, 2, 2, 8, 128), F32),
            vmem((CHUNKS, 8, 64, 256), F32),
            vmem((CHUNKS, 8, 64, 256), F32),
            vmem((CHUNKS, 16, 2, 2, 8, 256), F32),
            vmem((2, 2, 512, 256), F32),
            vmem((2, 256, 256), F32),
            vmem((2, 256, 256), F32),
            vmem((2, 2, 256, 256), F32),
            vmem((2, 2, 512, 256), F32),
            vmem((CHUNKS, 16, 2, 2, 8, 256), F32),
            vmem((CHUNKS, 8, 64, 256), F32),
            vmem((CHUNKS, 8, 64, 256), F32),
            vmem((4, 256, 128), F32),
            vmem((CHUNKS, 2, 8, 8, 128), F32),
            vmem((CHUNKS, 2, 8, 8, 128), F32),
            vmem((2, 2, 4, 32, 128), F32),
            vmem((2, 2, 2, 8, 128), F32),
            dma((5,)),
            dma,
            dma,
            dma((8,)),
            dma((8,)),
            dma((8,)),
            dma((CHUNKS, 2)),
            dma((6,)),
            dma,
            dma((CHUNKS,)),
            dma,
            dma,
            dma,
            dma((CHUNKS,)),
            dma,
            dma((CHUNKS,)),
        ],
        compiler_params=pltpu.CompilerParams(
            collective_id=0, has_side_effects=True, vmem_limit_bytes=58 << 20
        ),
        cost_estimate=pl.CostEstimate(flops=10**10, bytes_accessed=10**7, transcendentals=0),
    )(grid, count, pairs, charges, matrices, kernel, *tables)


def shards(charges, projection, anchors, block_count, near_pairs, near_matrices, kernel_hat):
    panels = charges.shape[1]
    grid = scatter(anchors.T, block_count, projection, charges)
    levels = jnp.transpose(kernel_hat.reshape(NX, 4, 2, 128), (0, 2, 1, 3)).reshape(NX * 8, 128)
    count = jnp.broadcast_to(block_count[:, None], (1, panels))
    potential, near = field(grid, count, near_pairs.T, charges, near_matrices, levels)
    return gather(anchors.T, block_count, projection, potential, near)


def solution(mesh):
    return jax.shard_map(
        shards,
        mesh=mesh,
        in_specs=(
            P(("slab", "pencil"), None),
            P(("slab", "pencil"), None, None),
            P(("slab", "pencil"), None),
            P(("slab", "pencil")),
            P(("slab", "pencil"), None),
            P(("slab", "pencil"), None, None),
            P(None, ("slab", "pencil"), None),
        ),
        out_specs=P(("slab", "pencil"), None),
        check_vma=False,
    )
```

time: 159 us -> 125 us (0.79)
  local copies, waits for them, and re-layouts: 15.1 us -> 0.51 us
  Pallas kernels: 131 us -> 121 us
  matrix products: 7.78 us -> 0 us
  other arithmetic: 2.64 us -> 0 us
    unnamed x11 -> x0, local copies, waits for them, and re-layouts: 11.4 us -> none
    dot_general x1 -> x0, matrix products: 7.78 us -> none  [shards(): jnp.einsum('ntp,np->nt', near_matrices, sources, preferred_element_type=F32)]
    pallas_call x1, Pallas kernels: 103 us -> 95.5 us  [field(): pl.pallas_call(field_kernel, in_specs=[pl.BlockSpec(memory_space=vmem)] *...]
    pallas_call x1, Pallas kernels: 14.7 us -> 12.6 us  [gather(): pl.pallas_call(gather_kernel, grid_spec=pltpu.PrefetchScalarGridSpec(num_...]
    slice x1 -> x0, local copies, waits for them, and re-layouts: 1.95 us -> none  [shards(): nyquist = lax.ppermute(kernel_hat[:, 0, :], ('slab', 'pencil'), [(64, 0)])]
  transfers between devices with their start and end apart: 1 -> 0, of which waited for: 0 -> 0; matrix products, arithmetic and copies ran while one was open for 7% -> 0% of each run, Pallas kernels for 9% -> 0%
where the time goes in v3:
time: 125 us; the launch traced here: 123 us
  Pallas kernels  121 us (97%)
    pallas_call x1, Pallas kernels, field(): pl.pallas_call(field_kernel, in_specs=[pl.BlockSpec(memory_space=vmem)] *...  95.5 us
    pallas_call x1, Pallas kernels, scatter(): pl.pallas_call(scatter_kernel, grid_spec=pltpu.PrefetchScalarGridSpec(num...  13.4 us
    pallas_call x1, Pallas kernels, gather(): pl.pallas_call(gather_kernel, grid_spec=pltpu.PrefetchScalarGridSpec(num_...  12.6 us

profile of v3, /device:TPU:1, one launch (start us, length us, event | category | flops | bytes accessed | tf_op | source)
XLA Modules:
  0.0 122.6 jit_solution(8301432070196787450)
XLA Ops:
  0.7 0.5 broadcast_in_dim.9.count
  1.2 13.4 %shard_map.100.grid = f32[36,4,48,128]{3,2,1,0:T(8,128)} custom-call(s32[3,256]{1,0:T(4,128)} %bitcast.9, s32[1]{0:T(128)} %copy.12.count, f32[256,64,128]{2,1,0:T(8,128)} %projection.3, f32[256,128]{1,0:T(8,128)} %charges.3), custom_call_target="tpu_custom_call" | custom-call | tf_op jit(solution)/shard_map/pallas_call | solution.py:78
  14.5 95.5 %shard_map.101 = (f32[36,4,48,128]{3,2,1,0:T(8,128)}, f32[256,128]{1,0:T(8,128)}) custom-call(f32[36,4,48,128]{3,2,1,0:T(8,128)} %shard_map.100.grid, s32[1,128]{1,0:T(1,128)} %broadcast_in_dim.9.count, s32[2,256]{1,0:T(2,128)} %bitcast.12, f32[256,128]{1,0:T(8,128)} %charges.3, bf16[256,128,128]{2,1,0:T(8,128)(2,1)} %matrices_at.1, f32[4096,128]{1,0:T(8,128)} %bitcast.11, ...), custom_call_target="tpu_custom_call" | custom-call | flops 10000000000 | bytes 10000000 | tf_op jit(solution)/shard_map/pallas_call | solution.py:620
  110.0 12.6 %shard_map.102 = f32[256,128]{1,0:T(8,128)} custom-call(s32[3,256]{1,0:T(4,128)} %bitcast.10, s32[1]{0:T(128)} %copy.12.count, f32[256,64,128]{2,1,0:T(8,128)} %projection.3, f32[36,4,48,128]{3,2,1,0:T(8,128)} %get-tuple-element.7.grid, f32[256,128]{1,0:T(8,128)} %get-tuple-element.8.near), custom_call_target="tpu_custom_call" | custom-call | tf_op jit(solution)/shard_map/pallas_call | solution.py:123

commit v4 on v3

--- a/solution.py
+++ b/solution.py
@@ -24,8 +24,8 @@
 
 
 def window(anchors, slot):
-    x_at = anchors[0, slot] - lax.axis_index("pencil") * 32
-    z_at = anchors[2, slot] - lax.axis_index("slab") * 32
+    x_at = lax.rem(anchors[0, slot], 32)
+    z_at = lax.rem(anchors[2, slot], 32)
     y_at = lax.rem(anchors[1, slot] + (NY - 2), NY)
     tile_0 = y_at // 128
     return x_at, z_at + 6, tile_0, lax.rem(tile_0 + 1, 4), lax.rem(y_at, 128)
@@ -38,104 +38,72 @@
     return (shifted == 0, shifted == 2), (shifted == -128, shifted == -126)
 
 
-def scatter_kernel(anchors, count, projection, charges, grid, values):
-    step = pl.program_id(0)
-
-    @pl.when(step == 0)
-    def _():
-        def clear(x, carry):
-            grid[x] = jnp.zeros(grid.shape[1:], F32)
+def group_loads(source, target, sems):
+    return [
+        pltpu.make_async_copy(source.at[i * GROUP : (i + 1) * GROUP], target.at[i * GROUP : (i + 1) * GROUP], sems.at[i])
+        for i in range(source.shape[0] // GROUP)
+    ]
+
+
+def group_wait(step, source, target, sems):
+    rows = pl.ds(pl.multiple_of(step * GROUP, GROUP), GROUP)
+    pltpu.make_async_copy(source.at[rows], target.at[rows], sems.at[step]).wait()
+    return rows
+
+
+def scatter_kernel(anchors, count, projection_at, charges, grid, projection, values, load):
+    for copy in group_loads(projection_at, projection, load):
+        copy.start()
+
+    def clear(x, carry):
+        grid[x] = jnp.zeros(grid.shape[1:], F32)
+        return carry
+
+    lax.fori_loop(0, grid.shape[0], clear, 0)
+    top = lax.broadcasted_iota(jnp.int32, (8, 128), 0) < 4
+
+    def group(step, carry):
+        rows = group_wait(step, projection_at, projection, load)
+        slot = step * GROUP + lax.broadcasted_iota(jnp.int32, (GROUP, 128), 0)
+        masked = jnp.where(slot < count[0], charges[rows, :], 0.0)
+        products = projection[rows] * masked[:, None, :]
+        values[...] = lane_sums(products.reshape(GROUP * BOX, 128)).reshape(GROUP, BOX, 128)
+
+        def place(turn, carry):
+            patches = []
+            for u in range(UNROLL):
+                b = turn * UNROLL + u
+                x_at, z_row, tile_0, tile_1, lane_0 = window(anchors, step * GROUP + b)
+                for tile, masks in zip((tile_0, tile_1), window_masks(lane_0)):
+                    for i in range(4):
+                        patch = jnp.where(masks[0], values[b, 16 * i : 16 * i + 8], 0.0)
+                        patch = jnp.where(masks[1], values[b, 16 * i + 8 : 16 * i + 16], patch)
+                        patch = jnp.where(top, patch + pltpu.roll(patch, 4, 0), 0.0)
+                        patches.append((x_at + i, tile, pl.ds(z_row, 8), patch))
+            for x_at, tile, rows, patch in patches:
+                grid[x_at, tile, rows, :] += patch
             return carry
 
-        lax.fori_loop(0, grid.shape[0], clear, 0)
-
-    slot = step * GROUP + lax.broadcasted_iota(jnp.int32, (GROUP, 128), 0)
-    masked = jnp.where(slot < count[0], charges[...], 0.0)
-    products = projection[...] * masked[:, None, :]
-    values[...] = lane_sums(products.reshape(GROUP * BOX, 128)).reshape(GROUP, BOX, 128)
-    top = lax.broadcasted_iota(jnp.int32, (8, 128), 0) < 4
-
-    def place(turn, carry):
-        patches = []
-        for u in range(UNROLL):
-            b = turn * UNROLL + u
-            x_at, z_row, tile_0, tile_1, lane_0 = window(anchors, step * GROUP + b)
-            for tile, masks in zip((tile_0, tile_1), window_masks(lane_0)):
-                for i in range(4):
-                    patch = jnp.where(masks[0], values[b, 16 * i : 16 * i + 8], 0.0)
-                    patch = jnp.where(masks[1], values[b, 16 * i + 8 : 16 * i + 16], patch)
-                    patch = jnp.where(top, patch + pltpu.roll(patch, 4, 0), 0.0)
-                    patches.append((x_at + i, tile, pl.ds(z_row, 8), patch))
-        for x_at, tile, rows, patch in patches:
-            grid[x_at, tile, rows, :] += patch
-        return carry
-
-    lax.fori_loop(0, GROUP // UNROLL, place, 0)
+        return lax.fori_loop(0, GROUP // UNROLL, place, carry)
+
+    lax.fori_loop(0, charges.shape[0] // GROUP, group, 0)
 
 
 def scatter(anchors, count, projection, charges):
     slots = charges.shape[0]
+    smem, vmem = pl.BlockSpec(memory_space=pltpu.SMEM), pl.BlockSpec(memory_space=pltpu.VMEM)
     return pl.pallas_call(
         scatter_kernel,
-        grid_spec=pltpu.PrefetchScalarGridSpec(
-            num_scalar_prefetch=2,
-            grid=(slots // GROUP,),
-            in_specs=[
-                pl.BlockSpec((GROUP, BOX, 128), lambda i, *_: (i, 0, 0)),
-                pl.BlockSpec((GROUP, 128), lambda i, *_: (i, 0)),
-            ],
-            out_specs=pl.BlockSpec((36, 4, 48, 128), lambda i, *_: (0, 0, 0, 0)),
-            scratch_shapes=[pltpu.VMEM((GROUP, BOX, 128), F32)],
-        ),
+        in_specs=[smem, smem, pl.BlockSpec(memory_space=pl.ANY), vmem],
+        out_specs=vmem,
+        scratch_shapes=[
+            pltpu.VMEM(projection.shape, F32),
+            pltpu.VMEM((GROUP, BOX, 128), F32),
+            pltpu.SemaphoreType.DMA((slots // GROUP,)),
+        ],
         out_shape=jax.ShapeDtypeStruct((36, 4, 48, 128), F32),
         compiler_params=pltpu.CompilerParams(vmem_limit_bytes=60 << 20),
     )(anchors, count, projection, charges)
-
-
-def gather_kernel(anchors, count, projection, grid, near, out, picked):
-    step = pl.program_id(0)
-    top = lax.broadcasted_iota(jnp.int32, (8, 128), 0) < 4
-
-    def pick(turn, carry):
-        for u in range(UNROLL):
-            b = turn * UNROLL + u
-            x_at, z_row, tile_0, tile_1, lane_0 = window(anchors, step * GROUP + b)
-            masks_0, masks_1 = window_masks(lane_0)
-            for i in range(4):
-                both = []
-                for tile in (tile_0, tile_1):
-                    rows = grid[x_at + i, tile, pl.ds(z_row, 8), :]
-                    both.append(jnp.where(top, rows, pltpu.roll(rows, 4, 0)))
-                for j in range(2):
-                    value = jnp.where(masks_0[j], both[0], jnp.where(masks_1[j], both[1], 0.0))
-                    picked[b, 16 * i + 8 * j : 16 * i + 8 * j + 8] = value
-        return carry
-
-    lax.fori_loop(0, GROUP // UNROLL, pick, 0)
-    box = lane_sums(picked[...].reshape(GROUP * BOX, 128)).reshape(GROUP, BOX, 128)
-    far = jnp.sum(projection[...] * box, axis=1)
-    slot = step * GROUP + lax.broadcasted_iota(jnp.int32, (GROUP, 128), 0)
-    out[...] = jnp.where(slot < count[0], far + near[...], 0.0)
-
-
-def gather(anchors, count, projection, grid, near):
-    slots = projection.shape[0]
-    return pl.pallas_call(
-        gather_kernel,
-        grid_spec=pltpu.PrefetchScalarGridSpec(
-            num_scalar_prefetch=2,
-            grid=(slots // GROUP,),
-            in_specs=[
-                pl.BlockSpec((GROUP, BOX, 128), lambda i, *_: (i, 0, 0)),
-                pl.BlockSpec((36, 4, 48, 128), lambda i, *_: (0, 0, 0, 0)),
-                pl.BlockSpec((GROUP, 128), lambda i, *_: (i, 0)),
-            ],
-            out_specs=pl.BlockSpec((GROUP, 128), lambda i, *_: (i, 0)),
-            scratch_shapes=[pltpu.VMEM((GROUP, BOX, 128), F32)],
-        ),
-        out_shape=jax.ShapeDtypeStruct((slots, 128), F32),
-        compiler_params=pltpu.CompilerParams(vmem_limit_bytes=60 << 20),
-    )(anchors, count, projection, grid, near)
 
 
 CHUNKS = 4
@@ -209,12 +177,12 @@
 
 
 def field_kernel(
-    grid, count, pairs, charges, matrices_at, kernel_at, ty_at, tz_at, tx_at,
-    out, near,
-    matrices, kernel, ty, tz, tx, sources, terms,
-    charge, z_out, z_in, x_in, corner_in, sent_1, got_1, sent_2, got_2, level_out, level_in, spectra, back_2, took_2,
+    anchors, count, pairs, charges, grid_at, projection_at, matrices_at, kernel_at, ty_at, tz_at, tx_at,
+    result,
+    projection, matrices, kernel, ty, tz, tx, sources, terms, near, values, out,
+    charge, z_rows, z_out, z_in, x_in, corner_in, sent_1, got_1, sent_2, got_2, level_out, level_in, spectra, back_2, took_2,
     back_1, took_1, lines, last_z_out, last_z_in, last_x_in, last_corner_in,
-    load, level_send, level_recv, rim_send, rim_recv, last_send, last_recv, corner_recv,
+    load, group_load, level_send, level_recv, rim_send, rim_recv, last_send, last_recv, corner_recv,
     send_1, recv_1, send_2, recv_2, send_3, recv_3, send_4, recv_4,
 ):
     slab, pencil = lax.axis_index("slab"), lax.axis_index("pencil")
@@ -263,18 +231,29 @@
     loads = [
         pltpu.make_async_copy(source, target, load.at[i])
         for i, (source, target) in enumerate(
-            ((ty_at, ty), (tz_at, tz), (kernel_at, kernel), (tx_at, tx), (matrices_at, matrices))
+            (
+                (grid_at.at[:, :, 0:8, :], z_rows.at[0]),
+                (grid_at.at[:, :, 40:48, :], z_rows.at[1]),
+                (grid_at.at[2:34, :, 8:40, :], charge),
+                (ty_at, ty),
+                (tz_at, tz),
+                (kernel_at, kernel),
+                (tx_at, tx),
+                (matrices_at, matrices),
+            )
         )
     ]
-    for copy in loads:
+    for copy in loads + group_loads(projection_at, projection, group_load):
         copy.start()
 
     def pack_rims(x, carry):
         for tile in range(4):
-            z_out[0, x, 2 * tile : 2 * tile + 2, :] = grid[x, tile, 6:8, :]
-            z_out[1, x, 2 * tile : 2 * tile + 2, :] = grid[x, tile, 40:42, :]
-        return carry
-
+            z_out[0, x, 2 * tile : 2 * tile + 2, :] = z_rows[0, x, tile, 6:8, :]
+            z_out[1, x, 2 * tile : 2 * tile + 2, :] = z_rows[1, x, tile, 0:2, :]
+        return carry
+
+    loads[0].wait()
+    loads[1].wait()
     lax.fori_loop(0, 36, pack_rims, 0, unroll=4)
     pl.semaphore_wait(barrier, n_slab + n_pencil + 2)
     ends = ((0, 2), (34, 36))
@@ -282,18 +261,14 @@
     for a, dz in sides:
         rims.append((z_out.at[a, 2:34], z_in.at[1 - a], on_slab(dz)))
     for b, dx in sides:
-        rims.append((grid.at[ends[b][0] : ends[b][1], :, 8:40, :], x_in.at[1 - b], on_pencil(dx)))
+        rims.append((grid_at.at[ends[b][0] : ends[b][1], :, 8:40, :], x_in.at[1 - b], on_pencil(dx)))
     for a, dz in sides:
         for b, dx in sides:
             rims.append((z_out.at[a, ends[b][0] : ends[b][1]], corner_in.at[1 - a, 1 - b], at(dz, dx)))
     for i, (source, target, device) in enumerate(rims):
         remote(source, target, rim_send.at[i], rim_recv.at[i], device).start()
 
-    def bring(x, carry):
-        charge[x] = grid[2 + x, :, 8:40, :]
-        return carry
-
-    lax.fori_loop(0, 32, bring, 0, unroll=2)
+    loads[2].wait()
     wait_recv(z_in.at[1], rim_recv.at[0])
     wait_recv(z_in.at[0], rim_recv.at[1])
 
@@ -304,7 +279,7 @@
         return carry
 
     lax.fori_loop(0, 32, add_rims, 0, unroll=4)
-    loads[0].wait()
+    loads[3].wait()
 
     def forward_y(step, carry):
         chunk = lax.rem(step + 1, CHUNKS)
@@ -341,7 +316,7 @@
     lax.fori_loop(0, CHUNKS, forward_y, 0)
 
     slots, panels = charges.shape
-    loads[2].wait()
+    loads[5].wait()
     first = jnp.logical_and(slab == 0, pencil == 0)
     middle = jnp.logical_and(slab == 4, pencil == 0)
 
@@ -357,8 +332,8 @@
     slot = lax.broadcasted_iota(jnp.int32, (slots, slots), 0)
     chosen = jnp.where(slot == pairs[1:2, :], 1.0, 0.0)
     sources[...] = jnp.dot(chosen.T.astype(BF16), coarse, preferred_element_type=F32)
-    loads[1].wait()
     loads[4].wait()
+    loads[7].wait()
 
     def near_group(group, carry):
         rows = pl.ds(pl.multiple_of(8 * group, 8), 8)
@@ -409,7 +384,7 @@
     lax.fori_loop(0, CHUNKS, forward_z, 0)
     wait_recv(got_2.at[:, :, 0 : 32 * (n_pencil - 1), :], recv_2)
 
-    loads[3].wait()
+    loads[6].wait()
     unit = 1.0 / (NX * NY * NZ)
 
     def stacked(real, imag):
@@ -611,27 +586,61 @@
     for a in range(2):
         wait_send(last_z_out.at[:, a], last_send.at[6 + a])
 
-
-def field(grid, count, pairs, charges, matrices, kernel):
+    top = lax.broadcasted_iota(jnp.int32, (8, 128), 0) < 4
+
+    def gather_group(step, carry):
+        def pick(turn, carry):
+            for u in range(UNROLL):
+                b = turn * UNROLL + u
+                x_at, z_row, tile_0, tile_1, lane_0 = window(anchors, step * GROUP + b)
+                masks_0, masks_1 = window_masks(lane_0)
+                for i in range(4):
+                    both = []
+                    for tile in (tile_0, tile_1):
+                        rows = out[x_at + i, tile, pl.ds(z_row, 8), :]
+                        both.append(jnp.where(top, rows, pltpu.roll(rows, 4, 0)))
+                    for j in range(2):
+                        value = jnp.where(masks_0[j], both[0], jnp.where(masks_1[j], both[1], 0.0))
+                        values[b, 16 * i + 8 * j : 16 * i + 8 * j + 8] = value
+            return carry
+
+        lax.fori_loop(0, GROUP // UNROLL, pick, 0)
+        rows = group_wait(step, projection_at, projection, group_load)
+        box = lane_sums(values[...].reshape(GROUP * BOX, 128)).reshape(GROUP, BOX, 128)
+        far = jnp.sum(projection[rows] * box, axis=1)
+        slot = step * GROUP + lax.broadcasted_iota(jnp.int32, (GROUP, 128), 0)
+        result[rows, :] = jnp.where(slot < count[...], far + near[rows, :], 0.0)
+        return carry
+
+    lax.fori_loop(0, slots // GROUP, gather_group, 0)
+
+
+def field(anchors, count, pairs, charges, grid, projection, matrices, kernel):
     tables = [jnp.asarray(np.stack(split_table(table))) for table in (y_tables(), z_table(), x_tables())]
     slots, panels = charges.shape
     dma = pltpu.SemaphoreType.DMA
     vmem = pltpu.VMEM
     return pl.pallas_call(
         field_kernel,
-        in_specs=[pl.BlockSpec(memory_space=vmem)] * 4 + [pl.BlockSpec(memory_space=pl.ANY)] * 5,
-        out_specs=[pl.BlockSpec(memory_space=vmem)] * 2,
-        out_shape=[
-            jax.ShapeDtypeStruct((36, 4, 48, 128), F32),
-            jax.ShapeDtypeStruct((slots, panels), F32),
+        in_specs=[
+            pl.BlockSpec(memory_space=pltpu.SMEM),
+            *[pl.BlockSpec(memory_space=vmem)] * 3,
+            *[pl.BlockSpec(memory_space=pl.ANY)] * 7,
         ],
+        out_specs=pl.BlockSpec(memory_space=vmem),
+        out_shape=jax.ShapeDtypeStruct((slots, panels), F32),
         scratch_shapes=[
+            vmem(projection.shape, F32),
             vmem(matrices.shape, BF16),
             vmem(kernel.shape, F32),
             *(vmem(table.shape, BF16) for table in tables),
             vmem((slots, panels), F32),
             vmem((slots, panels), F32),
+            vmem((slots, panels), F32),
+            vmem((GROUP, BOX, panels), F32),
+            vmem((36, 4, 48, 128), F32),
             vmem((32, 4, 32, 128), F32),
+            vmem((2, 36, 4, 8, 128), F32),
             vmem((2, 36, 8, 128), F32),
             vmem((2, 32, 8, 128), F32),
             vmem((2, 2, 4, 32, 128), F32),
@@ -652,7 +661,8 @@
             vmem((CHUNKS, 2, 8, 8, 128), F32),
             vmem((2, 2, 4, 32, 128), F32),
             vmem((2, 2, 2, 8, 128), F32),
-            dma((5,)),
+            dma((8,)),
+            dma((slots // GROUP,)),
             dma,
             dma,
             dma((8,)),
@@ -670,10 +680,10 @@
             dma((CHUNKS,)),
         ],
         compiler_params=pltpu.CompilerParams(
-            collective_id=0, has_side_effects=True, vmem_limit_bytes=58 << 20
+            collective_id=0, has_side_effects=True, vmem_limit_bytes=62 << 20
         ),
         cost_estimate=pl.CostEstimate(flops=10**10, bytes_accessed=10**7, transcendentals=0),
-    )(grid, count, pairs, charges, matrices, kernel, *tables)
+    )(anchors, count, pairs, charges, grid, projection, matrices, kernel, *tables)
 
 
 def shards(charges, projection, anchors, block_count, near_pairs, near_matrices, kernel_hat):
@@ -681,8 +691,7 @@
     grid = scatter(anchors.T, block_count, projection, charges)
     levels = jnp.transpose(kernel_hat.reshape(NX, 4, 2, 128), (0, 2, 1, 3)).reshape(NX * 8, 128)
     count = jnp.broadcast_to(block_count[:, None], (1, panels))
-    potential, near = field(grid, count, near_pairs.T, charges, near_matrices, levels)
-    return gather(anchors.T, block_count, projection, potential, near)
+    return field(anchors.T, count, near_pairs.T, charges, grid, projection, near_matrices, levels)
 
 
 def solution(mesh):

time: 125 us -> 119 us (0.952); the launches traced: 123 us -> 118 us
  Pallas kernels: 121 us -> 115 us
  local copies, waits for them, and re-layouts: 0.51 us -> 2.08 us
    pallas_call x3 -> x2, Pallas kernels: 121 us -> 115 us  [the longest x1 102 us: field(): pl.pallas_call(field_kernel, in_specs=[pl.BlockSpec(memory_space=pltpu.SM...]
    unnamed x0 -> x1, local copies, waits for them, and re-layouts: none -> 1.57 us
where the time goes in v4:
time: 119 us; the launch traced here: 118 us
  Pallas kernels  115 us (97%)
  local copies, waits for them, and re-layouts  2.08 us (2%)
    pallas_call x1, Pallas kernels, field(): pl.pallas_call(field_kernel, in_specs=[pl.BlockSpec(memory_space=pltpu.SM...  102 us
    pallas_call x1, Pallas kernels, scatter(): pl.pallas_call(scatter_kernel, in_specs=[smem, smem, pl.BlockSpec(memory_...  12.9 us

profile of v4, /device:TPU:1, one launch (start us, length us, event | category | flops | bytes accessed | tf_op | source)
XLA Modules:
  0.0 118.1 jit_solution(15002744387711062344)
XLA Ops:
  0.7 0.5 broadcast_in_dim.9.count
  1.2 12.9 %shard_map.100.grid_at = f32[36,4,48,128]{3,2,1,0:T(8,128)} custom-call(s32[3,256]{1,0:T(4,128)} %bitcast.9, s32[1]{0:T(128)} %copy.13.count, f32[256,64,128]{2,1,0:T(8,128)} %projection_at.3, f32[256,128]{1,0:T(8,128)} %charges.3), custom_call_target="tpu_custom_call" | custom-call | tf_op jit(solution)/shard_map/pallas_call | solution.py:95
  14.1 102.4 %shard_map.101 = f32[256,128]{1,0:T(8,128)} custom-call(s32[3,256]{1,0:T(4,128)} %bitcast.10, s32[1,128]{1,0:T(1,128)} %broadcast_in_dim.9.count, s32[2,256]{1,0:T(2,128)} %bitcast.12, f32[256,128]{1,0:T(8,128)} %charges.3, f32[36,4,48,128]{3,2,1,0:T(8,128)} %shard_map.100.grid_at, f32[256,64,128]{2,1,0:T(8,128)} %projection_at.3, ...), custom_call_target="tpu_custom_call" | custom-call | flops 10000000000 | bytes 10000000 | tf_op jit(solution)/shard_map/pallas_call | solution.py:623
  116.5 1.6 %copy.14 = f32[256,128]{1,0:T(8,128)} copy(f32[256,128]{1,0:T(8,128)} %shard_map.101) | data formatting | bytes 262144

commit v5 on v4

--- a/solution.py
+++ b/solution.py
@@ -10,6 +10,7 @@
 NX, NY, NZ, BOX = 512, 512, 256, 64
 GROUP = 32
 UNROLL = 4
+AHEAD = 2
 F32, BF16 = jnp.float32, jnp.bfloat16
 
 
@@ -23,65 +24,76 @@
     return jnp.dot(both, jnp.ones((256, 128), BF16), preferred_element_type=F32)
 
 
+def row_of(x, tile, z):
+    return (x * 4 + tile) * 48 + z
+
+
 def window(anchors, slot):
-    x_at = lax.rem(anchors[0, slot], 32)
-    z_at = lax.rem(anchors[2, slot], 32)
-    y_at = lax.rem(anchors[1, slot] + (NY - 2), NY)
-    tile_0 = y_at // 128
-    return x_at, z_at + 6, tile_0, lax.rem(tile_0 + 1, 4), lax.rem(y_at, 128)
+    corner = row_of(anchors[0, slot] & 31, 0, (anchors[2, slot] & 31) + 6)
+    y_at = (anchors[1, slot] + (NY - 2)) & (NY - 1)
+    tile = y_at >> 7
+    return corner + 48 * tile, corner + 48 * ((tile + 1) & 3), y_at & 127
 
 
 def window_masks(lane_0):
     row = lax.broadcasted_iota(jnp.int32, (8, 128), 0)
     lane = lax.broadcasted_iota(jnp.int32, (8, 128), 1)
-    shifted = lane - row // 4 - lane_0
-    return (shifted == 0, shifted == 2), (shifted == -128, shifted == -126)
-
-
-def group_loads(source, target, sems):
-    return [
-        pltpu.make_async_copy(source.at[i * GROUP : (i + 1) * GROUP], target.at[i * GROUP : (i + 1) * GROUP], sems.at[i])
-        for i in range(source.shape[0] // GROUP)
-    ]
-
-
-def group_wait(step, source, target, sems):
-    rows = pl.ds(pl.multiple_of(step * GROUP, GROUP), GROUP)
-    pltpu.make_async_copy(source.at[rows], target.at[rows], sems.at[step]).wait()
-    return rows
+    shifted = (lane - row // 4 - lane_0) & 127
+    return (shifted == 0, shifted == 2), lane >= lane_0, row < 4
+
+
+def group_rows(step):
+    return pl.ds(pl.multiple_of(step * GROUP, GROUP), GROUP)
+
+
+def group_copy(step, source, target, sems):
+    return pltpu.make_async_copy(source.at[group_rows(step)], target.at[group_rows(step)], sems.at[step])
 
 
 def scatter_kernel(anchors, count, projection_at, charges, grid, projection, values, load):
-    for copy in group_loads(projection_at, projection, load):
-        copy.start()
+    for step in range(AHEAD):
+        group_copy(step, projection_at, projection, load).start()
 
     def clear(x, carry):
-        grid[x] = jnp.zeros(grid.shape[1:], F32)
-        return carry
-
-    lax.fori_loop(0, grid.shape[0], clear, 0)
-    top = lax.broadcasted_iota(jnp.int32, (8, 128), 0) < 4
+        grid[pl.ds(pl.multiple_of(x * 192, 8), 192), :] = jnp.zeros((192, 128), F32)
+        return carry
+
+    lax.fori_loop(0, 36, clear, 0)
 
     def group(step, carry):
-        rows = group_wait(step, projection_at, projection, load)
+        @pl.when(step < charges.shape[0] // GROUP - AHEAD)
+        def _():
+            group_copy(step + AHEAD, projection_at, projection, load).start()
+
+        group_copy(step, projection_at, projection, load).wait()
+        rows = group_rows(step)
         slot = step * GROUP + lax.broadcasted_iota(jnp.int32, (GROUP, 128), 0)
         masked = jnp.where(slot < count[0], charges[rows, :], 0.0)
         products = projection[rows] * masked[:, None, :]
         values[...] = lane_sums(products.reshape(GROUP * BOX, 128)).reshape(GROUP, BOX, 128)
 
         def place(turn, carry):
-            patches = []
+            firsts, seconds, furthest = [], [], 0
             for u in range(UNROLL):
                 b = turn * UNROLL + u
-                x_at, z_row, tile_0, tile_1, lane_0 = window(anchors, step * GROUP + b)
-                for tile, masks in zip((tile_0, tile_1), window_masks(lane_0)):
-                    for i in range(4):
-                        patch = jnp.where(masks[0], values[b, 16 * i : 16 * i + 8], 0.0)
-                        patch = jnp.where(masks[1], values[b, 16 * i + 8 : 16 * i + 16], patch)
-                        patch = jnp.where(top, patch + pltpu.roll(patch, 4, 0), 0.0)
-                        patches.append((x_at + i, tile, pl.ds(z_row, 8), patch))
-            for x_at, tile, rows, patch in patches:
-                grid[x_at, tile, rows, :] += patch
+                row_0, row_1, lane_0 = window(anchors, step * GROUP + b)
+                masks, beyond, top = window_masks(lane_0)
+                here, there = beyond & top, top & ~beyond
+                furthest = jnp.maximum(furthest, lane_0)
+                for i in range(4):
+                    patch = jnp.where(masks[0], values[b, 16 * i : 16 * i + 8], 0.0)
+                    patch = jnp.where(masks[1], values[b, 16 * i + 8 : 16 * i + 16], patch)
+                    patch = patch + pltpu.roll(patch, 4, 0)
+                    firsts.append((row_0 + 192 * i, jnp.where(here, patch, 0.0)))
+                    seconds.append((row_1 + 192 * i, there, patch))
+            for row, patch in firsts:
+                grid[pl.ds(row, 8), :] += patch
+
+            @pl.when(furthest > 124)
+            def _():
+                for row, there, patch in seconds:
+                    grid[pl.ds(row, 8), :] += jnp.where(there, patch, 0.0)
+
             return carry
 
         return lax.fori_loop(0, GROUP // UNROLL, place, carry)
@@ -101,7 +113,7 @@
             pltpu.VMEM((GROUP, BOX, 128), F32),
             pltpu.SemaphoreType.DMA((slots // GROUP,)),
         ],
-        out_shape=jax.ShapeDtypeStruct((36, 4, 48, 128), F32),
+        out_shape=jax.ShapeDtypeStruct((36 * 4 * 48, 128), F32),
         compiler_params=pltpu.CompilerParams(vmem_limit_bytes=60 << 20),
     )(anchors, count, projection, charges)
 
@@ -181,7 +193,7 @@
     result,
     projection, matrices, kernel, ty, tz, tx, sources, terms, near, values, out,
     charge, z_rows, z_out, z_in, x_in, corner_in, sent_1, got_1, sent_2, got_2, level_out, level_in, spectra, back_2, took_2,
-    back_1, took_1, lines, last_z_out, last_z_in, last_x_in, last_corner_in,
+    back_1, took_1, lines, last_z_out, last_z_in, last_x_out, last_x_in, last_corner_in,
     load, group_load, level_send, level_recv, rim_send, rim_recv, last_send, last_recv, corner_recv,
     send_1, recv_1, send_2, recv_2, send_3, recv_3, send_4, recv_4,
 ):
@@ -243,8 +255,10 @@
             )
         )
     ]
-    for copy in loads + group_loads(projection_at, projection, group_load):
+    for copy in loads:
         copy.start()
+    for step in range(charges.shape[0] // GROUP):
+        group_copy(step, projection_at, projection, group_load).start()
 
     def pack_rims(x, carry):
         for tile in range(4):
@@ -512,10 +526,10 @@
         total = total + jnp.dot(chosen, part, preferred_element_type=F32)
     near[...] = total
 
-    row_ends = ((2, 4), (32, 34))
+    row_starts = (2, 32)
     last = []
     for b, dx in sides:
-        last.append((out.at[row_ends[b][0] : row_ends[b][1], :, 8:40, :], last_x_in.at[1 - b], on_pencil(dx)))
+        last.append((last_x_out.at[b], last_x_in.at[1 - b], on_pencil(dx)))
         for a, dz in sides:
             rows = (0, 2) if b == 0 else (6, 8)
             last.append(
@@ -531,7 +545,7 @@
             wait_recv(last_z_in.at[chunk, a], last_recv.at[chunk, a])
             for x in range(8):
                 for tile in range(4):
-                    out[2 + 8 * chunk + x, tile, row : row + 2, :] = last_z_in[chunk, a, x, 2 * tile : 2 * tile + 2, :]
+                    out[pl.ds(row_of(2 + 8 * chunk + x, tile, row), 2), :] = last_z_in[chunk, a, x, 2 * tile : 2 * tile + 2, :]
         return carry
 
     def inverse_y(step, carry):
@@ -545,7 +559,8 @@
         for tile in range(4):
             lanes = slice(128 * (tile % 2), 128 * (tile % 2) + 128)
             cells = space[tile // 2][:, lanes].reshape(8, 32, 128)
-            out[pl.ds(2 + 8 * chunk, 8), tile, 8:40, :] = cells
+            for x in range(8):
+                out[pl.ds(pl.multiple_of(row_of(2 + 8 * chunk + x, tile, 8), 8), 32), :] = cells[x]
             last_z_out[chunk, 0, :, 2 * tile : 2 * tile + 2, :] = cells[:, 0:2, :]
             last_z_out[chunk, 1, :, 2 * tile : 2 * tile + 2, :] = cells[:, 30:32, :]
         for a, dz in sides:
@@ -554,6 +569,9 @@
 
             @pl.when(chunk == 3 * b)
             def _():
+                for x in range(2):
+                    for tile in range(4):
+                        last_x_out[b, x, tile] = out[pl.ds(row_of(row_starts[b] + x, tile, 8), 32), :]
                 for i in range(3 * b, 3 * b + 3):
                     source, target, device = last[i]
                     remote(source, target, last_send.at[i], corner_recv.at[i], device).start()
@@ -566,11 +584,11 @@
         wait_recv(target, corner_recv.at[i])
         wait_send(source, last_send.at[i])
     for b, start in ((0, 0), (1, 34)):
-        out[start : start + 2, :, 8:40, :] = last_x_in[b]
-        for a, row in ((0, 6), (1, 40)):
-            for x in range(2):
-                for tile in range(4):
-                    out[start + x, tile, row : row + 2, :] = last_corner_in[b, a, x, 2 * tile : 2 * tile + 2, :]
+        for x in range(2):
+            for tile in range(4):
+                out[pl.ds(row_of(start + x, tile, 8), 32), :] = last_x_in[b, x, tile]
+                for a, row in ((0, 6), (1, 40)):
+                    out[pl.ds(row_of(start + x, tile, row), 2), :] = last_corner_in[b, a, x, 2 * tile : 2 * tile + 2, :]
     for i, (source, target, device) in enumerate(rims):
         wait_send(source, rim_send.at[i])
     wait_send(sent_1.at[:, 0 : n_slab - 1], send_1)
@@ -586,26 +604,22 @@
     for a in range(2):
         wait_send(last_z_out.at[:, a], last_send.at[6 + a])
 
-    top = lax.broadcasted_iota(jnp.int32, (8, 128), 0) < 4
-
     def gather_group(step, carry):
         def pick(turn, carry):
             for u in range(UNROLL):
                 b = turn * UNROLL + u
-                x_at, z_row, tile_0, tile_1, lane_0 = window(anchors, step * GROUP + b)
-                masks_0, masks_1 = window_masks(lane_0)
+                row_0, row_1, lane_0 = window(anchors, step * GROUP + b)
+                masks, beyond, top = window_masks(lane_0)
                 for i in range(4):
-                    both = []
-                    for tile in (tile_0, tile_1):
-                        rows = out[x_at + i, tile, pl.ds(z_row, 8), :]
-                        both.append(jnp.where(top, rows, pltpu.roll(rows, 4, 0)))
+                    cells = jnp.where(beyond, out[pl.ds(row_0 + 192 * i, 8), :], out[pl.ds(row_1 + 192 * i, 8), :])
+                    cells = jnp.where(top, cells, pltpu.roll(cells, 4, 0))
                     for j in range(2):
-                        value = jnp.where(masks_0[j], both[0], jnp.where(masks_1[j], both[1], 0.0))
-                        values[b, 16 * i + 8 * j : 16 * i + 8 * j + 8] = value
+                        values[b, 16 * i + 8 * j : 16 * i + 8 * j + 8] = jnp.where(masks[j], cells, 0.0)
             return carry
 
         lax.fori_loop(0, GROUP // UNROLL, pick, 0)
-        rows = group_wait(step, projection_at, projection, group_load)
+        group_copy(step, projection_at, projection, group_load).wait()
+        rows = group_rows(step)
         box = lane_sums(values[...].reshape(GROUP * BOX, 128)).reshape(GROUP, BOX, 128)
         far = jnp.sum(projection[rows] * box, axis=1)
         slot = step * GROUP + lax.broadcasted_iota(jnp.int32, (GROUP, 128), 0)
@@ -638,7 +652,7 @@
             vmem((slots, panels), F32),
             vmem((slots, panels), F32),
             vmem((GROUP, BOX, panels), F32),
-            vmem((36, 4, 48, 128), F32),
+            vmem((36 * 4 * 48, 128), F32),
             vmem((32, 4, 32, 128), F32),
             vmem((2, 36, 4, 8, 128), F32),
             vmem((2, 36, 8, 128), F32),
@@ -659,6 +673,7 @@
             vmem((4, 256, 128), F32),
             vmem((CHUNKS, 2, 8, 8, 128), F32),
             vmem((CHUNKS, 2, 8, 8, 128), F32),
+            vmem((2, 2, 4, 32, 128), F32),
             vmem((2, 2, 4, 32, 128), F32),
             vmem((2, 2, 2, 8, 128), F32),
             dma((8,)),
@@ -688,7 +703,7 @@
 
 def shards(charges, projection, anchors, block_count, near_pairs, near_matrices, kernel_hat):
     panels = charges.shape[1]
-    grid = scatter(anchors.T, block_count, projection, charges)
+    grid = scatter(anchors.T, block_count, projection, charges).reshape(36, 4, 48, 128)
     levels = jnp.transpose(kernel_hat.reshape(NX, 4, 2, 128), (0, 2, 1, 3)).reshape(NX * 8, 128)
     count = jnp.broadcast_to(block_count[:, None], (1, panels))
     return field(anchors.T, count, near_pairs.T, charges, grid, projection, near_matrices, levels)

time: 119 us -> 114 us (0.958)
  Pallas kernels: 115 us -> 110 us
    pallas_call x1, Pallas kernels: 102 us -> 99.7 us  [field(): pl.pallas_call(field_kernel, in_specs=[pl.BlockSpec(memory_space=pltpu.SM...]
    pallas_call x1, Pallas kernels: 12.9 us -> 10.7 us  [scatter(): pl.pallas_call(scatter_kernel, in_specs=[smem, smem, pl.BlockSpec(memory_...]
where the time goes in v5:
time: 114 us; the launch traced here: 113 us
  Pallas kernels  110 us (96%)
  local copies, waits for them, and re-layouts  2.08 us (2%)
    pallas_call x1, Pallas kernels, field(): pl.pallas_call(field_kernel, in_specs=[pl.BlockSpec(memory_space=pltpu.SM...  99.7 us
    pallas_call x1, Pallas kernels, scatter(): pl.pallas_call(scatter_kernel, in_specs=[smem, smem, pl.BlockSpec(memory_...  10.7 us

profile of v5, /device:TPU:1, one launch (start us, length us, event | category | flops | bytes accessed | tf_op | source)
XLA Modules:
  0.0 113.1 jit_solution(10074422289652552653)
XLA Ops:
  0.7 0.5 broadcast_in_dim.9.count
  1.2 10.7 %shard_map.100 = f32[6912,128]{1,0:T(8,128)} custom-call(s32[3,256]{1,0:T(4,128)} %bitcast.11, s32[1]{0:T(128)} %copy.13.count, f32[256,64,128]{2,1,0:T(8,128)} %projection_at.3, f32[256,128]{1,0:T(8,128)} %charges.3), custom_call_target="tpu_custom_call" | custom-call | tf_op jit(solution)/shard_map/pallas_call | solution.py:107
  11.9 99.7 %shard_map.101 = f32[256,128]{1,0:T(8,128)} custom-call(s32[3,256]{1,0:T(4,128)} %bitcast.12, s32[1,128]{1,0:T(1,128)} %broadcast_in_dim.9.count, s32[2,256]{1,0:T(2,128)} %bitcast.14, f32[256,128]{1,0:T(8,128)} %charges.3, f32[36,4,48,128]{3,2,1,0:T(8,128)} %bitcast.10, f32[256,64,128]{2,1,0:T(8,128)} %projection_at.3, bf16[256,128,128]{2,1,0:T(8,128)(2,1)} %matrices_at.1, ...), custom_call_target="tpu_custom_call" | custom-call | flops 10000000000 | bytes 10000000 | tf_op jit(solution)/shard_map/pallas_call | solution.py:637
  111.5 1.6 %copy.14 = f32[256,128]{1,0:T(8,128)} copy(f32[256,128]{1,0:T(8,128)} %shard_map.101) | data formatting | bytes 262144

commit v6 on v5

--- a/solution.py
+++ b/solution.py
@@ -317,17 +317,23 @@
                 halved = [tiles[0] + tiles[2], tiles[1] + tiles[3]]
             columns = halves(jnp.concatenate(halved, axis=1))
             freqs = dot_3((ty[0, parity], ty[1, parity]), columns, ((1,), (1,)))
-            sent_1[chunk, :, 32 * parity : 32 * parity + 32, :] = freqs.reshape(n_slab, 32, 256)
-        got_1[chunk, slab] = sent_1[chunk, slab]
+            sent_1[parity, chunk] = freqs.reshape(n_slab, 32, 256)
+        return to_slabs(0, chunk)
+
+    def to_slabs(parity, chunk):
+        got_1[parity, chunk, slab] = sent_1[parity, chunk, slab]
 
         def send(k, carry):
             device = on_slab(k)
-            remote(sent_1.at[chunk, device[0]], got_1.at[chunk, slab], send_1, recv_1.at[chunk], device).start()
+            remote(
+                sent_1.at[parity, chunk, device[0]], got_1.at[parity, chunk, slab], send_1, recv_1.at[parity, chunk], device
+            ).start()
             return carry
 
-        return lax.fori_loop(1, n_slab, send, carry)
+        return lax.fori_loop(1, n_slab, send, 0)
 
     lax.fori_loop(0, CHUNKS, forward_y, 0)
+    lax.fori_loop(0, CHUNKS, lambda step, carry: to_slabs(1, lax.rem(step + 1, CHUNKS)), 0)
 
     slots, panels = charges.shape
     loads[5].wait()
@@ -362,41 +368,38 @@
         terms[rows, :] = total
         return carry
 
-    near_groups = slots // 8 // (2 * CHUNKS)
+    near_groups = slots // 8 // (4 * CHUNKS)
 
     def near_share(turn):
         lax.fori_loop(turn * near_groups, (turn + 1) * near_groups, near_group, 0)
 
-    def forward_z(step, carry):
-        chunk = lax.rem(step + 1, CHUNKS)
-        near_share(step)
-        wait_recv(got_1.at[chunk, 0 : n_slab - 1], recv_1.at[chunk])
+    def forward_z(turn, carry):
+        parity, chunk = turn // CHUNKS, lax.rem(turn + 1, CHUNKS)
+        near_share(turn)
+        wait_recv(got_1.at[parity, chunk, 0 : n_slab - 1], recv_1.at[parity, chunk])
         for h in range(2):
             for q in range(2):
-                tiles = swap_groups([got_1[chunk, 4 * q + s, :, 128 * h : 128 * h + 128] for s in range(4)])
+                tiles = swap_groups([got_1[parity, chunk, 4 * q + s, :, 128 * h : 128 * h + 128] for s in range(4)])
                 for a in range(4):
-                    for parity in range(2):
-                        for part in range(2):
-                            row = 32 * parity + 16 * part
-                            lines[2 * part + q, pl.ds(128 * parity + 4 * h + a, 16, stride=8), :] = tiles[a][row : row + 16]
+                    for part in range(2):
+                        lines[2 * part + q, pl.ds(4 * h + a, 16, stride=8), :] = tiles[a][16 * part : 16 * part + 16]
         rows = halves(jnp.concatenate([lines[i] for i in range(4)], axis=1))
         freqs = dot_3(rows, (tz[0], tz[1]))
-        for parity in range(2):
-            for part in range(2):
-                block = freqs[128 * parity : 128 * parity + 128, 256 * part : 256 * part + 256]
-                sent_2[chunk, :, parity, part] = block.reshape(n_pencil, 8, 256)
+        for part in range(2):
+            sent_2[parity, chunk, :, part] = freqs[:, 256 * part : 256 * part + 256].reshape(n_pencil, 8, 256)
         mine = pl.ds(pl.multiple_of(pencil * 32 + chunk * 8, 8), 8)
-        got_2[:, :, mine, :] = sent_2[chunk, pencil]
+        got_2[parity, :, mine, :] = sent_2[parity, chunk, pencil]
 
         def send(k, carry):
             device = on_pencil(k)
-            remote(sent_2.at[chunk, device[1]], got_2.at[:, :, mine, :], send_2, recv_2, device).start()
+            remote(
+                sent_2.at[parity, chunk, device[1]], got_2.at[parity, :, mine, :], send_2, recv_2.at[parity], device
+            ).start()
             return carry
 
         return lax.fori_loop(1, n_pencil, send, carry)
 
-    lax.fori_loop(0, CHUNKS, forward_z, 0)
-    wait_recv(got_2.at[:, :, 0 : 32 * (n_pencil - 1), :], recv_2)
+    lax.fori_loop(0, 2 * CHUNKS - 2, forward_z, 0)
 
     loads[6].wait()
     unit = 1.0 / (NX * NY * NZ)
@@ -408,7 +411,8 @@
             for r, i in zip(real, imag)
         )
 
-    for parity in range(2):
+    def along_x(parity):
+        wait_recv(got_2.at[parity, :, 0 : 32 * (n_pencil - 1), :], recv_2.at[parity])
         for kx in range(2):
             parts = []
             for part in range(2):
@@ -463,58 +467,55 @@
     def turns(step):
         return jnp.where(step < 2, 3 * step, step - 1)
 
-    def return_x(step, carry):
-        chunk = turns(step)
+    def return_x(turn, carry):
+        parity, chunk = turn // CHUNKS, turns(lax.rem(turn, CHUNKS))
         own = pl.ds(pl.multiple_of(pencil * 32 + chunk * 8, 8), 8)
-        took_2[chunk, pencil] = back_2[:, :, own, :]
+        took_2[parity, chunk, pencil] = back_2[parity, :, own, :]
 
         def send(k, carry):
             device = on_pencil(k)
             rows = pl.ds(pl.multiple_of(device[1] * 32 + chunk * 8, 8), 8)
-            remote(back_2.at[:, :, rows, :], took_2.at[chunk, pencil], send_3, recv_3.at[chunk], device).start()
+            remote(
+                back_2.at[parity, :, rows, :], took_2.at[parity, chunk, pencil], send_3, recv_3.at[parity, chunk], device
+            ).start()
             return carry
 
         return lax.fori_loop(1, n_pencil, send, carry)
 
-    lax.fori_loop(0, CHUNKS, return_x, 0)
-
-    def inverse_z(step, carry):
-        chunk = turns(step)
-        near_share(CHUNKS + step)
-        wait_recv(took_2.at[chunk, 0 : n_pencil - 1], recv_3.at[chunk])
-        blocks = []
-        for parity in range(2):
-            blocks.append(jnp.concatenate([took_2[chunk, :, parity, part].reshape(128, 256) for part in range(2)], axis=1))
-        rows = halves(jnp.concatenate(blocks, axis=0))
-        space = dot_3(rows, (tz[0], tz[1]), ((1,), (1,)))
+    def inverse_z(turn, carry):
+        parity, chunk = turn // CHUNKS, turns(lax.rem(turn, CHUNKS))
+        near_share(2 * CHUNKS + turn)
+        wait_recv(took_2.at[parity, chunk, 0 : n_pencil - 1], recv_3.at[parity, chunk])
+        rows = jnp.concatenate([took_2[parity, chunk, :, part].reshape(128, 256) for part in range(2)], axis=1)
+        space = dot_3(halves(rows), (tz[0], tz[1]), ((1,), (1,)))
         for i in range(4):
             lines[i] = space[:, 128 * i : 128 * i + 128]
         for h in range(2):
             for q in range(2):
                 tiles = []
                 for a in range(4):
-                    tiles.append(
-                        jnp.concatenate(
-                            [
-                                lines[2 * part + q, pl.ds(128 * parity + 4 * h + a, 16, stride=8), :]
-                                for parity in range(2)
-                                for part in range(2)
-                            ],
-                            axis=0,
-                        )
-                    )
+                    pieces = [lines[2 * part + q, pl.ds(4 * h + a, 16, stride=8), :] for part in range(2)]
+                    tiles.append(jnp.concatenate(pieces, axis=0))
                 for s, tile in enumerate(swap_groups(tiles)):
-                    back_1[chunk, 4 * q + s, :, 128 * h : 128 * h + 128] = tile
-        took_1[chunk, slab] = back_1[chunk, slab]
+                    back_1[parity, chunk, 4 * q + s, :, 128 * h : 128 * h + 128] = tile
+        took_1[parity, chunk, slab] = back_1[parity, chunk, slab]
 
         def send(k, carry):
             device = on_slab(k)
-            remote(back_1.at[chunk, device[0]], took_1.at[chunk, slab], send_4, recv_4.at[chunk], device).start()
+            remote(
+                back_1.at[parity, chunk, device[0]], took_1.at[parity, chunk, slab], send_4, recv_4.at[parity, chunk], device
+            ).start()
             return carry
 
         return lax.fori_loop(1, n_slab, send, carry)
 
-    lax.fori_loop(0, CHUNKS, inverse_z, 0)
+    along_x(0)
+    lax.fori_loop(0, 2, return_x, 0)
+    lax.fori_loop(2, 4, lambda turn, carry: return_x(turn, forward_z(turn + 4, carry)), 0)
+    lax.fori_loop(0, 2, inverse_z, 0)
+    along_x(1)
+    lax.fori_loop(4, 8, return_x, 0)
+    lax.fori_loop(2, 8, inverse_z, 0)
 
     slot = lax.broadcasted_iota(jnp.int32, (slots, slots), 0)
     chosen = jnp.where(slot == pairs[0:1, :], 1.0, 0.0).astype(BF16)
@@ -550,10 +551,10 @@
 
     def inverse_y(step, carry):
         chunk = turns(step)
-        wait_recv(took_1.at[chunk, 0 : n_slab - 1], recv_4.at[chunk])
         ends = []
         for parity in range(2):
-            columns = took_1[chunk, :, 32 * parity : 32 * parity + 32, :].reshape(256, 256).T
+            wait_recv(took_1.at[parity, chunk, 0 : n_slab - 1], recv_4.at[parity, chunk])
+            columns = took_1[parity, chunk].reshape(256, 256).T
             ends.append(dot_3(halves(columns), (ty[0, parity], ty[1, parity])))
         space = (ends[0] + ends[1], ends[0] - ends[1])
         for tile in range(4):
@@ -591,10 +592,10 @@
                     out[pl.ds(row_of(start + x, tile, row), 2), :] = last_corner_in[b, a, x, 2 * tile : 2 * tile + 2, :]
     for i, (source, target, device) in enumerate(rims):
         wait_send(source, rim_send.at[i])
-    wait_send(sent_1.at[:, 0 : n_slab - 1], send_1)
+    wait_send(sent_1.at[:, :, 0 : n_slab - 1], send_1)
     wait_send(got_2.at[:, :, 0 : 32 * (n_pencil - 1), :], send_2)
     wait_send(got_2.at[:, :, 0 : 32 * (n_pencil - 1), :], send_3)
-    wait_send(back_1.at[:, 0 : n_slab - 1], send_4)
+    wait_send(back_1.at[:, :, 0 : n_slab - 1], send_4)
 
     @pl.when(middle)
     def _():
@@ -659,18 +660,18 @@
             vmem((2, 32, 8, 128), F32),
             vmem((2, 2, 4, 32, 128), F32),
             vmem((2, 2, 2, 8, 128), F32),
-            vmem((CHUNKS, 8, 64, 256), F32),
-            vmem((CHUNKS, 8, 64, 256), F32),
-            vmem((CHUNKS, 16, 2, 2, 8, 256), F32),
+            vmem((2, CHUNKS, 8, 32, 256), F32),
+            vmem((2, CHUNKS, 8, 32, 256), F32),
+            vmem((2, CHUNKS, 16, 2, 8, 256), F32),
             vmem((2, 2, 512, 256), F32),
             vmem((2, 256, 256), F32),
             vmem((2, 256, 256), F32),
             vmem((2, 2, 256, 256), F32),
             vmem((2, 2, 512, 256), F32),
-            vmem((CHUNKS, 16, 2, 2, 8, 256), F32),
-            vmem((CHUNKS, 8, 64, 256), F32),
-            vmem((CHUNKS, 8, 64, 256), F32),
-            vmem((4, 256, 128), F32),
+            vmem((2, CHUNKS, 16, 2, 8, 256), F32),
+            vmem((2, CHUNKS, 8, 32, 256), F32),
+            vmem((2, CHUNKS, 8, 32, 256), F32),
+            vmem((4, 128, 128), F32),
             vmem((CHUNKS, 2, 8, 8, 128), F32),
             vmem((CHUNKS, 2, 8, 8, 128), F32),
             vmem((2, 2, 4, 32, 128), F32),
@@ -686,13 +687,13 @@
             dma((CHUNKS, 2)),
             dma((6,)),
             dma,
-            dma((CHUNKS,)),
+            dma((2, CHUNKS)),
             dma,
+            dma((2,)),
             dma,
+            dma((2, CHUNKS)),
             dma,
-            dma((CHUNKS,)),
-            dma,
-            dma((CHUNKS,)),
+            dma((2, CHUNKS)),
         ],
         compiler_params=pltpu.CompilerParams(
             collective_id=0, has_side_effects=True, vmem_limit_bytes=62 << 20

time: 114 us -> 105 us (0.921)
  Pallas kernels: 110 us -> 101 us
    pallas_call x1, Pallas kernels: 99.7 us -> 90 us  [field(): pl.pallas_call(field_kernel, in_specs=[pl.BlockSpec(memory_space=pltpu.SM...]
where the time goes in v6:
time: 105 us; the launch traced here: 104 us
  Pallas kernels  101 us (96%)
  local copies, waits for them, and re-layouts  2.08 us (2%)
    pallas_call x1, Pallas kernels, field(): pl.pallas_call(field_kernel, in_specs=[pl.BlockSpec(memory_space=pltpu.SM...  90 us
    pallas_call x1, Pallas kernels, scatter(): pl.pallas_call(scatter_kernel, in_specs=[smem, smem, pl.BlockSpec(memory_...  10.8 us

profile of v6, /device:TPU:1, one launch (start us, length us, event | category | flops | bytes accessed | tf_op | source)
XLA Modules:
  0.0 103.6 jit_solution(12090107701399878672)
XLA Ops:
  0.7 0.5 broadcast_in_dim.9.count
  1.2 10.8 %shard_map.100 = f32[6912,128]{1,0:T(8,128)} custom-call(s32[3,256]{1,0:T(4,128)} %bitcast.11, s32[1]{0:T(128)} %copy.13.count, f32[256,64,128]{2,1,0:T(8,128)} %projection_at.3, f32[256,128]{1,0:T(8,128)} %charges.3), custom_call_target="tpu_custom_call" | custom-call | tf_op jit(solution)/shard_map/pallas_call | solution.py:107
  12.0 90.0 %shard_map.101 = f32[256,128]{1,0:T(8,128)} custom-call(s32[3,256]{1,0:T(4,128)} %bitcast.12, s32[1,128]{1,0:T(1,128)} %broadcast_in_dim.9.count, s32[2,256]{1,0:T(2,128)} %bitcast.14, f32[256,128]{1,0:T(8,128)} %charges.3, f32[36,4,48,128]{3,2,1,0:T(8,128)} %bitcast.10, f32[256,64,128]{2,1,0:T(8,128)} %projection_at.3, bf16[256,128,128]{2,1,0:T(8,128)(2,1)} %matrices_at.1, ...), custom_call_target="tpu_custom_call" | custom-call | flops 10000000000 | bytes 10000000 | tf_op jit(solution)/shard_map/pallas_call | solution.py:638
  102.0 1.6 %copy.14 = f32[256,128]{1,0:T(8,128)} copy(f32[256,128]{1,0:T(8,128)} %shard_map.101) | data formatting | bytes 262144

commit v7 on v6

--- a/solution.py
+++ b/solution.py
@@ -8,7 +8,7 @@
 from jax.sharding import PartitionSpec as P
 
 NX, NY, NZ, BOX = 512, 512, 256, 64
-GROUP = 32
+GROUP = 64
 UNROLL = 4
 AHEAD = 2
 F32, BF16 = jnp.float32, jnp.bfloat16
@@ -20,8 +20,9 @@
 
 
 def lane_sums(value):
-    both = jnp.concatenate(halves(value), axis=1)
-    return jnp.dot(both, jnp.ones((256, 128), BF16), preferred_element_type=F32)
+    ones = jnp.ones((128, 128), BF16)
+    high, low = halves(value)
+    return jnp.dot(high, ones, preferred_element_type=F32) + jnp.dot(low, ones, preferred_element_type=F32)
 
 
 def row_of(x, tile, z):
@@ -50,7 +51,8 @@
     return pltpu.make_async_copy(source.at[group_rows(step)], target.at[group_rows(step)], sems.at[step])
 
 
-def scatter_kernel(anchors, count, projection_at, charges, grid, projection, values, load):
+def scatter_kernel(anchors, count, projection_at, charges, cells, projection, values, load):
+    grid = cells.reshape(36 * 4 * 48, 128)
     for step in range(AHEAD):
         group_copy(step, projection_at, projection, load).start()
 
@@ -107,14 +109,14 @@
     return pl.pallas_call(
         scatter_kernel,
         in_specs=[smem, smem, pl.BlockSpec(memory_space=pl.ANY), vmem],
-        out_specs=vmem,
+        out_specs=pl.BlockSpec(memory_space=pltpu.VMEM),
         scratch_shapes=[
             pltpu.VMEM(projection.shape, F32),
             pltpu.VMEM((GROUP, BOX, 128), F32),
             pltpu.SemaphoreType.DMA((slots // GROUP,)),
         ],
-        out_shape=jax.ShapeDtypeStruct((36 * 4 * 48, 128), F32),
-        compiler_params=pltpu.CompilerParams(vmem_limit_bytes=60 << 20),
+        out_shape=pltpu.VMEM((36, 4, 48, 128), F32),
+        compiler_params=pltpu.CompilerParams(vmem_limit_bytes=57 << 20),
     )(anchors, count, projection, charges)
 
 
@@ -189,10 +191,10 @@
 
 
 def field_kernel(
-    anchors, count, pairs, charges, grid_at, projection_at, matrices_at, kernel_at, ty_at, tz_at, tx_at,
+    anchors, count, pairs, charges, grid, projection_at, matrices_at, kernel_at, ty_at, tz_at, tx_at,
     result,
     projection, matrices, kernel, ty, tz, tx, sources, terms, near, values, out,
-    charge, z_rows, z_out, z_in, x_in, corner_in, sent_1, got_1, sent_2, got_2, level_out, level_in, spectra, back_2, took_2,
+    charge, z_out, z_in, x_in, corner_in, sent_1, got_1, sent_2, got_2, level_out, level_in, spectra, back_2, took_2,
     back_1, took_1, lines, last_z_out, last_z_in, last_x_out, last_x_in, last_corner_in,
     load, group_load, level_send, level_recv, rim_send, rim_recv, last_send, last_recv, corner_recv,
     send_1, recv_1, send_2, recv_2, send_3, recv_3, send_4, recv_4,
@@ -244,9 +246,7 @@
         pltpu.make_async_copy(source, target, load.at[i])
         for i, (source, target) in enumerate(
             (
-                (grid_at.at[:, :, 0:8, :], z_rows.at[0]),
-                (grid_at.at[:, :, 40:48, :], z_rows.at[1]),
-                (grid_at.at[2:34, :, 8:40, :], charge),
+                (grid.at[2:34, :, 8:40, :], charge),
                 (ty_at, ty),
                 (tz_at, tz),
                 (kernel_at, kernel),
@@ -255,19 +255,15 @@
             )
         )
     ]
-    for copy in loads:
+    for copy in loads[:2]:
         copy.start()
-    for step in range(charges.shape[0] // GROUP):
-        group_copy(step, projection_at, projection, group_load).start()
 
     def pack_rims(x, carry):
         for tile in range(4):
-            z_out[0, x, 2 * tile : 2 * tile + 2, :] = z_rows[0, x, tile, 6:8, :]
-            z_out[1, x, 2 * tile : 2 * tile + 2, :] = z_rows[1, x, tile, 0:2, :]
-        return carry
-
-    loads[0].wait()
-    loads[1].wait()
+            z_out[0, x, 2 * tile : 2 * tile + 2, :] = grid[x, tile, 6:8, :]
+            z_out[1, x, 2 * tile : 2 * tile + 2, :] = grid[x, tile, 40:42, :]
+        return carry
+
     lax.fori_loop(0, 36, pack_rims, 0, unroll=4)
     pl.semaphore_wait(barrier, n_slab + n_pencil + 2)
     ends = ((0, 2), (34, 36))
@@ -275,14 +271,16 @@
     for a, dz in sides:
         rims.append((z_out.at[a, 2:34], z_in.at[1 - a], on_slab(dz)))
     for b, dx in sides:
-        rims.append((grid_at.at[ends[b][0] : ends[b][1], :, 8:40, :], x_in.at[1 - b], on_pencil(dx)))
+        rims.append((grid.at[ends[b][0] : ends[b][1], :, 8:40, :], x_in.at[1 - b], on_pencil(dx)))
     for a, dz in sides:
         for b, dx in sides:
             rims.append((z_out.at[a, ends[b][0] : ends[b][1]], corner_in.at[1 - a, 1 - b], at(dz, dx)))
     for i, (source, target, device) in enumerate(rims):
         remote(source, target, rim_send.at[i], rim_recv.at[i], device).start()
-
-    loads[2].wait()
+    for copy in loads[2:]:
+        copy.start()
+
+    loads[0].wait()
     wait_recv(z_in.at[1], rim_recv.at[0])
     wait_recv(z_in.at[0], rim_recv.at[1])
 
@@ -293,7 +291,7 @@
         return carry
 
     lax.fori_loop(0, 32, add_rims, 0, unroll=4)
-    loads[3].wait()
+    loads[1].wait()
 
     def forward_y(step, carry):
         chunk = lax.rem(step + 1, CHUNKS)
@@ -334,9 +332,11 @@
 
     lax.fori_loop(0, CHUNKS, forward_y, 0)
     lax.fori_loop(0, CHUNKS, lambda step, carry: to_slabs(1, lax.rem(step + 1, CHUNKS)), 0)
+    for step in range(charges.shape[0] // GROUP):
+        group_copy(step, projection_at, projection, group_load).start()
 
     slots, panels = charges.shape
-    loads[5].wait()
+    loads[3].wait()
     first = jnp.logical_and(slab == 0, pencil == 0)
     middle = jnp.logical_and(slab == 4, pencil == 0)
 
@@ -348,12 +348,12 @@
         remote(level_out, level_in, level_send, level_recv, (0, pencil)).start()
 
     slot = lax.broadcasted_iota(jnp.int32, (slots, panels), 0)
-    coarse = jnp.where(slot < count[...], charges[...], 0.0).astype(BF16)
+    coarse = jnp.where(slot < count[0], charges[...], 0.0).astype(BF16)
     slot = lax.broadcasted_iota(jnp.int32, (slots, slots), 0)
     chosen = jnp.where(slot == pairs[1:2, :], 1.0, 0.0)
     sources[...] = jnp.dot(chosen.T.astype(BF16), coarse, preferred_element_type=F32)
-    loads[4].wait()
-    loads[7].wait()
+    loads[2].wait()
+    loads[5].wait()
 
     def near_group(group, carry):
         rows = pl.ds(pl.multiple_of(8 * group, 8), 8)
@@ -401,7 +401,7 @@
 
     lax.fori_loop(0, 2 * CHUNKS - 2, forward_z, 0)
 
-    loads[6].wait()
+    loads[4].wait()
     unit = 1.0 / (NX * NY * NZ)
 
     def stacked(real, imag):
@@ -517,16 +517,6 @@
     lax.fori_loop(4, 8, return_x, 0)
     lax.fori_loop(2, 8, inverse_z, 0)
 
-    slot = lax.broadcasted_iota(jnp.int32, (slots, slots), 0)
-    chosen = jnp.where(slot == pairs[0:1, :], 1.0, 0.0).astype(BF16)
-    rest = terms[...]
-    total = jnp.zeros(near.shape, F32)
-    for _ in range(3):
-        part = rest.astype(BF16)
-        rest = rest - part.astype(F32)
-        total = total + jnp.dot(chosen, part, preferred_element_type=F32)
-    near[...] = total
-
     row_starts = (2, 32)
     last = []
     for b, dx in sides:
@@ -580,6 +570,17 @@
         return carry
 
     lax.fori_loop(0, CHUNKS, inverse_y, 0)
+
+    slot = lax.broadcasted_iota(jnp.int32, (slots, slots), 0)
+    chosen = jnp.where(slot == pairs[0:1, :], 1.0, 0.0).astype(BF16)
+    rest = terms[...]
+    total = jnp.zeros(near.shape, F32)
+    for _ in range(3):
+        part = rest.astype(BF16)
+        rest = rest - part.astype(F32)
+        total = total + jnp.dot(chosen, part, preferred_element_type=F32)
+    near[...] = total
+
     lax.fori_loop(0, CHUNKS - 1, take_planes, 0)
     for i, (source, target, device) in enumerate(last):
         wait_recv(target, corner_recv.at[i])
@@ -623,8 +624,7 @@
         rows = group_rows(step)
         box = lane_sums(values[...].reshape(GROUP * BOX, 128)).reshape(GROUP, BOX, 128)
         far = jnp.sum(projection[rows] * box, axis=1)
-        slot = step * GROUP + lax.broadcasted_iota(jnp.int32, (GROUP, 128), 0)
-        result[rows, :] = jnp.where(slot < count[...], far + near[rows, :], 0.0)
+        result[rows, :] = far + near[rows, :]
         return carry
 
     lax.fori_loop(0, slots // GROUP, gather_group, 0)
@@ -638,9 +638,9 @@
     return pl.pallas_call(
         field_kernel,
         in_specs=[
-            pl.BlockSpec(memory_space=pltpu.SMEM),
+            *[pl.BlockSpec(memory_space=pltpu.SMEM)] * 2,
             *[pl.BlockSpec(memory_space=vmem)] * 3,
-            *[pl.BlockSpec(memory_space=pl.ANY)] * 7,
+            *[pl.BlockSpec(memory_space=pl.ANY)] * 6,
         ],
         out_specs=pl.BlockSpec(memory_space=vmem),
         out_shape=jax.ShapeDtypeStruct((slots, panels), F32),
@@ -655,7 +655,6 @@
             vmem((GROUP, BOX, panels), F32),
             vmem((36 * 4 * 48, 128), F32),
             vmem((32, 4, 32, 128), F32),
-            vmem((2, 36, 4, 8, 128), F32),
             vmem((2, 36, 8, 128), F32),
             vmem((2, 32, 8, 128), F32),
             vmem((2, 2, 4, 32, 128), F32),
@@ -677,7 +676,7 @@
             vmem((2, 2, 4, 32, 128), F32),
             vmem((2, 2, 4, 32, 128), F32),
             vmem((2, 2, 2, 8, 128), F32),
-            dma((8,)),
+            dma((6,)),
             dma((slots // GROUP,)),
             dma,
             dma,
@@ -696,18 +695,18 @@
             dma((2, CHUNKS)),
         ],
         compiler_params=pltpu.CompilerParams(
-            collective_id=0, has_side_effects=True, vmem_limit_bytes=62 << 20
+            collective_id=0, has_side_effects=True, vmem_limit_bytes=57 << 20
         ),
         cost_estimate=pl.CostEstimate(flops=10**10, bytes_accessed=10**7, transcendentals=0),
     )(anchors, count, pairs, charges, grid, projection, matrices, kernel, *tables)
 
 
 def shards(charges, projection, anchors, block_count, near_pairs, near_matrices, kernel_hat):
-    panels = charges.shape[1]
-    grid = scatter(anchors.T, block_count, projection, charges).reshape(36, 4, 48, 128)
+    grid = pltpu.with_memory_space_constraint(scatter(anchors.T, block_count, projection, charges), pltpu.VMEM)
     levels = jnp.transpose(kernel_hat.reshape(NX, 4, 2, 128), (0, 2, 1, 3)).reshape(NX * 8, 128)
-    count = jnp.broadcast_to(block_count[:, None], (1, panels))
-    return field(anchors.T, count, near_pairs.T, charges, grid, projection, near_matrices, levels)
+    total = field(anchors.T, block_count, near_pairs.T, charges, grid, projection, near_matrices, levels)
+    in_use = lax.broadcasted_iota(jnp.int32, total.shape, 0) < block_count[0]
+    return jnp.where(in_use, total, 0.0)
 
 
 def solution(mesh):

time: 105 us -> 101 us (0.962)
  Pallas kernels: 101 us -> 98.2 us
  local copies, waits for them, and re-layouts: 2.08 us -> 0 us
  other arithmetic: 0 us -> 1.67 us
    pallas_call x1, Pallas kernels: 10.8 us -> 8.57 us  [scatter(): pl.pallas_call(scatter_kernel, in_specs=[smem, smem, pl.BlockSpec(memory_...]
    select_n x0 -> x1, other arithmetic: none -> 1.66 us  [shards(): return jnp.where(in_use, total, 0.0)]
    unnamed x1 -> x0, local copies, waits for them, and re-layouts: 1.57 us -> none
where the time goes in v7:
time: 101 us
  Pallas kernels  98.2 us (97%)
  other arithmetic  1.67 us (2%)
    pallas_call x1, Pallas kernels, field(): pl.pallas_call(field_kernel, in_specs=[*[pl.BlockSpec(memory_space=pltpu....  89.7 us
    pallas_call x1, Pallas kernels, scatter(): pl.pallas_call(scatter_kernel, in_specs=[smem, smem, pl.BlockSpec(memory_...  8.57 us

profile of v7, /device:TPU:1, one launch (start us, length us, event | category | flops | bytes accessed | tf_op | source)
XLA Modules:
  0.0 100.6 jit_solution(16128484110865715019)
XLA Ops:
  0.7 8.6 %shard_map.100.grid = f32[36,4,48,128]{3,2,1,0:T(8,128)S(1)} custom-call(s32[3,256]{1,0:T(4,128)} %bitcast.9, s32[1]{0:T(128)} %copy.12.count, f32[256,64,128]{2,1,0:T(8,128)} %projection_at.3, f32[256,128]{1,0:T(8,128)} %charges.3), custom_call_target="tpu_custom_call" | custom-call | tf_op jit(solution)/shard_map/pallas_call | solution.py:109
  9.2 89.7 %shard_map.101 = f32[256,128]{1,0:T(8,128)} custom-call(s32[3,256]{1,0:T(4,128)} %bitcast.10, s32[1]{0:T(128)} %copy.12.count, s32[2,256]{1,0:T(2,128)} %bitcast.12, f32[256,128]{1,0:T(8,128)} %charges.3, f32[36,4,48,128]{3,2,1,0:T(8,128)S(1)} %shard_map.100.grid, f32[256,64,128]{2,1,0:T(8,128)} %projection_at.3, bf16[256,128,128]{2,1,0:T(8,128)(2,1)} %matrices_at.1, ...), custom_call_target="tpu_custom_call" | custom-call | flops 10000000000 | bytes 10000000 | tf_op jit(solution)/shard_map/pallas_call | solution.py:638
  98.9 1.7 %broadcast_select_fusion = f32[256,128]{1,0:T(8,128)} fusion(f32[256,128]{1,0:T(8,128)} %shard_map.101, pred[256]{0:T(512)(128)(4,1)S(1)} %iota_compare_fusion), kind=kLoop, calls=%fused_computation | loop fusion | flops 32768 | bytes 262400 | tf_op jit(solution)/shard_map/jit(_where)/select_n | solution.py:709
  (1 shorter events, 0.0 us)

commit v8 on v7

--- a/solution.py
+++ b/solution.py
@@ -193,7 +193,7 @@
 def field_kernel(
     anchors, count, pairs, charges, grid, projection_at, matrices_at, kernel_at, ty_at, tz_at, tx_at,
     result,
-    projection, matrices, kernel, ty, tz, tx, sources, terms, near, values, out,
+    projection, matrices, kernel, ty, tz, tx, sources, terms, near, values, out, mirror,
     charge, z_out, z_in, x_in, corner_in, sent_1, got_1, sent_2, got_2, level_out, level_in, spectra, back_2, took_2,
     back_1, took_1, lines, last_z_out, last_z_in, last_x_out, last_x_in, last_corner_in,
     load, group_load, level_send, level_recv, rim_send, rim_recv, last_send, last_recv, corner_recv,
@@ -351,6 +351,9 @@
     coarse = jnp.where(slot < count[0], charges[...], 0.0).astype(BF16)
     slot = lax.broadcasted_iota(jnp.int32, (slots, slots), 0)
     chosen = jnp.where(slot == pairs[1:2, :], 1.0, 0.0)
+    row = lax.broadcasted_iota(jnp.int32, (256, 256), 0)
+    lane = lax.broadcasted_iota(jnp.int32, (256, 256), 1)
+    mirror[...] = jnp.where((row + lane) & 255 == 0, 1.0, 0.0).astype(BF16)
     sources[...] = jnp.dot(chosen.T.astype(BF16), coarse, preferred_element_type=F32)
     loads[2].wait()
     loads[5].wait()
@@ -405,50 +408,54 @@
     unit = 1.0 / (NX * NY * NZ)
 
     def stacked(real, imag):
-        real, imag = halves(real), halves(imag)
         return tuple(
             jnp.concatenate([jnp.concatenate([r, i], axis=1), jnp.concatenate([i, -r], axis=1)], axis=0)
             for r, i in zip(real, imag)
         )
 
+    def mirrored(pieces):
+        return tuple(jnp.dot(piece, mirror[...], preferred_element_type=F32).astype(BF16) for piece in pieces)
+
+    def levels(start, unit):
+        pieces = [kernel[pl.ds(start + 4 * i, 256, stride=16), :] for i in range(2)]
+        return jnp.concatenate(pieces, axis=1) * unit
+
     def along_x(parity):
         wait_recv(got_2.at[parity, :, 0 : 32 * (n_pencil - 1), :], recv_2.at[parity])
-        for kx in range(2):
+
+        def found(kx, twin):
             parts = []
             for part in range(2):
                 low, high = got_2[parity, part, 0:256, :], got_2[parity, part, 256:512, :]
-                parts.append(low - high if kx else low + high)
-            table = (tx[0, kx], tx[1, kx])
-            found = dot_3(table, stacked(*parts))
-            if parity:
-                green = jnp.concatenate(
-                    [kernel[pl.ds(8 * kx + 4 * i + 1, 256, stride=16), :] for i in range(2)], axis=1
-                ) * (2.0 * unit)
-            else:
-                own = jnp.where(slab < 4, 0, 2)
-                green = jnp.concatenate(
-                    [kernel[pl.ds(own + 8 * kx + 4 * i, 256, stride=16), :] for i in range(2)], axis=1
-                ) * jnp.where(first, unit, 2.0 * unit)
-            spectra[kx, 0] = found[:, 0:256] * green
-            spectra[kx, 1] = found[:, 256:512] * green
-            if not parity:
-
-                @pl.when(first)
-                def _():
-                    if not kx:
-                        wait_recv(level_in, level_recv)
-                    other = level_in[kx] * unit
-                    row = lax.broadcasted_iota(jnp.int32, (256, 256), 0)
-                    lane = lax.broadcasted_iota(jnp.int32, (256, 256), 1)
-                    mirror = jnp.where((row + lane) % 256 == 0, 1.0, 0.0).astype(BF16)
-                    flipped = [
-                        sum(jnp.dot(piece, mirror, preferred_element_type=F32) for piece in halves(value)) for value in parts
-                    ]
-                    twin = dot_3(table, stacked(flipped[0], -flipped[1]))
-                    mean, rest = 0.5 * (green + other), 0.5 * (green - other)
+                parts.append(halves(low - high if kx else low + high))
+            right = stacked(*parts)
+            if twin:
+                real, imag = (mirrored(pieces) for pieces in parts)
+                other = stacked(real, tuple(-piece for piece in imag))
+                right = tuple(jnp.concatenate(both, axis=1) for both in zip(right, other))
+            return dot_3((tx[0, kx], tx[1, kx]), right)
+
+        def plain():
+            own = 1 if parity else jnp.where(slab < 4, 0, 2)
+            for kx in range(2):
+                both, green = found(kx, False), levels(own + 8 * kx, 2.0 * unit)
+                spectra[kx, 0] = both[:, 0:256] * green
+                spectra[kx, 1] = both[:, 256:512] * green
+
+        if parity:
+            plain()
+        else:
+            pl.when(jnp.logical_not(first))(plain)
+
+            @pl.when(first)
+            def _():
+                wait_recv(level_in, level_recv)
+                for kx in range(2):
+                    both, green, other = found(kx, True), levels(8 * kx, 0.5 * unit), level_in[kx] * (0.5 * unit)
+                    mean, rest = green + other, green - other
                     for part in range(2):
-                        lanes = slice(256 * part, 256 * part + 256)
-                        spectra[kx, part] = mean * found[:, lanes] + rest * twin[:, lanes]
+                        one, two = (both[:, 256 * k : 256 * k + 256] for k in (part, part + 2))
+                        spectra[kx, part] = mean * one + rest * two
 
         ends = []
         for kx in range(2):
@@ -510,8 +517,9 @@
         return lax.fori_loop(1, n_slab, send, carry)
 
     along_x(0)
-    lax.fori_loop(0, 2, return_x, 0)
-    lax.fori_loop(2, 4, lambda turn, carry: return_x(turn, forward_z(turn + 4, carry)), 0)
+    lax.fori_loop(0, 1, return_x, 0)
+    lax.fori_loop(1, 3, lambda turn, carry: return_x(turn, forward_z(turn + 5, carry)), 0)
+    lax.fori_loop(3, 4, return_x, 0)
     lax.fori_loop(0, 2, inverse_z, 0)
     along_x(1)
     lax.fori_loop(4, 8, return_x, 0)
@@ -643,7 +651,7 @@
             *[pl.BlockSpec(memory_space=pl.ANY)] * 6,
         ],
         out_specs=pl.BlockSpec(memory_space=vmem),
-        out_shape=jax.ShapeDtypeStruct((slots, panels), F32),
+        out_shape=pltpu.VMEM((slots, panels), F32),
         scratch_shapes=[
             vmem(projection.shape, F32),
             vmem(matrices.shape, BF16),
@@ -654,6 +662,7 @@
             vmem((slots, panels), F32),
             vmem((GROUP, BOX, panels), F32),
             vmem((36 * 4 * 48, 128), F32),
+            vmem((256, 256), BF16),
             vmem((32, 4, 32, 128), F32),
             vmem((2, 36, 8, 128), F32),
             vmem((2, 32, 8, 128), F32),

time: 101 us -> 101 us (level)
  no operation moved by 1% of the time
where the time goes in v8:
time: 101 us; the launch traced here: 100 us
  Pallas kernels  99 us (98%)
    pallas_call x1, Pallas kernels, field(): pl.pallas_call(field_kernel, in_specs=[*[pl.BlockSpec(memory_space=pltpu....  90.5 us
    pallas_call x1, Pallas kernels, scatter(): pl.pallas_call(scatter_kernel, in_specs=[smem, smem, pl.BlockSpec(memory_...  8.59 us

profile of v8, /device:TPU:1, one launch (start us, length us, event | category | flops | bytes accessed | tf_op | source)
XLA Modules:
  0.0 100.5 jit_solution(12433974898695910395)
XLA Ops:
  0.7 8.6 %shard_map.100.grid = f32[36,4,48,128]{3,2,1,0:T(8,128)S(1)} custom-call(s32[3,256]{1,0:T(4,128)} %bitcast.9, s32[1]{0:T(128)} %copy.12.count, f32[256,64,128]{2,1,0:T(8,128)} %projection_at.3, f32[256,128]{1,0:T(8,128)} %charges.3), custom_call_target="tpu_custom_call" | custom-call | tf_op jit(solution)/shard_map/pallas_call | solution.py:109
  9.2 90.5 %shard_map.101 = f32[256,128]{1,0:T(8,128)S(1)} custom-call(s32[3,256]{1,0:T(4,128)} %bitcast.10, s32[1]{0:T(128)} %copy.12.count, s32[2,256]{1,0:T(2,128)} %bitcast.12, f32[256,128]{1,0:T(8,128)} %charges.3, f32[36,4,48,128]{3,2,1,0:T(8,128)S(1)} %shard_map.100.grid, f32[256,64,128]{2,1,0:T(8,128)} %projection_at.3, bf16[256,128,128]{2,1,0:T(8,128)(2,1)} %matrices_at.1, ...), custom_call_target="tpu_custom_call" | custom-call | flops 10000000000 | bytes 10000000 | tf_op jit(solution)/shard_map/pallas_call | solution.py:646
  99.7 0.8 broadcast_select_fusion
  (1 shorter events, 0.0 us)

commit v9 on v8

--- a/solution.py
+++ b/solution.py
@@ -247,15 +247,15 @@
         for i, (source, target) in enumerate(
             (
                 (grid.at[2:34, :, 8:40, :], charge),
+                (kernel_at, kernel),
                 (ty_at, ty),
                 (tz_at, tz),
-                (kernel_at, kernel),
                 (tx_at, tx),
                 (matrices_at, matrices),
             )
         )
     ]
-    for copy in loads[:2]:
+    for copy in loads[:3]:
         copy.start()
 
     def pack_rims(x, carry):
@@ -277,7 +277,18 @@
             rims.append((z_out.at[a, ends[b][0] : ends[b][1]], corner_in.at[1 - a, 1 - b], at(dz, dx)))
     for i, (source, target, device) in enumerate(rims):
         remote(source, target, rim_send.at[i], rim_recv.at[i], device).start()
-    for copy in loads[2:]:
+    first = jnp.logical_and(slab == 0, pencil == 0)
+    middle = jnp.logical_and(slab == 4, pencil == 0)
+    loads[1].wait()
+
+    @pl.when(middle)
+    def _():
+        for kx in range(2):
+            for i in range(2):
+                level_out[kx, :, 128 * i : 128 * i + 128] = kernel[pl.ds(8 * kx + 4 * i, 256, stride=16), :]
+        remote(level_out, level_in, level_send, level_recv, (0, pencil)).start()
+
+    for copy in loads[3:]:
         copy.start()
 
     loads[0].wait()
@@ -291,7 +302,7 @@
         return carry
 
     lax.fori_loop(0, 32, add_rims, 0, unroll=4)
-    loads[1].wait()
+    loads[2].wait()
 
     def forward_y(step, carry):
         chunk = lax.rem(step + 1, CHUNKS)
@@ -316,7 +327,9 @@
             columns = halves(jnp.concatenate(halved, axis=1))
             freqs = dot_3((ty[0, parity], ty[1, parity]), columns, ((1,), (1,)))
             sent_1[parity, chunk] = freqs.reshape(n_slab, 32, 256)
-        return to_slabs(0, chunk)
+            if not parity:
+                to_slabs(0, chunk)
+        return carry
 
     def to_slabs(parity, chunk):
         got_1[parity, chunk, slab] = sent_1[parity, chunk, slab]
@@ -336,17 +349,6 @@
         group_copy(step, projection_at, projection, group_load).start()
 
     slots, panels = charges.shape
-    loads[3].wait()
-    first = jnp.logical_and(slab == 0, pencil == 0)
-    middle = jnp.logical_and(slab == 4, pencil == 0)
-
-    @pl.when(middle)
-    def _():
-        for kx in range(2):
-            for i in range(2):
-                level_out[kx, :, 128 * i : 128 * i + 128] = kernel[pl.ds(8 * kx + 4 * i, 256, stride=16), :]
-        remote(level_out, level_in, level_send, level_recv, (0, pencil)).start()
-
     slot = lax.broadcasted_iota(jnp.int32, (slots, panels), 0)
     coarse = jnp.where(slot < count[0], charges[...], 0.0).astype(BF16)
     slot = lax.broadcasted_iota(jnp.int32, (slots, slots), 0)
@@ -355,7 +357,7 @@
     lane = lax.broadcasted_iota(jnp.int32, (256, 256), 1)
     mirror[...] = jnp.where((row + lane) & 255 == 0, 1.0, 0.0).astype(BF16)
     sources[...] = jnp.dot(chosen.T.astype(BF16), coarse, preferred_element_type=F32)
-    loads[2].wait()
+    loads[3].wait()
     loads[5].wait()
 
     def near_group(group, carry):
@@ -592,27 +594,13 @@
     lax.fori_loop(0, CHUNKS - 1, take_planes, 0)
     for i, (source, target, device) in enumerate(last):
         wait_recv(target, corner_recv.at[i])
-        wait_send(source, last_send.at[i])
     for b, start in ((0, 0), (1, 34)):
         for x in range(2):
             for tile in range(4):
                 out[pl.ds(row_of(start + x, tile, 8), 32), :] = last_x_in[b, x, tile]
                 for a, row in ((0, 6), (1, 40)):
                     out[pl.ds(row_of(start + x, tile, row), 2), :] = last_corner_in[b, a, x, 2 * tile : 2 * tile + 2, :]
-    for i, (source, target, device) in enumerate(rims):
-        wait_send(source, rim_send.at[i])
-    wait_send(sent_1.at[:, :, 0 : n_slab - 1], send_1)
-    wait_send(got_2.at[:, :, 0 : 32 * (n_pencil - 1), :], send_2)
-    wait_send(got_2.at[:, :, 0 : 32 * (n_pencil - 1), :], send_3)
-    wait_send(back_1.at[:, :, 0 : n_slab - 1], send_4)
-
-    @pl.when(middle)
-    def _():
-        wait_send(level_out, level_send)
-
     take_planes(CHUNKS - 1, 0)
-    for a in range(2):
-        wait_send(last_z_out.at[:, a], last_send.at[6 + a])
 
     def gather_group(step, carry):
         def pick(turn, carry):
@@ -636,6 +624,20 @@
         return carry
 
     lax.fori_loop(0, slots // GROUP, gather_group, 0)
+    for i, (source, target, device) in enumerate(last):
+        wait_send(source, last_send.at[i])
+    for a in range(2):
+        wait_send(last_z_out.at[:, a], last_send.at[6 + a])
+    for i, (source, target, device) in enumerate(rims):
+        wait_send(source, rim_send.at[i])
+    wait_send(sent_1.at[:, :, 0 : n_slab - 1], send_1)
+    wait_send(got_2.at[:, :, 0 : 32 * (n_pencil - 1), :], send_2)
+    wait_send(got_2.at[:, :, 0 : 32 * (n_pencil - 1), :], send_3)
+    wait_send(back_1.at[:, :, 0 : n_slab - 1], send_4)
+
+    @pl.when(middle)
+    def _():
+        wait_send(level_out, level_send)
 
 
 def field(anchors, count, pairs, charges, grid, projection, matrices, kernel):

time: 101 us -> 101 us (level)
  no operation moved by 1% of the time
where the time goes in v9:
time: 101 us; the launch traced here: 99.9 us
  Pallas kernels  98.5 us (98%)
    pallas_call x1, Pallas kernels, field(): pl.pallas_call(field_kernel, in_specs=[*[pl.BlockSpec(memory_space=pltpu....  89.9 us
    pallas_call x1, Pallas kernels, scatter(): pl.pallas_call(scatter_kernel, in_specs=[smem, smem, pl.BlockSpec(memory_...  8.61 us

profile of v9, /device:TPU:1, one launch (start us, length us, event | category | flops | bytes accessed | tf_op | source)
XLA Modules:
  0.0 99.9 jit_solution(18062112234776154897)
XLA Ops:
  0.7 8.6 %shard_map.100.grid = f32[36,4,48,128]{3,2,1,0:T(8,128)S(1)} custom-call(s32[3,256]{1,0:T(4,128)} %bitcast.9, s32[1]{0:T(128)} %copy.12.count, f32[256,64,128]{2,1,0:T(8,128)} %projection_at.3, f32[256,128]{1,0:T(8,128)} %charges.3), custom_call_target="tpu_custom_call" | custom-call | tf_op jit(solution)/shard_map/pallas_call | solution.py:109
  9.3 89.9 %shard_map.101 = f32[256,128]{1,0:T(8,128)S(1)} custom-call(s32[3,256]{1,0:T(4,128)} %bitcast.10, s32[1]{0:T(128)} %copy.12.count, s32[2,256]{1,0:T(2,128)} %bitcast.12, f32[256,128]{1,0:T(8,128)} %charges.3, f32[36,4,48,128]{3,2,1,0:T(8,128)S(1)} %shard_map.100.grid, f32[256,64,128]{2,1,0:T(8,128)} %projection_at.3, bf16[256,128,128]{2,1,0:T(8,128)(2,1)} %matrices_at.1, ...), custom_call_target="tpu_custom_call" | custom-call | flops 10000000000 | bytes 10000000 | tf_op jit(solution)/shard_map/pallas_call | solution.py:648
  99.2 0.8 broadcast_select_fusion
  (1 shorter events, 0.0 us)

commit v10 on v9

--- a/solution.py
+++ b/solution.py
@@ -247,15 +247,15 @@
         for i, (source, target) in enumerate(
             (
                 (grid.at[2:34, :, 8:40, :], charge),
+                (ty_at, ty),
                 (kernel_at, kernel),
-                (ty_at, ty),
                 (tz_at, tz),
                 (tx_at, tx),
                 (matrices_at, matrices),
             )
         )
     ]
-    for copy in loads[:3]:
+    for copy in loads[:2]:
         copy.start()
 
     def pack_rims(x, carry):
@@ -279,17 +279,17 @@
         remote(source, target, rim_send.at[i], rim_recv.at[i], device).start()
     first = jnp.logical_and(slab == 0, pencil == 0)
     middle = jnp.logical_and(slab == 4, pencil == 0)
-    loads[1].wait()
+    for copy in loads[2:]:
+        copy.start()
 
     @pl.when(middle)
     def _():
+        loads[2].wait()
         for kx in range(2):
             for i in range(2):
                 level_out[kx, :, 128 * i : 128 * i + 128] = kernel[pl.ds(8 * kx + 4 * i, 256, stride=16), :]
         remote(level_out, level_in, level_send, level_recv, (0, pencil)).start()
 
-    for copy in loads[3:]:
-        copy.start()
 
     loads[0].wait()
     wait_recv(z_in.at[1], rim_recv.at[0])
@@ -302,7 +302,7 @@
         return carry
 
     lax.fori_loop(0, 32, add_rims, 0, unroll=4)
-    loads[2].wait()
+    loads[1].wait()
 
     def forward_y(step, carry):
         chunk = lax.rem(step + 1, CHUNKS)
@@ -357,6 +357,7 @@
     lane = lax.broadcasted_iota(jnp.int32, (256, 256), 1)
     mirror[...] = jnp.where((row + lane) & 255 == 0, 1.0, 0.0).astype(BF16)
     sources[...] = jnp.dot(chosen.T.astype(BF16), coarse, preferred_element_type=F32)
+    pl.when(jnp.logical_not(middle))(loads[2].wait)
     loads[3].wait()
     loads[5].wait()
 
@@ -373,10 +374,11 @@
         terms[rows, :] = total
         return carry
 
-    near_groups = slots // 8 // (4 * CHUNKS)
+    near_turns = 2 * CHUNKS - 2
 
     def near_share(turn):
-        lax.fori_loop(turn * near_groups, (turn + 1) * near_groups, near_group, 0)
+        start, stop = ((slots // 8) * t // near_turns for t in (jnp.minimum(turn, near_turns), jnp.minimum(turn + 1, near_turns)))
+        lax.fori_loop(start, stop, near_group, 0)
 
     def forward_z(turn, carry):
         parity, chunk = turn // CHUNKS, lax.rem(turn + 1, CHUNKS)
@@ -493,7 +495,6 @@
 
     def inverse_z(turn, carry):
         parity, chunk = turn // CHUNKS, turns(lax.rem(turn, CHUNKS))
-        near_share(2 * CHUNKS + turn)
         wait_recv(took_2.at[parity, chunk, 0 : n_pencil - 1], recv_3.at[parity, chunk])
         rows = jnp.concatenate([took_2[parity, chunk, :, part].reshape(128, 256) for part in range(2)], axis=1)
         space = dot_3(halves(rows), (tz[0], tz[1]), ((1,), (1,)))

time: 101 us -> 99.9 us (0.989)
  no operation moved by 1% of the time
where the time goes in v10:
time: 99.9 us; the launch traced here: 99.7 us
  Pallas kernels  98.3 us (98%)
    pallas_call x1, Pallas kernels, field(): pl.pallas_call(field_kernel, in_specs=[*[pl.BlockSpec(memory_space=pltpu....  89.7 us
    pallas_call x1, Pallas kernels, scatter(): pl.pallas_call(scatter_kernel, in_specs=[smem, smem, pl.BlockSpec(memory_...  8.55 us

profile of v10, /device:TPU:1, one launch (start us, length us, event | category | flops | bytes accessed | tf_op | source)
XLA Modules:
  0.0 99.7 jit_solution(16983431350016223265)
XLA Ops:
  0.7 8.6 %shard_map.100.grid = f32[36,4,48,128]{3,2,1,0:T(8,128)S(1)} custom-call(s32[3,256]{1,0:T(4,128)} %bitcast.9, s32[1]{0:T(128)} %copy.12.count, f32[256,64,128]{2,1,0:T(8,128)} %projection_at.3, f32[256,128]{1,0:T(8,128)} %charges.3), custom_call_target="tpu_custom_call" | custom-call | tf_op jit(solution)/shard_map/pallas_call | solution.py:109
  9.2 89.7 %shard_map.101 = f32[256,128]{1,0:T(8,128)S(1)} custom-call(s32[3,256]{1,0:T(4,128)} %bitcast.10, s32[1]{0:T(128)} %copy.12.count, s32[2,256]{1,0:T(2,128)} %bitcast.12, f32[256,128]{1,0:T(8,128)} %charges.3, f32[36,4,48,128]{3,2,1,0:T(8,128)S(1)} %shard_map.100.grid, f32[256,64,128]{2,1,0:T(8,128)} %projection_at.3, bf16[256,128,128]{2,1,0:T(8,128)(2,1)} %matrices_at.1, ...), custom_call_target="tpu_custom_call" | custom-call | flops 10000000000 | bytes 10000000 | tf_op jit(solution)/shard_map/pallas_call | solution.py:649
  98.9 0.8 broadcast_select_fusion
  (1 shorter events, 0.0 us)

commit v11 on v10

--- a/solution.py
+++ b/solution.py
@@ -236,8 +236,8 @@
         return carry
 
     sides = ((0, -1), (1, 1))
-    lax.fori_loop(1, n_slab, greet_slab, 0)
-    lax.fori_loop(1, n_pencil, greet_pencil, 0)
+    lax.fori_loop(1, n_slab, greet_slab, 0, unroll=7)
+    lax.fori_loop(1, n_pencil, greet_pencil, 0, unroll=5)
     for _, dz in sides:
         for _, dx in sides:
             greet(at(dz, dx))
@@ -341,7 +341,7 @@
             ).start()
             return carry
 
-        return lax.fori_loop(1, n_slab, send, 0)
+        return lax.fori_loop(1, n_slab, send, 0, unroll=7)
 
     lax.fori_loop(0, CHUNKS, forward_y, 0)
     lax.fori_loop(0, CHUNKS, lambda step, carry: to_slabs(1, lax.rem(step + 1, CHUNKS)), 0)
@@ -404,7 +404,7 @@
             ).start()
             return carry
 
-        return lax.fori_loop(1, n_pencil, send, carry)
+        return lax.fori_loop(1, n_pencil, send, carry, unroll=5)
 
     lax.fori_loop(0, 2 * CHUNKS - 2, forward_z, 0)
 
@@ -491,7 +491,7 @@
             ).start()
             return carry
 
-        return lax.fori_loop(1, n_pencil, send, carry)
+        return lax.fori_loop(1, n_pencil, send, carry, unroll=5)
 
     def inverse_z(turn, carry):
         parity, chunk = turn // CHUNKS, turns(lax.rem(turn, CHUNKS))
@@ -517,7 +517,7 @@
             ).start()
             return carry
 
-        return lax.fori_loop(1, n_slab, send, carry)
+        return lax.fori_loop(1, n_slab, send, carry, unroll=7)
 
     along_x(0)
     lax.fori_loop(0, 1, return_x, 0)
@@ -525,8 +525,10 @@
     lax.fori_loop(3, 4, return_x, 0)
     lax.fori_loop(0, 2, inverse_z, 0)
     along_x(1)
-    lax.fori_loop(4, 8, return_x, 0)
-    lax.fori_loop(2, 8, inverse_z, 0)
+    lax.fori_loop(4, 5, return_x, 0)
+    lax.fori_loop(5, 7, lambda turn, carry: inverse_z(turn - 3, return_x(turn, carry)), 0)
+    lax.fori_loop(7, 8, return_x, 0)
+    lax.fori_loop(4, 8, inverse_z, 0)
 
     row_starts = (2, 32)
     last = []

time: 99.9 us -> 99.8 us (level)
  no operation moved by 1% of the time
where the time goes in v11:
time: 99.8 us; the launch traced here: 99.7 us
  Pallas kernels  98.3 us (98%)
    pallas_call x1, Pallas kernels, field(): pl.pallas_call(field_kernel, in_specs=[*[pl.BlockSpec(memory_space=pltpu....  89.8 us
    pallas_call x1, Pallas kernels, scatter(): pl.pallas_call(scatter_kernel, in_specs=[smem, smem, pl.BlockSpec(memory_...  8.54 us

profile of v11, /device:TPU:1, one launch (start us, length us, event | category | flops | bytes accessed | tf_op | source)
XLA Modules:
  0.0 99.7 jit_solution(16448628621279658146)
XLA Ops:
  0.7 8.5 %shard_map.100.grid = f32[36,4,48,128]{3,2,1,0:T(8,128)S(1)} custom-call(s32[3,256]{1,0:T(4,128)} %bitcast.9, s32[1]{0:T(128)} %copy.12.count, f32[256,64,128]{2,1,0:T(8,128)} %projection_at.3, f32[256,128]{1,0:T(8,128)} %charges.3), custom_call_target="tpu_custom_call" | custom-call | tf_op jit(solution)/shard_map/pallas_call | solution.py:109
  9.2 89.8 %shard_map.101 = f32[256,128]{1,0:T(8,128)S(1)} custom-call(s32[3,256]{1,0:T(4,128)} %bitcast.10, s32[1]{0:T(128)} %copy.12.count, s32[2,256]{1,0:T(2,128)} %bitcast.12, f32[256,128]{1,0:T(8,128)} %charges.3, f32[36,4,48,128]{3,2,1,0:T(8,128)S(1)} %shard_map.100.grid, f32[256,64,128]{2,1,0:T(8,128)} %projection_at.3, bf16[256,128,128]{2,1,0:T(8,128)(2,1)} %matrices_at.1, ...), custom_call_target="tpu_custom_call" | custom-call | flops 10000000000 | bytes 10000000 | tf_op jit(solution)/shard_map/pallas_call | solution.py:651
  99.0 0.8 broadcast_select_fusion
  (1 shorter events, 0.0 us)

commit v12 on v11

--- a/solution.py
+++ b/solution.py
@@ -210,6 +210,15 @@
 
     def on_pencil(step):
         return at(0, step)
+
+    def to_pencil(step):
+        core = lax.rem(slab, 2)
+        one, two = lax.div(step, 4), lax.rem(step, 4)
+        y_step = (1 - core) * one + core * (4 - two)
+        x_step = (1 - core) * two + core * (4 - one)
+        y_at = lax.rem(lax.div(pencil, 4) + y_step, 4)
+        x_at = lax.rem(lax.rem(pencil, 4) + x_step, 4)
+        return (slab, 4 * y_at + x_at)
 
     def remote(source, target, send_sem, recv_sem, device):
         return pltpu.make_async_remote_copy(
@@ -398,7 +407,7 @@
         got_2[parity, :, mine, :] = sent_2[parity, chunk, pencil]
 
         def send(k, carry):
-            device = on_pencil(k)
+            device = to_pencil(k)
             remote(
                 sent_2.at[parity, chunk, device[1]], got_2.at[parity, :, mine, :], send_2, recv_2.at[parity], device
             ).start()
@@ -484,7 +493,7 @@
         took_2[parity, chunk, pencil] = back_2[parity, :, own, :]
 
         def send(k, carry):
-            device = on_pencil(k)
+            device = to_pencil(k)
             rows = pl.ds(pl.multiple_of(device[1] * 32 + chunk * 8, 8), 8)
             remote(
                 back_2.at[parity, :, rows, :], took_2.at[parity, chunk, pencil], send_3, recv_3.at[parity, chunk], device

time: 99.8 us -> 101 us (1.012)
  no operation moved by 1% of the time
where the time goes in v12:
time: 101 us; the launch traced here: 100 us
  Pallas kernels  99 us (98%)
    pallas_call x1, Pallas kernels, field(): pl.pallas_call(field_kernel, in_specs=[*[pl.BlockSpec(memory_space=pltpu....  90.5 us
    pallas_call x1, Pallas kernels, scatter(): pl.pallas_call(scatter_kernel, in_specs=[smem, smem, pl.BlockSpec(memory_...  8.55 us

profile of v12, /device:TPU:1, one launch (start us, length us, event | category | flops | bytes accessed | tf_op | source)
XLA Modules:
  0.0 100.4 jit_solution(8179690432363271236)
XLA Ops:
  0.7 8.6 %shard_map.100.grid = f32[36,4,48,128]{3,2,1,0:T(8,128)S(1)} custom-call(s32[3,256]{1,0:T(4,128)} %bitcast.9, s32[1]{0:T(128)} %copy.12.count, f32[256,64,128]{2,1,0:T(8,128)} %projection_at.3, f32[256,128]{1,0:T(8,128)} %charges.3), custom_call_target="tpu_custom_call" | custom-call | tf_op jit(solution)/shard_map/pallas_call | solution.py:109
  9.2 90.5 %shard_map.101 = f32[256,128]{1,0:T(8,128)S(1)} custom-call(s32[3,256]{1,0:T(4,128)} %bitcast.10, s32[1]{0:T(128)} %copy.12.count, s32[2,256]{1,0:T(2,128)} %bitcast.12, f32[256,128]{1,0:T(8,128)} %charges.3, f32[36,4,48,128]{3,2,1,0:T(8,128)S(1)} %shard_map.100.grid, f32[256,64,128]{2,1,0:T(8,128)} %projection_at.3, bf16[256,128,128]{2,1,0:T(8,128)(2,1)} %matrices_at.1, ...), custom_call_target="tpu_custom_call" | custom-call | flops 10000000000 | bytes 10000000 | tf_op jit(solution)/shard_map/pallas_call | solution.py:660
  99.7 0.8 broadcast_select_fusion
  (1 shorter events, 0.0 us)
